TPU v7x, 32 devices: a whole 2x2x4 slice. The times are simulated.
32 devices in a mesh: exp: 8 (over z, x), seq: 4 (over y, core).
Axes of the slice: x: 2, y: 2, z: 4, core: 2. Of those that a mesh axis runs over, the one named last changes fastest.
Arguments:
- tokens: bfloat16 [16, 2048, 768], P('exp', 'seq'), may hold values from -6 to 6
- query_weight: bfloat16 [768, 768], P(('exp', 'seq')), may hold values from -0.21875 to 0.21875
- key_weight: bfloat16 [768, 768], P(('exp', 'seq')), may hold values from -0.21875 to 0.21875
- value_weight: bfloat16 [768, 768], P(('exp', 'seq')), may hold values from -0.21875 to 0.21875
- out_weight: bfloat16 [768, 768], P(('exp', 'seq')), may hold values from -3.5 to 3.5
- router_weight: bfloat16 [768, 8], P(('exp', 'seq')), may hold values from -0.15625 to 0.15625
- attn_gain: bfloat16 [768], P(('exp', 'seq')), may hold values from 0.5 to 1.5
- moe_gain: bfloat16 [768], P(('exp', 'seq')), may hold values from 0.5 to 1.5
- bias_table: float32 [32, 12], replicated, may hold values from -4 to 4
- expert_in: bfloat16 [8, 768, 3072], P('exp', None, 'seq'), may hold values from -0.21875 to 0.21875
- expert_out: bfloat16 [8, 3072, 768], P('exp', 'seq'), may hold values from -1.5 to 1.5
- expert_id: int32 [16, 2048], P('exp', 'seq'), may hold values from 0 to 7, as said below
- slot_id: int32 [16, 2048], P('exp', 'seq'), may hold values from 0 to 160, as said below
- bucket_id: int32 [4095], replicated, may hold values from 0 to 31, as said below
- cotangent: bfloat16 [16, 2048, 768], P('exp', 'seq'), may hold values from -6 to 6
Outputs:
- output: bfloat16 [16, 2048, 768], P('exp', 'seq')
- input_grad: float32 [16, 2048, 768], P('exp', 'seq')
- query_weight_grad: float32 [768, 768], P(('exp', 'seq'))
- key_weight_grad: float32 [768, 768], P(('exp', 'seq'))
- value_weight_grad: float32 [768, 768], P(('exp', 'seq'))
- out_weight_grad: float32 [768, 768], P(('exp', 'seq'))
- router_weight_grad: float32 [768, 8], P(('exp', 'seq'))
- attn_gain_grad: float32 [768], P(('exp', 'seq'))
- moe_gain_grad: float32 [768], P(('exp', 'seq'))
- bias_table_grad: float32 [32, 12], replicated
- expert_in_grad: float32 [8, 768, 3072], P('exp', None, 'seq')
- expert_out_grad: float32 [8, 3072, 768], P('exp', 'seq')
Inputs may be any that keep to these rules, and one draw needn't show every extreme that they name: `expert_id`: in the tokens of one device (sequences n with equal n // 2, positions with equal p // 512), some expert is named by more than 160 tokens. slot_id is the number of earlier tokens of the same device with the same expert_id, earlier meaning a lower sequence, then a lower position; it is 160 where that number is 160 or more, and the token is then dropped. `bucket_id`: for offsets o - (2047) of zero or more the bucket is below 16, for negative ones 32 // 2 or more; on each side it never falls as the offset's magnitude grows.
All inputs are finite; a program needn't handle non-finite values.
Results may differ from a plain program's by a relative error of at most 0.015.
Values may be sent and summed in bfloat16 or wider, within the bound.
A program may use at most 256 MiB of HBM per device.

v0:
```python
import functools
import jax
import jax.numpy as jnp
import numpy as np
from jax import lax
from jax.experimental import pallas as pl
from jax.experimental.pallas import tpu as pltpu
NT=(((1,),(1,)),((),()))
NN=(((1,),(0,)),((),()))
LOG2E=1.4426950408889634
MIB=1024*1024

def lane_iota(rows):
    return lax.broadcasted_iota(jnp.int32,(rows,128),1)

def dup_head(values,head):
    values=values.astype(jnp.float32)
    turned=pltpu.roll(values,64,1)
    low=lane_iota(values.shape[0])<64
    return jnp.where(low,values,turned) if head==0 else jnp.where(low,turned,values)

def three_parts(column):
    first=column.astype(jnp.bfloat16).astype(jnp.float32)
    rest=column-first
    second=rest.astype(jnp.bfloat16).astype(jnp.float32)
    return first,second,rest-second

def columns_at(lanes,start,parts,other):
    out=other
    for place,part in enumerate(parts):
        out=jnp.where(lanes==start+place,part,out)
    return out

def split_query(query,head,scale):
    both=dup_head(query,head)*scale
    high=both.astype(jnp.bfloat16).astype(jnp.float32)
    return jnp.where(lane_iota(query.shape[0])<64,high,both-high).astype(jnp.bfloat16)

def fill_strip(strip,vector,rows,width):
    full=width+rows
    step=8
    spread=jnp.broadcast_to(vector,(rows,full))
    turned=pltpu.roll(spread,0,1,stride=1,stride_axis=0)
    strip[...]=turned[:,rows:]

def forward_kernel(heads,length,block,scale,q_ref,k_ref,v_ref,bias_ref,out_ref,o32_ref,lse_ref,strip,kd,va):
    strip_width=strip.shape[1]
    for head in range(heads):
        fill_strip(strip,bias_ref[head:head+1,:],block,strip_width)
        lanes=lane_iota(length)
        kd[...]=dup_head(k_ref[...],head).astype(jnp.bfloat16)
        va[...]=jnp.where(lanes<64,dup_head(v_ref[...],head),jnp.where(lanes==64,1.0,0.0)).astype(jnp.bfloat16)
        def body(step,carry):
            rows=pl.ds(pl.multiple_of(step*block,block),block)
            qa=split_query(q_ref[rows,:],head,scale)
            raw=lax.dot_general(qa,kd[...],NT,preferred_element_type=jnp.float32)
            start=pl.multiple_of(length-block-step*block,block)
            scores=raw+strip[:,pl.ds(start,length)]
            top=jnp.max(scores,axis=1,keepdims=True)
            weights=jnp.exp2(scores-top).astype(jnp.bfloat16)
            mixed=jnp.dot(weights,va[...],preferred_element_type=jnp.float32)
            total=mixed[:,64:65]
            result=mixed/total
            log_total=top+jnp.log2(total)
            lse_ref[rows,:]=jnp.where(lane_iota(block)==head,log_total,lse_ref[rows,:]) if head else jnp.broadcast_to(log_total,(block,128))
            if head==0:
                o32_ref[rows,:]=result
            else:
                both=jnp.where(lane_iota(block)<64,o32_ref[rows,:],pltpu.roll(result,64,1))
                o32_ref[rows,:]=both
            return carry
        lax.fori_loop(0,length//block,body,0)
    out_ref[...]=o32_ref[...].astype(jnp.bfloat16)

def attend(q,k,v,bias_vec,heads,chunk_ids,block=256):
    length=q.shape[0]
    scale=LOG2E/8
    spec=lambda c: pl.BlockSpec((length,128),lambda i,c=c:(0,c))
    full=pl.BlockSpec((length,128),lambda i:(0,0))
    width=2*length-block
    return pl.pallas_call(
        functools.partial(forward_kernel,heads,length,block,scale),
        grid=(1,),
        in_specs=[spec(chunk_ids[0]),spec(chunk_ids[1]),spec(chunk_ids[2]),pl.BlockSpec(bias_vec.shape,lambda i:(0,0))],
        out_specs=[full,full,full],
        out_shape=[jax.ShapeDtypeStruct((length,128),jnp.bfloat16),jax.ShapeDtypeStruct((length,128),jnp.float32),jax.ShapeDtypeStruct((length,128),jnp.float32)],
        scratch_shapes=[pltpu.VMEM((block,width),jnp.float32),pltpu.VMEM((length,128),jnp.bfloat16),pltpu.VMEM((length,128),jnp.bfloat16)],
        compiler_params=pltpu.CompilerParams(vmem_limit_bytes=56*MIB),
        name="attend_forward",
    )(q,k,v,bias_vec)

def backward_kernel(heads,length,bq,bk,scale,q_ref,k_ref,v_ref,do_ref,o32_ref,lse_ref,bias_ref,dqt_ref,dk_ref,dv_ref,diag_ref,strip,grads,ka,va,kt,qa,da,dd,qd,dk_acc,dv_acc):
    width=strip.shape[1]
    full_width=2*length
    lanes=lane_iota(length)
    for head in range(heads):
        fill_strip(strip,bias_ref[head:head+1,:],bk,width)
        grads[...]=jnp.zeros_like(grads)
        kd=dup_head(k_ref[...],head)
        ka[:,:128]=kd.astype(jnp.bfloat16)
        ka[:,128:]=jnp.where(lanes<3,1.0,0.0).astype(jnp.bfloat16)
        kt[...]=jnp.transpose(kd)[:64,:].astype(jnp.bfloat16)
        va[...]=jnp.where(lanes<64,dup_head(v_ref[...],head),jnp.where(lanes<67,1.0,0.0)).astype(jnp.bfloat16)
        qa[:,:128]=split_query(q_ref[...],head,scale)
        qa[:,128:]=columns_at(lanes,0,three_parts(-lse_ref[:,head:head+1]),0.0).astype(jnp.bfloat16)
        qd[...]=dup_head(q_ref[...],head).astype(jnp.bfloat16)
        dod=dup_head(do_ref[...],head)
        dd[...]=dod.astype(jnp.bfloat16)
        od=dup_head(o32_ref[...],head)
        delta=0.5*jnp.sum(dod*od,axis=1,keepdims=True)
        da[...]=columns_at(lanes,64,three_parts(-delta),jnp.where(lanes<64,dod,0.0)).astype(jnp.bfloat16)
        dk_acc[...]=jnp.zeros_like(dk_acc)
        dv_acc[...]=jnp.zeros_like(dv_acc)
        for qb in range(length//bq):
            qs=slice(qb*bq,(qb+1)*bq)
            def body(kb,dq):
                ks=pl.ds(pl.multiple_of(kb*bk,bk),bk)
                raw=lax.dot_general(ka[ks,:],qa[qs,:],NT,preferred_element_type=jnp.float32)
                start=pl.multiple_of(qb*bq+(length-bk)-kb*bk,128)
                probs=jnp.exp2(raw+strip[:,pl.ds(start,bq)])
                up=lax.dot_general(va[ks,:],da[qs,:],NT,preferred_element_type=jnp.float32)
                score_grad=probs*up
                grads[:,pl.ds(pl.multiple_of(start+bk,128),bq)]+=score_grad
                low=score_grad.astype(jnp.bfloat16)
                dv_acc[ks,:]+=jnp.dot(probs.astype(jnp.bfloat16),dd[qs,:],preferred_element_type=jnp.float32)
                dk_acc[ks,:]+=jnp.dot(low,qd[qs,:],preferred_element_type=jnp.float32)
                return dq+jnp.dot(kt[:,ks],low,preferred_element_type=jnp.float32)
            dq=lax.fori_loop(0,length//bk,body,jnp.zeros((64,bq),jnp.float32))
            dqt_ref[head*64:(head+1)*64,qs]=(dq*0.125).astype(jnp.bfloat16)
        if head==0:
            dk_ref[...]=(dk_acc[...]*0.125).astype(jnp.bfloat16)
            dv_ref[...]=dv_acc[...].astype(jnp.bfloat16)
        else:
            dk_ref[...]=jnp.where(lanes<64,dk_ref[...].astype(jnp.float32),dk_acc[...]*0.125).astype(jnp.bfloat16)
            dv_ref[...]=jnp.where(lanes<64,dv_ref[...].astype(jnp.float32),dv_acc[...]).astype(jnp.bfloat16)
        total=grads[0:8,:]
        for group in range(1,bk//8):
            total=total+pltpu.roll(grads[8*group:8*group+8,:],full_width-8*group,1)
        row=lax.broadcasted_iota(jnp.int32,(8,full_width),0)
        for part in range(1,8):
            total=jnp.where(row==part,pltpu.roll(total,full_width-part,1),total)
        diag_ref[head:head+1,:]=jnp.sum(total,axis=0,keepdims=True)

def attend_back(q,k,v,do,o32,lse,bias_vec,heads,chunk_ids,bq=512,bk=256):
    length=q.shape[0]
    scale=LOG2E/8
    spec=lambda c: pl.BlockSpec((length,128),lambda i,c=c:(0,c))
    full=pl.BlockSpec((length,128),lambda i:(0,0))
    width=2*length-bk
    f32,b16=jnp.float32,jnp.bfloat16
    return pl.pallas_call(
        functools.partial(backward_kernel,heads,length,bq,bk,scale),
        grid=(1,),
        in_specs=[spec(chunk_ids[0]),spec(chunk_ids[1]),spec(chunk_ids[2]),spec(chunk_ids[3]),full,full,pl.BlockSpec(bias_vec.shape,lambda i:(0,0))],
        out_specs=[pl.BlockSpec((128,length),lambda i:(0,0)),full,full,pl.BlockSpec((8,2*length),lambda i:(0,0))],
        out_shape=[jax.ShapeDtypeStruct((128,length),b16),jax.ShapeDtypeStruct((length,128),b16),jax.ShapeDtypeStruct((length,128),b16),jax.ShapeDtypeStruct((8,2*length),f32)],
        scratch_shapes=[pltpu.VMEM((bk,width),f32),pltpu.VMEM((bk,2*length),f32),pltpu.VMEM((length,256),b16),pltpu.VMEM((length,128),b16),pltpu.VMEM((64,length),b16),
            pltpu.VMEM((length,256),b16),pltpu.VMEM((length,128),b16),pltpu.VMEM((length,128),b16),pltpu.VMEM((length,128),b16),pltpu.VMEM((length,128),f32),pltpu.VMEM((length,128),f32)],
        compiler_params=pltpu.CompilerParams(vmem_limit_bytes=56*MIB),
        name="attend_backward",
    )(q,k,v,do,o32,lse,bias_vec)


from jax.sharding import PartitionSpec as P

EPSILON=1e-06
BOTH=("exp","seq")

def inverse_rms(values):
    return lax.rsqrt(jnp.mean(values*values,axis=-1,keepdims=True)+EPSILON)

def matmul(left,right,dims=NN):
    return lax.dot_general(left,right,dims,preferred_element_type=jnp.float32)

TN=(((0,),(0,)),((),()))

def swap_parts(values,axis):
    return lax.all_to_all(values,axis,split_axis=0,concat_axis=0,tiled=True)

def reversed_ids(ids):
    flip=np.eye(128,dtype=np.float32)[::-1]
    rows=ids.shape[0]//128
    flip_rows=np.eye(rows,dtype=np.float32)[::-1]
    grid=ids.astype(jnp.bfloat16).reshape(rows,128)
    grid=matmul(grid,jnp.asarray(flip,jnp.bfloat16)).astype(jnp.bfloat16)
    return matmul(jnp.asarray(flip_rows,jnp.bfloat16),grid).reshape(-1)

def offset_rows(ids,table):
    hot=(ids[None,:].astype(jnp.int32)==jnp.arange(table.shape[0],dtype=jnp.int32)[:,None]).astype(jnp.float32)
    return lax.dot_general(table,hot,(((0,),(0,)),((),())),precision=lax.Precision.HIGHEST)

def shards(tokens,query_weight,key_weight,value_weight,out_weight,router_weight,attn_gain,moe_gain,bias_table,expert_in,expert_out,expert_id,slot_id,bucket_id,cotangent):
    f32,b16=jnp.float32,jnp.bfloat16
    seq_count,stretch,width=tokens.shape
    seq_devs=lax.axis_size("seq")
    experts=lax.axis_size("exp")
    devices=seq_devs*experts
    length=stretch*seq_devs
    count=seq_count*stretch
    capacity=(5*count+4*experts-1)//(4*experts)
    buckets,heads=bias_table.shape
    head_dim=width//heads
    groups=seq_devs//seq_count
    own_heads=heads//groups
    per_chunk=2 if own_heads%2==0 else 1
    chunks=own_heads//per_chunk
    used=per_chunk*head_dim
    span=chunks*128
    row_block=width//devices
    place=lax.axis_index("seq")
    group=place%groups
    def by_group(weight):
        cut=weight.reshape(weight.shape[0],groups,chunks,used)
        cut=jnp.pad(cut,((0,0),(0,0),(0,0),(0,128-used)))
        return cut.reshape(weight.shape[0],groups,span)
    stacked=jnp.stack([by_group(w) for w in (query_weight,key_weight,value_weight)],axis=2).reshape(row_block,groups*3*span)
    stacked_full=lax.all_gather(stacked,BOTH,axis=0,tiled=True)
    gains=jnp.stack([attn_gain,moe_gain],axis=1)
    small=jnp.pad(jnp.concatenate([router_weight,gains],axis=1),((0,0),(0,128-router_weight.shape[1]-2)))
    small_full=lax.all_gather(small,BOTH,axis=0,tiled=True)
    out_full=lax.all_gather(out_weight,BOTH,axis=0,tiled=True)
    first_full=lax.all_gather(expert_in,"seq",axis=2,tiled=True)[0]
    second_full=lax.all_gather(expert_out,"seq",axis=1,tiled=True)[0]
    copies=jnp.broadcast_to(tokens[:,None],(seq_count,groups,stretch,width)).reshape(seq_devs,stretch,width)
    own_sequence=swap_parts(copies,"seq").reshape(length,width).astype(f32)
    weight=lax.dynamic_slice_in_dim(stacked_full,group*3*span,3*span,axis=1)
    router_full=small_full[:,:experts]
    attn_gain_full=small_full[:,experts].astype(f32)
    moe_gain_full=small_full[:,experts+1].astype(f32)
    padded=jnp.concatenate([jnp.zeros((1,),jnp.int32),bucket_id])
    forward_ids=reversed_ids(jnp.concatenate([bucket_id,jnp.zeros((1,),jnp.int32)]))
    own_table=lax.dynamic_slice_in_dim(bias_table,group*own_heads,own_heads,axis=1)*LOG2E
    forward_bias=offset_rows(forward_ids,own_table)
    backward_bias=offset_rows(padded,own_table)
    sequence_inverse=inverse_rms(own_sequence)
    normed=(own_sequence*sequence_inverse*attn_gain_full).astype(b16)
    projected=matmul(normed,weight).astype(b16)
    saved,attended_parts=[],[]
    for chunk in range(chunks):
        bias_rows=slice(chunk*per_chunk,(chunk+1)*per_chunk)
        out,out32,log_total=attend(projected,projected,projected,forward_bias[bias_rows],per_chunk,(chunk,chunks+chunk,2*chunks+chunk))
        saved.append((out32,log_total))
        attended_parts.append(swap_parts(out[:,:used].reshape(seq_devs,stretch,used),"seq"))
    attended=jnp.stack(attended_parts,axis=2).reshape(seq_count,groups,stretch,own_heads*head_dim)
    attended=jnp.swapaxes(attended,1,2).reshape(count,width)
    tokens_f=tokens.astype(f32).reshape(count,width)
    hidden=tokens_f+matmul(attended,out_full)
    moe_inverse=inverse_rms(hidden)
    moe_in=(hidden*moe_inverse*moe_gain_full).astype(b16)
    logits=matmul(moe_in,router_full)
    gates=jax.nn.softmax(logits,axis=-1)
    expert_pick=expert_id.reshape(count)
    slot_pick=slot_id.reshape(count)
    picked=(expert_pick[:,None]==jnp.arange(experts,dtype=jnp.int32)[None,:]).astype(f32)
    gate=jnp.sum(gates*picked,axis=-1)
    slots=experts*capacity
    position=jnp.where(slot_pick<capacity,expert_pick*capacity+slot_pick,slots)
    grad_out=cotangent.astype(f32).reshape(count,width)
    result_grad=(gate[:,None]*grad_out).astype(b16)
    hot=(position[None,:]==jnp.arange(slots,dtype=jnp.int32)[:,None]).astype(b16)
    send_rows=matmul(hot,moe_in).astype(b16).reshape(experts,capacity,width)
    rows=swap_parts(send_rows,"exp").reshape(slots,width)
    back_rows=matmul(hot,result_grad).astype(b16).reshape(experts,capacity,width)
    flat_grad=swap_parts(back_rows,"exp").reshape(slots,width)
    pre=matmul(rows,first_full)
    act_f,gelu_pull=jax.vjp(jax.nn.gelu,pre)
    act=act_f.astype(b16)
    result=matmul(act,second_full).astype(b16).reshape(experts,capacity,width)
    returned=swap_parts(result,"exp").reshape(slots,width)
    act_grad=matmul(flat_grad,second_full,NT).astype(b16)
    (pre_grad_f,)=gelu_pull(act_grad.astype(f32))
    pre_grad=pre_grad_f.astype(b16)
    rows_grad=matmul(pre_grad,first_full,NT).astype(b16).reshape(experts,capacity,width)
    grad_home=swap_parts(rows_grad,"exp").reshape(slots,width)
    out_grad_local=matmul(act,flat_grad,TN)
    in_grad_local=matmul(rows,pre_grad,TN)
    expert_in_grad=lax.psum_scatter(in_grad_local[None].astype(b16),"seq",scatter_dimension=2,tiled=True).astype(f32)
    expert_out_grad=lax.psum_scatter(out_grad_local[None].astype(b16),"seq",scatter_dimension=1,tiled=True).astype(f32)
    result_tok=matmul(hot,returned,TN)
    output=(hidden+gate[:,None]*result_tok).astype(b16).reshape(seq_count,stretch,width)
    gate_grad=jnp.sum(grad_out*result_tok,axis=-1)
    rows_tok=matmul(hot,grad_home,TN)
    logits_grad=(gates*(picked-gate[:,None])*gate_grad[:,None]).astype(b16)
    router_part=matmul(moe_in,logits_grad,TN)
    moe_in_grad=rows_tok+matmul(logits_grad,router_full,NT)
    weighted=moe_in_grad*moe_gain_full
    moe_gain_part=jnp.sum(moe_in_grad*hidden*moe_inverse,axis=0)
    inner=jnp.mean(weighted*hidden,axis=-1,keepdims=True)
    hidden_grad=grad_out+weighted*moe_inverse-hidden*(moe_inverse*moe_inverse*moe_inverse)*inner
    branch_grad=hidden_grad.astype(b16)
    heads_grad=matmul(branch_grad,out_full,NT).astype(b16)
    outgoing=heads_grad.reshape(seq_count,stretch,groups,chunks,used)
    outgoing=jnp.transpose(outgoing,(3,0,2,1,4))
    out_part=matmul(attended,branch_grad,TN)
    extra=jnp.pad(jnp.concatenate([router_part,moe_gain_part[:,None]],axis=1),((0,0),(0,128-experts-1)))
    out_piece=jnp.concatenate([out_part,extra],axis=1).astype(b16).reshape(devices,row_block,width+128)
    out_sum=jnp.sum(swap_parts(out_piece,BOTH).astype(f32),axis=0)
    query_grads,key_grads,value_grads,diagonals=[],[],[],[]
    for chunk in range(chunks):
        arriving=swap_parts(outgoing[chunk].reshape(seq_devs,stretch,used),"seq").reshape(length,used)
        arriving=jnp.pad(arriving,((0,0),(0,128-used)))
        bias_rows=slice(chunk*per_chunk,(chunk+1)*per_chunk)
        out32,log_total=saved[chunk]
        dq,dk,dv,diagonal=attend_back(projected,projected,projected,arriving,out32,log_total,backward_bias[bias_rows],per_chunk,(chunk,chunks+chunk,2*chunks+chunk,0))
        query_grads.append(dq)
        key_grads.append(dk)
        value_grads.append(dv)
        diagonals.append(diagonal[:per_chunk])
    query_grad=jnp.concatenate(query_grads,axis=0)
    rest_grad=jnp.concatenate(key_grads+value_grads,axis=1)
    normed_part=matmul(query_grad,weight[:,:span],(((0,),(1,)),((),())))+matmul(rest_grad,weight[:,span:],NT)
    attn_gain_part=jnp.sum(normed_part*own_sequence*sequence_inverse,axis=0)
    normed_sum=jnp.sum(swap_parts(normed_part.astype(b16).reshape(seq_devs,stretch,width),"seq").reshape(seq_count,groups,stretch,width).astype(f32),axis=1)
    query_part=matmul(normed,query_grad,(((0,),(1,)),((),())))
    rest_part=matmul(normed,rest_grad,TN)
    diagonals=jnp.concatenate(diagonals,axis=0)
    hot_bucket=(padded[None,:]==jnp.arange(buckets,dtype=jnp.int32)[:,None]).astype(f32)
    hot_bucket=hot_bucket*(jnp.arange(length*2)>0)[None,:]
    table_part=lax.dot_general(hot_bucket,diagonals,(((1,),(1,)),((),())),precision=lax.Precision.HIGHEST)
    table_wide=jnp.zeros((buckets,heads),f32)
    table_wide=lax.dynamic_update_slice_in_dim(table_wide,table_part,group*own_heads,axis=1)
    bias_table_grad=lax.psum(table_wide,BOTH)
    piece=jnp.concatenate([query_part,rest_part,jnp.pad(attn_gain_part[:,None],((0,0),(0,127)))],axis=1).astype(b16)
    arrived=swap_parts(piece.reshape(devices,row_block,3*span+128),BOTH).astype(f32)
    arrived=jnp.sum(arrived.reshape(devices//groups,groups,row_block,3*span+128),axis=0)
    attn_gain_grad=jnp.sum(arrived[:,:,3*span],axis=0)
    grads=arrived[:,:,:3*span].reshape(groups,row_block,3,chunks,128)[...,:used]
    grads=jnp.transpose(grads,(2,1,0,3,4)).reshape(3,row_block,width)
    tokens_inverse=inverse_rms(tokens_f)
    normed_sum=normed_sum.reshape(count,width)
    weighted=normed_sum*attn_gain_full
    inner=jnp.mean(weighted*tokens_f,axis=-1,keepdims=True)
    input_grad=hidden_grad+weighted*tokens_inverse-tokens_f*(tokens_inverse*tokens_inverse*tokens_inverse)*inner
    return (
        output,
        input_grad.reshape(seq_count,stretch,width),
        grads[0],grads[1],grads[2],
        out_sum[:,:width],
        out_sum[:,width:width+experts],
        attn_gain_grad,
        out_sum[:,width+experts],
        bias_table_grad,
        expert_in_grad,
        expert_out_grad,
    )

def solution(mesh):
    tokens=P("exp","seq",None)
    rows=P(BOTH,None)
    return jax.shard_map(
        shards,
        mesh=mesh,
        in_specs=(tokens,rows,rows,rows,rows,rows,P(BOTH),P(BOTH),P(),P("exp",None,"seq"),P("exp","seq",None),P("exp","seq"),P("exp","seq"),P(),tokens),
        out_specs=(tokens,tokens,rows,rows,rows,rows,rows,P(BOTH),P(BOTH),P(),P("exp",None,"seq"),P("exp","seq",None)),
        check_vma=False,
    )
```

profile of v0, /device:TPU:0, one launch (start us, length us, event | category | flops | bytes accessed | tf_op | source)
XLA Modules:
  0.0 795.7 jit_solution(7764497756621024635)
XLA Ops:
  14.7 4.4 all-to-all-start
  20.2 72.9 %all_gather.15 = bf16[768,128]{1,0:T(8,128)(2,1)S(1)} all-gather(bf16[24,128]{1,0:T(8,128)(2,1)S(1)} %fusion.101), channel_id=1, replica_groups=mesh['exp'=8,'seq'=4] {'exp','seq'}, dimensions={0}, use_global_device_ids=true | all-gather | bytes 202752 | tf_op jit(solution)/shard_map/all_gather | solution.py:220
  98.8 8.9 %convolution_convert_fusion.1.q_ref.k_ref.v_ref = bf16[2048,1152]{1,0:T(8,128)(2,1)} fusion(bf16[2048,768]{1,0:T(8,128)(2,1)} %fusion.12, bf16[768,2304]{1,0:T(8,128)(2,1)} %all-gather.5.cloned.1.call-done, s32[]{:T(128)S(6)} %select_n.23), kind=kOutput, calls=%fused_computation.16 | convolution fusion | flops 3626237952 | bytes 9633796 | tf_op jit(solution)/shard_map/dot_general | solution.py:173
  107.6 22.9 %attend_forward.5 = (bf16[2048,128]{1,0:T(8,128)(2,1)}, f32[2048,128]{1,0:T(8,128)}, f32[2048,128]{1,0:T(8,128)}) custom-call(bf16[2048,1152]{1,0:T(8,128)(2,1)} %convolution_convert_fusion.1.q_ref.k_ref.v_ref, bf16[2048,1152]{1,0:T(8,128)(2,1)} %convolution_convert_fusion.1.q_ref.k_ref.v_ref, ...), custom_call_target="tpu_custom_call" | custom-call | tf_op jit(solution)/shard_map/attend_forward/pallas_call | solution.py:81
  136.3 23.0 %attend_forward.4 = (bf16[2048,128]{1,0:T(8,128)(2,1)}, f32[2048,128]{1,0:T(8,128)}, f32[2048,128]{1,0:T(8,128)}) custom-call(bf16[2048,1152]{1,0:T(8,128)(2,1)} %convolution_convert_fusion.1.q_ref.k_ref.v_ref, bf16[2048,1152]{1,0:T(8,128)(2,1)} %convolution_convert_fusion.1.q_ref.k_ref.v_ref, ...), custom_call_target="tpu_custom_call" | custom-call | tf_op jit(solution)/shard_map/attend_forward/pallas_call | solution.py:81
  164.8 22.9 %attend_forward.3 = (bf16[2048,128]{1,0:T(8,128)(2,1)}, f32[2048,128]{1,0:T(8,128)}, f32[2048,128]{1,0:T(8,128)}) custom-call(bf16[2048,1152]{1,0:T(8,128)(2,1)} %convolution_convert_fusion.1.q_ref.k_ref.v_ref, bf16[2048,1152]{1,0:T(8,128)(2,1)} %convolution_convert_fusion.1.q_ref.k_ref.v_ref, ...), custom_call_target="tpu_custom_call" | custom-call | tf_op jit(solution)/shard_map/attend_forward/pallas_call | solution.py:81
  193.7 8.8 %all-to-all-done.1 = bf16[4,512,128]{1,2,0:T(8,128)(2,1)S(1)} async-done(((bf16[4,512,128]{1,2,0:T(8,128)(2,1)}), bf16[4,512,128]{1,2,0:T(8,128)(2,1)S(1)}, u32[]{:S(2)}, u32[]{:S(2)}) %all-to-all-start.1) | async-done | bytes 524320 | tf_op jit(solution)/shard_map/all_to_all | solution.py:178
  221.1 5.3 fusion.35
  226.3 37.6 %all-to-all-done.4 = bf16[8,160,768]{2,1,0:T(8,128)(2,1)} async-done(((bf16[8,160,768]{2,1,0:T(8,128)(2,1)}), bf16[8,160,768]{2,1,0:T(8,128)(2,1)}, u32[]{:S(2)}, u32[]{:S(2)}) %all-to-all-start.4) | async-done | bytes 1966112 | tf_op jit(solution)/shard_map/all_to_all | solution.py:178
  268.5 12.2 %fusion.24 = f32[1280,3072]{1,0:T(8,128)} fusion(bf16[1280,768]{1,0:T(8,128)(2,1)} %bitcast.17, bf16[1,768,3072]{2,1,0:T(8,128)(2,1)} %all-gather.9.cloned.1.call-done), kind=kOutput, calls=%fused_computation.41 | convolution fusion | flops 6039797760 | bytes 22413312 | tf_op jit(solution)/shard_map/dot_general | solution.py:173
  280.7 32.6 %all-to-all-done.6 = bf16[8,160,768]{2,1,0:T(8,128)(2,1)} async-done(((bf16[8,160,768]{2,1,0:T(8,128)(2,1)}), bf16[8,160,768]{2,1,0:T(8,128)(2,1)}, u32[]{:S(2)}, u32[]{:S(2)}) %all-to-all-start.6) | async-done | bytes 1966112 | tf_op jit(solution)/shard_map/all_to_all | solution.py:178
  313.3 13.7 %fusion.27 = bf16[1,3072,768]{2,1,0:T(8,128)(2,1)} fusion(bf16[1280,768]{1,0:T(8,128)(2,1)} %bitcast.26, f32[1280,3072]{1,0:T(8,128)} %fusion.24), kind=kOutput, calls=%fused_computation.44 | convolution fusion | flops 6077546496 | bytes 22413312 | tf_op jit(solution)/shard_map/dot_general | solution.py:173
  327.1 15.6 %fusion.31 = bf16[1280,768]{1,0:T(8,128)(2,1)} fusion(bf16[1,3072,768]{2,1,0:T(8,128)(2,1)} %all-gather.11.cloned.1.call-done, f32[1280,3072]{1,0:T(8,128)} %fusion.24), kind=kOutput, calls=%fused_computation.48 | convolution fusion | flops 6076170240 | bytes 22413312 | tf_op jit(solution)/shard_map/dot_general | solution.py:173
  342.6 4.6 all-to-all-start.5
  347.2 18.5 %fusion.2 = bf16[1280,3072]{1,0:T(8,128)(2,1)S(1)} fusion(f32[1280,3072]{1,0:T(8,128)} %fusion.24, bf16[1280,768]{1,0:T(8,128)(2,1)} %bitcast.26, bf16[1,3072,768]{2,1,0:T(8,128)(2,1)} %all-gather.11.cloned.1.call-done), kind=kOutput, calls=%fused_computation.6 | convolution fusion | flops 6126305280 | bytes 30277632 | tf_op jit(solution)/shard_map/dot_general | solution.py:173
  368.8 9.8 %fusion.28 = bf16[1280,768]{1,0:T(8,128)(2,1)} fusion(bf16[1280,3072]{1,0:T(8,128)(2,1)S(1)} %fusion.2, bf16[1,768,3072]{2,1,0:T(8,128)(2,1)} %all-gather.9.cloned.1.call-done), kind=kOutput, calls=%fused_computation.47 | convolution fusion | flops 6040780800 | bytes 14548992 | tf_op jit(solution)/shard_map/dot_general | solution.py:173
  378.6 12.8 %all-to-all-done.5 = bf16[8,160,768]{2,1,0:T(8,128)(2,1)} async-done(((bf16[8,160,768]{2,1,0:T(8,128)(2,1)}), bf16[8,160,768]{2,1,0:T(8,128)(2,1)}, u32[]{:S(2)}, u32[]{:S(2)}) %all-to-all-start.5) | async-done | bytes 1966112 | tf_op jit(solution)/shard_map/all_to_all | solution.py:178
  391.4 4.3 all-to-all-start.7
  399.8 10.7 %fusion.26 = bf16[1,768,3072]{2,1,0:T(8,128)(2,1)} fusion(bf16[1280,768]{1,0:T(8,128)(2,1)} %bitcast.17, bf16[1280,3072]{1,0:T(8,128)(2,1)} %copy-done.31), kind=kOutput, calls=%fused_computation.43 | convolution fusion | flops 6042157056 | bytes 14548992 | tf_op jit(solution)/shard_map/dot_general | solution.py:173
  410.6 6.2 fusion.37
  417.0 23.7 %all-to-all-done.7 = bf16[8,160,768]{2,1,0:T(8,128)(2,1)} async-done(((bf16[8,160,768]{2,1,0:T(8,128)(2,1)}), bf16[8,160,768]{2,1,0:T(8,128)(2,1)}, u32[]{:S(2)}, u32[]{:S(2)}) %all-to-all-start.7) | async-done | bytes 1966112 | tf_op jit(solution)/shard_map/all_to_all | solution.py:178
  471.4 5.1 all-to-all-done.8
  485.3 46.4 %attend_backward.3 = (bf16[128,2048]{1,0:T(8,128)(2,1)}, bf16[2048,128]{1,0:T(8,128)(2,1)}, bf16[2048,128]{1,0:T(8,128)(2,1)}, f32[8,4096]{1,0:T(8,128)}) custom-call(bf16[2048,1152]{1,0:T(8,128)(2,1)} %convolution_convert_fusion.1.q_ref.k_ref.v_ref, bf16[2048,1152]{1,0:T(8,128)(2,1)} %convolution_convert_fusion.1.q_ref.k_ref.v_ref, ...), custom_call_target="tpu_custom_call" | custom-call | tf_op jit(solution)/shard_map/attend_backward/pallas_call | solution.py:151
  537.7 46.2 %attend_backward.4 = (bf16[128,2048]{1,0:T(8,128)(2,1)}, bf16[2048,128]{1,0:T(8,128)(2,1)}, bf16[2048,128]{1,0:T(8,128)(2,1)}, f32[8,4096]{1,0:T(8,128)}) custom-call(bf16[2048,1152]{1,0:T(8,128)(2,1)} %convolution_convert_fusion.1.q_ref.k_ref.v_ref, bf16[2048,1152]{1,0:T(8,128)(2,1)} %convolution_convert_fusion.1.q_ref.k_ref.v_ref, ...), custom_call_target="tpu_custom_call" | custom-call | tf_op jit(solution)/shard_map/attend_backward/pallas_call | solution.py:151
  590.9 46.2 %attend_backward.5 = (bf16[128,2048]{1,0:T(8,128)(2,1)}, bf16[2048,128]{1,0:T(8,128)(2,1)}, bf16[2048,128]{1,0:T(8,128)(2,1)}, f32[8,4096]{1,0:T(8,128)}) custom-call(bf16[2048,1152]{1,0:T(8,128)(2,1)} %convolution_convert_fusion.1.q_ref.k_ref.v_ref, bf16[2048,1152]{1,0:T(8,128)(2,1)} %convolution_convert_fusion.1.q_ref.k_ref.v_ref, ...), custom_call_target="tpu_custom_call" | custom-call | tf_op jit(solution)/shard_map/attend_backward/pallas_call | solution.py:151
  644.6 4.8 fusion.67
  649.5 5.8 fusion.14
  655.3 4.9 all-to-all-start.11
  660.2 4.7 copy.105
  673.7 23.5 %all-to-all-done.11 = bf16[4,512,768]{2,1,0:T(8,128)(2,1)} async-done(((bf16[4,512,768]{2,1,0:T(8,128)(2,1)}), bf16[4,512,768]{2,1,0:T(8,128)(2,1)}, u32[]{:S(2)}, u32[]{:S(2)}) %all-to-all-start.11) | async-done | bytes 3145760 | tf_op jit(solution)/shard_map/all_to_all | solution.py:178
  697.2 4.9 all-to-all-start.12
  705.6 62.9 %psum.7 = f32[32,12]{0,1:T(8,128)} all-reduce(f32[32,12]{0,1:T(8,128)S(1)} %dynamic_update_slice.3), channel_id=1, replica_groups=mesh['exp'=8,'seq'=4] {'exp','seq'}, use_global_device_ids=true, to_apply=%region_15.16 | all-reduce | flops 384 | bytes 3072 | tf_op jit(solution)/shard_map/psum | solution.py:322
  (201 shorter events, 153.8 us)
Async XLA Ops:
  7.2 91.6 %all-gather.5.cloned.1.call-start = ((), (), s32[]{:S(2)}) async-start(), calls=%async_computation.16 | async-start | bytes 3649536 | tf_op jit(solution)/shard_map/all_gather | solution.py:217
  10.6 195.7 %all-gather.7.cloned.1.call-start = ((), (), s32[]{:S(2)}) async-start(), calls=%async_computation.17 | async-start | bytes 1216512 | tf_op jit(solution)/shard_map/all_gather | solution.py:221
  14.7 78.4 %copy-start.22 = (bf16[128,128]{1,0:T(8,128)(2,1)S(1)}, bf16[128,128]{1,0:T(8,128)(2,1)}, u32[]{:S(2)}) copy-start(bf16[128,128]{1,0:T(8,128)(2,1)} %constant.78.clone) | copy-start | bytes 98308
  14.7 78.4 %copy-start.24 = (bf16[32,32]{1,0:T(8,128)(2,1)S(1)}, bf16[32,32]{1,0:T(8,128)(2,1)}, u32[]{:S(2)}) copy-start(bf16[32,32]{1,0:T(8,128)(2,1)} %constant.79.clone) | copy-start | bytes 6148
  14.7 79.0 %copy-start.23 = (f32[32,12]{0,1:T(8,128)S(1)}, f32[32,12]{0,1:T(8,128)}, u32[]{:S(2)}) copy-start(f32[32,12]{0,1:T(8,128)} %param.25) | copy-start | bytes 4612
  14.7 80.0 %all-to-all-start = ((bf16[4,512,768]{2,1,0:T(8,128)(2,1)}), bf16[4,512,768]{2,1,0:T(8,128)(2,1)S(1)}, u32[]{:S(2)}, u32[]{:S(2)}) async-start(bf16[4,512,768]{2,1,0:T(8,128)(2,1)} %bitcast.154), calls=%async_computation | async-start | bytes 6291456 | tf_op jit(solution)/shard_map/all_to_all | solution.py:178
  19.1 249.4 %all-gather.9.cloned.1.call-start = ((), (), s32[]{:S(2)}) async-start(), calls=%async_computation.18 | async-start | bytes 5898240 | tf_op jit(solution)/shard_map/all_gather | solution.py:222
  132.6 28.7 %all-to-all-start.3 = ((bf16[4,512,128]{1,2,0:T(8,128)(2,1)}), bf16[4,512,128]{1,2,0:T(8,128)(2,1)S(1)}, u32[]{:S(2)}, u32[]{:S(2)}) async-start(bf16[4,512,128]{1,2,0:T(8,128)(2,1)} %copy.99), calls=%async_computation.3 | async-start | bytes 1048576 | tf_op jit(solution)/shard_map/all_to_all | solution.py:178
  161.3 28.4 %all-to-all-start.2 = ((bf16[4,512,128]{1,2,0:T(8,128)(2,1)}), bf16[4,512,128]{1,2,0:T(8,128)(2,1)S(1)}, u32[]{:S(2)}, u32[]{:S(2)}) async-start(bf16[4,512,128]{1,2,0:T(8,128)(2,1)} %copy.98), calls=%async_computation.2 | async-start | bytes 1048576 | tf_op jit(solution)/shard_map/all_to_all | solution.py:178
  164.8 28.8 %copy-start.25 = (s32[2,512]{1,0:T(2,128)S(1)}, s32[2,512]{1,0:T(2,128)}, u32[]{:S(2)}) copy-start(s32[2,512]{1,0:T(2,128)} %param.28) | copy-start | bytes 12292
  164.8 28.9 %copy-start.26 = (s32[2,512]{1,0:T(2,128)S(1)}, s32[2,512]{1,0:T(2,128)}, u32[]{:S(2)}) copy-start(s32[2,512]{1,0:T(2,128)} %param.29) | copy-start | bytes 12292
  189.7 12.7 %all-to-all-start.1 = ((bf16[4,512,128]{1,2,0:T(8,128)(2,1)}), bf16[4,512,128]{1,2,0:T(8,128)(2,1)S(1)}, u32[]{:S(2)}, u32[]{:S(2)}) async-start(bf16[4,512,128]{1,2,0:T(8,128)(2,1)} %copy.97), calls=%async_computation.1 | async-start | bytes 1048576 | tf_op jit(solution)/shard_map/all_to_all | solution.py:178
  214.1 49.8 %all-to-all-start.4 = ((bf16[8,160,768]{2,1,0:T(8,128)(2,1)}), bf16[8,160,768]{2,1,0:T(8,128)(2,1)}, u32[]{:S(2)}, u32[]{:S(2)}) async-start(bf16[8,160,768]{2,1,0:T(8,128)(2,1)} %bitcast.172), calls=%async_computation.4 | async-start | bytes 3932160 | tf_op jit(solution)/shard_map/all_to_all | solution.py:178
  218.5 108.6 %all-gather.11.cloned.1.call-start = ((), (), s32[]{:S(2)}) async-start(), calls=%async_computation.19 | async-start | bytes 5898240 | tf_op jit(solution)/shard_map/all_gather | solution.py:223
  263.9 49.3 %all-to-all-start.6 = ((bf16[8,160,768]{2,1,0:T(8,128)(2,1)}), bf16[8,160,768]{2,1,0:T(8,128)(2,1)}, u32[]{:S(2)}, u32[]{:S(2)}) async-start(bf16[8,160,768]{2,1,0:T(8,128)(2,1)} %bitcast.173), calls=%async_computation.6 | async-start | bytes 3932160 | tf_op jit(solution)/shard_map/all_to_all | solution.py:178
  268.3 514.5 %reduce-scatter.5.cloned.1.call-start = ((), (), s32[]{:S(2)}) async-start(), calls=%async_computation.21 | async-start | bytes 5898240 | tf_op jit(solution)/shard_map/reduce_scatter | solution.py:278
  342.6 48.8 %all-to-all-start.5 = ((bf16[8,160,768]{2,1,0:T(8,128)(2,1)}), bf16[8,160,768]{2,1,0:T(8,128)(2,1)}, u32[]{:S(2)}, u32[]{:S(2)}) async-start(bf16[8,160,768]{2,1,0:T(8,128)(2,1)} %bitcast.174), calls=%async_computation.5 | async-start | bytes 3932160 | tf_op jit(solution)/shard_map/all_to_all | solution.py:178
  391.4 49.3 %all-to-all-start.7 = ((bf16[8,160,768]{2,1,0:T(8,128)(2,1)}), bf16[8,160,768]{2,1,0:T(8,128)(2,1)}, u32[]{:S(2)}, u32[]{:S(2)}) async-start(bf16[8,160,768]{2,1,0:T(8,128)(2,1)} %bitcast.171), calls=%async_computation.7 | async-start | bytes 3932160 | tf_op jit(solution)/shard_map/all_to_all | solution.py:178
  395.8 389.8 %reduce-scatter.3.cloned.1.call-start = ((), (), s32[]{:S(2)}) async-start(), calls=%async_computation.20 | async-start | bytes 5898240 | tf_op jit(solution)/shard_map/reduce_scatter | solution.py:277
  410.5 6.2 copy-start.3
  455.7 11.8 %copy-start.6 = (f32[1024,768]{1,0:T(8,128)S(1)}, f32[1024,768]{1,0:T(8,128)}, u32[]{:S(2)}) copy-start(f32[1024,768]{1,0:T(8,128)} %copy-done.5) | copy-start | bytes 9437188
  463.4 13.1 %all-to-all-start.8 = ((bf16[4,512,128]{2,1,0:T(8,128)(2,1)}), bf16[4,512,128]{2,1,0:T(8,128)(2,1)}, u32[]{:S(2)}, u32[]{:S(2)}) async-start(bf16[4,512,128]{2,1,0:T(8,128)(2,1)} %bitcast.167), calls=%async_computation.8 | async-start | bytes 1048576 | tf_op jit(solution)/shard_map/all_to_all | solution.py:178
  476.4 57.1 %all-to-all-start.9 = ((bf16[4,512,128]{2,1,0:T(8,128)(2,1)}), bf16[4,512,128]{2,1,0:T(8,128)(2,1)}, u32[]{:S(2)}, u32[]{:S(2)}) async-start(bf16[4,512,128]{2,1,0:T(8,128)(2,1)} %bitcast.165), calls=%async_computation.9 | async-start | bytes 1048576 | tf_op jit(solution)/shard_map/all_to_all | solution.py:178
  533.5 53.2 %all-to-all-start.10 = ((bf16[4,512,128]{2,1,0:T(8,128)(2,1)}), bf16[4,512,128]{2,1,0:T(8,128)(2,1)}, u32[]{:S(2)}, u32[]{:S(2)}) async-start(bf16[4,512,128]{2,1,0:T(8,128)(2,1)} %bitcast.166), calls=%async_computation.10 | async-start | bytes 1048576 | tf_op jit(solution)/shard_map/all_to_all | solution.py:178
  537.7 46.3 %copy-start.13 = (bf16[2048,128]{1,0:T(8,128)(2,1)S(1)}, bf16[2048,128]{1,0:T(8,128)(2,1)}, u32[]{:S(2)}) copy-start(bf16[2048,128]{1,0:T(8,128)(2,1)} %get-tuple-element.45) | copy-start | bytes 1572868
  586.7 68.6 %all-to-all-start.13 = ((bf16[32,24,896]{2,1,0:T(8,128)(2,1)}), bf16[32,24,896]{2,1,0:T(8,128)(2,1)}, u32[]{:S(2)}, u32[]{:S(2)}) async-start(bf16[32,24,896]{2,1,0:T(8,128)(2,1)} %pad_maximum_fusion.2), calls=%async_computation.13 | async-start | bytes 2752512 | tf_op jit(solution)/shard_map/all_to_all | solution.py:178
  590.9 48.3 %copy-start.12 = (bf16[2048,128]{1,0:T(8,128)(2,1)S(1)}, bf16[2048,128]{1,0:T(8,128)(2,1)}, u32[]{:S(2)}) copy-start(bf16[2048,128]{1,0:T(8,128)(2,1)} %get-tuple-element.46) | copy-start | bytes 1572868
  637.1 5.7 copy-start.11
  637.1 6.6 copy-start.14
  637.1 7.5 copy-start.15
  655.3 41.9 %all-to-all-start.11 = ((bf16[4,512,768]{2,1,0:T(8,128)(2,1)}), bf16[4,512,768]{2,1,0:T(8,128)(2,1)}, u32[]{:S(2)}, u32[]{:S(2)}) async-start(bf16[4,512,768]{2,1,0:T(8,128)(2,1)} %bitcast.156), calls=%async_computation.11 | async-start | bytes 6291456 | tf_op jit(solution)/shard_map/all_to_all | solution.py:178
  697.2 80.8 %all-to-all-start.12 = ((bf16[32,24,1280]{2,1,0:T(8,128)(2,1)}), bf16[32,24,1280]{2,1,0:T(8,128)(2,1)}, u32[]{:S(2)}, u32[]{:S(2)}) async-start(bf16[32,24,1280]{2,1,0:T(8,128)(2,1)} %pad_maximum_fusion), calls=%async_computation.12 | async-start | bytes 3932160 | tf_op jit(solution)/shard_map/all_to_all | solution.py:178
  (20 other events, 76.8 us)
Sparse Core Ops, SparseCore 0:
  11.5 63.7 all-gather.4
  78.2 52.9 all-gather.6
  132.7 41.4 all-gather.8
  220.6 37.8 all-gather.10
  327.2 46.1 reduce-scatter.4
  410.7 48.3 reduce-scatter.2
where the time goes:
time: 806 us; the launch traced here: 796 us
  Pallas kernels  208 us (26%)
  waiting for transfers between devices  146 us (18%)
  matrix products  140 us (17%)
  blocking collectives  136 us (17%)
  local copies, waits for them, and re-layouts  65 us (8%)
  starting transfers between devices  59.9 us (7%)
  other arithmetic  26.2 us (3%)
  between operations  15.3 us (2%)
    all_to_all x14, waiting for transfers between devices, swap_parts(): return lax.all_to_all(values, axis, split_axis=0, concat_axis=0, tiled=True)  144 us
    dot_general x22, matrix products, matmul(): lax.dot_general(left, right, dims, preferred_element_type=jnp.float32)  139 us
    pallas_call x3, Pallas kernels, attend_back(): pl.pallas_call(functools.partial(backward_kernel, heads, length, bq, bk,...  139 us
    all_gather x1, blocking collectives, shards(): small_full = lax.all_gather(small, BOTH, axis=0, tiled=True)  72.9 us
    pallas_call x3, Pallas kernels, attend(): pl.pallas_call(functools.partial(forward_kernel, heads, length, block, sc...  68.7 us
    psum x1, blocking collectives, shards(): bias_table_grad = lax.psum(table_wide, BOTH)  62.9 us
    all_to_all x14, starting transfers between devices, swap_parts(): return lax.all_to_all(values, axis, split_axis=0, concat_axis=0, tiled=True)  59.5 us
    unnamed x80, local copies, waits for them, and re-layouts  18.5 us
  transfers between devices with their start and end apart: 20, of which 7 were waited for; matrix products, arithmetic and copies ran while one was open for 27% of the time, Pallas kernels for 26%

commit v1 on v0

v1 whole, which is shorter than its diff:
```python
import functools
import jax
import jax.numpy as jnp
import numpy as np
from jax import lax
from jax.experimental import pallas as pl
from jax.experimental.pallas import tpu as pltpu
from jax.sharding import PartitionSpec as P
NT=(((1,),(1,)),((),()))
NN=(((1,),(0,)),((),()))
LOG2E=1.4426950408889634
MIB=1024*1024
TN=(((0,),(0,)),((),()))
MESH=pl.DeviceIdType.MESH
EPSILON=1e-06
BOTH=("exp","seq")

def lane_iota(rows):
    return lax.broadcasted_iota(jnp.int32,(rows,128),1)

def dup_head(values,head):
    values=values.astype(jnp.float32)
    turned=pltpu.roll(values,64,1)
    low=lane_iota(values.shape[0])<64
    return jnp.where(low,values,turned) if head==0 else jnp.where(low,turned,values)

def three_parts(column):
    first=column.astype(jnp.bfloat16).astype(jnp.float32)
    rest=column-first
    second=rest.astype(jnp.bfloat16).astype(jnp.float32)
    return first,second,rest-second

def columns_at(lanes,start,parts,other):
    out=other
    for place,part in enumerate(parts):
        out=jnp.where(lanes==start+place,part,out)
    return out

def split_query(query,head,scale):
    both=dup_head(query,head)*scale
    high=both.astype(jnp.bfloat16).astype(jnp.float32)
    return jnp.where(lane_iota(query.shape[0])<64,high,both-high).astype(jnp.bfloat16)

def fill_strip(strip,vector,rows,width):
    full=width+rows
    step=8
    spread=jnp.broadcast_to(vector,(rows,full))
    turned=pltpu.roll(spread,0,1,stride=1,stride_axis=0)
    strip[...]=turned[:,rows:]


def forward_kernel(heads,block,srows,scale,q_ref,k_ref,v_ref,bias_ref,out_ref,o32_ref,lse_ref,strip,kd,va,scr):
    length=q_ref.shape[0]
    width=strip.shape[1]
    wide=256
    blocks=length//block
    pieces=length//wide
    lanes=lane_iota(length)
    block_lanes=lane_iota(block)
    for head in range(heads):
        fill_strip(strip,bias_ref[head:head+1,:],srows,width)
        kd[...]=dup_head(k_ref[...],head).astype(jnp.bfloat16)
        va[...]=jnp.where(lanes<64,dup_head(v_ref[...],head),jnp.where(lanes==64,1.0,0.0)).astype(jnp.bfloat16)
        def rows_of(step):
            return pl.ds(pl.multiple_of(step*block,block),block)
        def score_piece(step,qa,c,slot,top):
            raw=lax.dot_general(qa,kd[c*wide:(c+1)*wide,:],NT,preferred_element_type=jnp.float32)
            parts=[]
            for part in range(block//srows):
                start=pl.multiple_of(length-srows-step*block-part*srows+c*wide,128)
                parts.append(raw[part*srows:(part+1)*srows]+strip[:,pl.ds(start,wide)])
            scores=jnp.concatenate(parts,axis=0)
            scr[slot,:,c*wide:(c+1)*wide]=scores
            for j in range(wide//128):
                top=jnp.maximum(top,scores[:,j*128:(j+1)*128])
            return top
        def mix_piece(slot,c,top,total):
            weights=jnp.exp2(scr[slot,:,c*wide:(c+1)*wide]-top).astype(jnp.bfloat16)
            return total+jnp.dot(weights,va[c*wide:(c+1)*wide,:],preferred_element_type=jnp.float32)
        def finish(step,top,mixed):
            rows=rows_of(step)
            total=mixed[:,64:65]
            result=mixed/total
            log_total=top+jnp.log2(total)
            if head==0:
                lse_ref[rows,:]=jnp.broadcast_to(log_total,(block,128))
                o32_ref[rows,:]=result
            else:
                lse_ref[rows,:]=jnp.where(block_lanes==head,log_total,lse_ref[rows,:])
                o32_ref[rows,:]=jnp.where(block_lanes<64,o32_ref[rows,:],pltpu.roll(result,64,1))
        def advance(step,slot,top):
            mixing=top is not None
            qa=split_query(q_ref[rows_of(step),:],head,scale)
            new=jnp.full((block,128),-jnp.inf,jnp.float32)
            mixed=jnp.zeros((block,128),jnp.float32)
            for c in range(pieces):
                new=score_piece(step,qa,c,slot,new)
                if mixing:
                    mixed=mix_piece(1-slot,c,top,mixed)
            if mixing:
                finish(step-1,top,mixed)
            return jnp.max(new,axis=1,keepdims=True)
        def body(i,top):
            top=advance(2*i+1,1,top)
            return advance(2*i+2,0,top)
        top=advance(0,0,None)
        top=lax.fori_loop(0,(blocks-1)//2,body,top)
        last=0
        if blocks%2==0:
            top=advance(blocks-1,1,top)
            last=1
        mixed=jnp.zeros((block,128),jnp.float32)
        for c in range(pieces):
            mixed=mix_piece(last,c,top,mixed)
        finish(blocks-1,top,mixed)
    out_ref[...]=o32_ref[...].astype(jnp.bfloat16)

def attend(projected,chunk,bias_vec,block=512,srows=128):
    length=projected.shape[0]
    heads=bias_vec.shape[0]
    f32,b16=jnp.float32,jnp.bfloat16
    spec=lambda c: pl.BlockSpec((length,128),lambda i,c=c:(0,c))
    full=pl.BlockSpec((length,128),lambda i:(0,0))
    shape=lambda kind: jax.ShapeDtypeStruct((length,128),kind)
    return pl.pallas_call(
        functools.partial(forward_kernel,heads,block,srows,LOG2E/8),
        grid=(1,),
        in_specs=[spec(3*chunk),spec(3*chunk+1),spec(3*chunk+2),pl.BlockSpec(bias_vec.shape,lambda i:(0,0))],
        out_specs=[full]*3,
        out_shape=[shape(b16),shape(f32),shape(f32)],
        scratch_shapes=[pltpu.VMEM((srows,2*length-srows),f32),pltpu.VMEM((length,128),b16),pltpu.VMEM((length,128),b16),pltpu.VMEM((2,block,length),f32)],
        compiler_params=pltpu.CompilerParams(vmem_limit_bytes=40*MIB),
        cost_estimate=pl.CostEstimate(flops=16*heads*length*length*64,bytes_accessed=8*MIB,transcendentals=heads*length*length),
        name="attend_forward",
    )(projected,projected,projected,bias_vec)

def backward_kernel(heads,bq,bk,srows,scale,q_ref,k_ref,v_ref,do_ref,o32_ref,lse_ref,bias_ref,out_ref,diag_ref,strip,grads,ka,va,kt,qa,da,dd,qd,dk_acc,dv_acc):
    length=q_ref.shape[0]
    width=strip.shape[1]
    full_width=2*length
    lanes=lane_iota(length)
    f32,b16=jnp.float32,jnp.bfloat16
    count=length//bk
    for head in range(heads):
        fill_strip(strip,bias_ref[head:head+1,:],srows,width)
        grads[...]=jnp.zeros_like(grads)
        kd=dup_head(k_ref[...],head)
        ka[:,:128]=kd.astype(b16)
        ka[:,128:]=jnp.where(lanes<3,1.0,0.0).astype(b16)
        kt[...]=jnp.transpose(kd).astype(b16)
        va[...]=jnp.where(lanes<64,dup_head(v_ref[...],head),jnp.where(lanes<67,1.0,0.0)).astype(b16)
        qa[:,:128]=split_query(q_ref[...],head,scale)
        qa[:,128:]=columns_at(lanes,0,three_parts(-lse_ref[:,head:head+1]),0.0).astype(b16)
        qd[...]=dup_head(q_ref[...],head).astype(b16)
        upstream=dup_head(do_ref[...],head)
        dd[...]=upstream.astype(b16)
        delta=0.5*jnp.sum(upstream*dup_head(o32_ref[...],head),axis=1,keepdims=True)
        da[...]=columns_at(lanes,64,three_parts(-delta),jnp.where(lanes<64,upstream,0.0)).astype(b16)
        dk_acc[...]=jnp.zeros_like(dk_acc)
        dv_acc[...]=jnp.zeros_like(dv_acc)
        def keep(columns,rows,values):
            held=out_ref[rows,columns].astype(f32)
            out_ref[rows,columns]=(jnp.where(lane_iota(values.shape[0])<64,held,values) if head else values).astype(b16)
        def query_block(qb,carry):
            qs=pl.ds(pl.multiple_of(qb*bq,bq),bq)
            def products(kb):
                ks=slice(kb*bk,(kb+1)*bk)
                raw=lax.dot_general(ka[ks,:],qa[qs,:],NT,preferred_element_type=f32)
                up=lax.dot_general(va[ks,:],da[qs,:],NT,preferred_element_type=f32)
                return raw,up
            def consume(kb,raw,up,dq):
                ks=slice(kb*bk,(kb+1)*bk)
                probs,score_grads=[],[]
                for part in range(bk//srows):
                    start=qb*bq+(length-srows)-kb*bk-part*srows
                    rows=slice(part*srows,(part+1)*srows)
                    prob=jnp.exp2(raw[rows]+strip[:,pl.ds(pl.multiple_of(start,128),bq)])
                    grad=prob*up[rows]
                    grads[:,pl.ds(pl.multiple_of(start+srows,128),bq)]+=grad
                    probs.append(prob.astype(b16))
                    score_grads.append(grad.astype(b16))
                low=jnp.concatenate(score_grads,axis=0)
                dv_acc[ks,:]+=jnp.dot(jnp.concatenate(probs,axis=0),dd[qs,:],preferred_element_type=f32)
                dk_acc[ks,:]+=jnp.dot(low,qd[qs,:],preferred_element_type=f32)
                return dq+jnp.dot(kt[:,ks],low,preferred_element_type=f32)
            dq=jnp.zeros((128,bq),f32)
            ready=products(0)
            for kb in range(count):
                following=products(kb+1) if kb+1<count else None
                dq=consume(kb,*ready,dq)
                ready=following
            keep(slice(0,128),qs,jnp.transpose(dq)*0.125)
            return carry
        lax.fori_loop(0,length//bq,query_block,0)
        every=slice(0,length)
        keep(slice(128,256),every,dk_acc[...]*0.125)
        keep(slice(256,384),every,dv_acc[...])
        total=grads[0:8,:]
        for part in range(1,srows//8):
            total=total+pltpu.roll(grads[8*part:8*part+8,:],full_width-8*part,1)
        row=lax.broadcasted_iota(jnp.int32,(8,full_width),0)
        for part in range(1,8):
            total=jnp.where(row==part,pltpu.roll(total,full_width-part,1),total)
        diag_ref[head:head+1,:]=jnp.sum(total,axis=0,keepdims=True)

def attend_back(projected,chunk,upstream,o32,lse,bias_vec,bq=512,bk=512,srows=128):
    length=projected.shape[0]
    heads=bias_vec.shape[0]
    f32,b16=jnp.float32,jnp.bfloat16
    spec=lambda c: pl.BlockSpec((length,128),lambda i,c=c:(0,c))
    full=pl.BlockSpec((length,128),lambda i:(0,0))
    vm=lambda kind,*shape: pltpu.VMEM(shape,kind)
    return pl.pallas_call(
        functools.partial(backward_kernel,heads,bq,bk,srows,LOG2E/8),
        grid=(1,),
        in_specs=[spec(3*chunk),spec(3*chunk+1),spec(3*chunk+2),full,full,full,pl.BlockSpec(bias_vec.shape,lambda i:(0,0))],
        out_specs=[pl.BlockSpec((length,384),lambda i:(0,0)),pl.BlockSpec((8,2*length),lambda i:(0,0))],
        out_shape=[jax.ShapeDtypeStruct((length,384),b16),jax.ShapeDtypeStruct((8,2*length),f32)],
        scratch_shapes=[vm(f32,srows,2*length-srows),vm(f32,srows,2*length),vm(b16,length,256),vm(b16,length,128),vm(b16,128,length),
            vm(b16,length,256),vm(b16,length,128),vm(b16,length,128),vm(b16,length,128),vm(f32,length,128),vm(f32,length,128)],
        compiler_params=pltpu.CompilerParams(vmem_limit_bytes=48*MIB),
        cost_estimate=pl.CostEstimate(flops=40*heads*length*length*64,bytes_accessed=12*MIB,transcendentals=heads*length*length),
        name="attend_backward",
    )(projected,projected,projected,upstream,o32,lse,bias_vec)

def gelu_pair(u):
    c=0.7978845608028654
    square=u*u
    t=jnp.tanh(c*u*(1.0+0.044715*square))
    half=0.5*(1.0+t)
    return u*half,half+(0.5*c)*u*(1.0-t*t)*(1.0+0.134145*square)

def expert_kernel(experts,cap,width,hidden_width,send_ref,cot_hbm,w1_hbm,w2_hbm,router_ref,home,result_out,dw1,dw2,router_part,
                  rows,cots,grads,results,row_grads,logit_grads,act,slope,w1,w2,rows_t,
                  local_sem,cot_sem,out_sem,s_rows,r_rows,s_home,r_home):
    f32,b16=jnp.float32,jnp.bfloat16
    pairs=experts//2
    me=lax.axis_index("exp")
    seq=lax.axis_index("seq")
    pair,side=me//2,me%2
    other=1-side
    def device(offset,member):
        return lax.rem(pair+offset+pairs,pairs)*2+member
    barrier=pltpu.get_barrier_semaphore()
    for step in range(1,experts):
        pl.semaphore_signal(barrier,inc=1,device_id=(lax.rem(me+step,experts),seq),device_id_type=MESH)
    load1=pltpu.make_async_copy(w1_hbm,w1,local_sem.at[0])
    load2=pltpu.make_async_copy(w2_hbm,w2,local_sem.at[1])
    own_rows=pltpu.make_async_copy(send_ref.at[me],rows.at[side],local_sem.at[2])
    local=[load1,load2,own_rows]
    cot_loads=[pltpu.make_async_copy(cot_hbm.at[device(-j,m)],cots.at[2*j+m],cot_sem.at[2*j+m]) for j in range(pairs) for m in range(2)]
    for copy in local+cot_loads:
        copy.start()
    pl.semaphore_wait(barrier,experts-1)
    def remote(src,dst,s,r,target):
        return pltpu.make_async_remote_copy(src_ref=src,dst_ref=dst,send_sem=s,recv_sem=r,device_id=(target,seq),device_id_type=MESH)
    started=[]
    def launch(copy):
        copy.start()
        started.append(copy)
    visit=[j for step in range(1,pairs//2+1) for j in sorted({step,pairs-step})]
    launch(remote(send_ref.at[device(0,other)],rows.at[side],s_rows.at[1],r_rows.at[side],device(0,other)))
    for j in visit:
        for m in range(2):
            member=side if m==0 else other
            launch(remote(send_ref.at[device(j,member)],rows.at[2*j+side],s_rows.at[2*j+m],r_rows.at[2*j+side],device(j,member)))
    def wait_slot(landing,r,slot):
        remote(landing,landing,s_rows.at[0],r.at[slot],me).wait_recv()
    chunk=512 if hidden_width%512==0 else 128
    steps=hidden_width//chunk
    lanes=lax.broadcasted_iota(jnp.int32,(2*cap,128),1)
    onehot=jnp.where(lanes==me,1.0,0.0)
    outputs=[]
    def process(j):
        x=rows[2*j:2*j+2].reshape(2*cap,width)
        base=2*j*cap
        span=slice(base,base+2*cap)
        logits=jnp.dot(x,router_ref[...],preferred_element_type=f32)
        logits=jnp.where(lanes<experts,logits,-jnp.inf)
        raised=jnp.exp(logits-jnp.max(logits,axis=1,keepdims=True))
        gates=raised/jnp.sum(raised,axis=1,keepdims=True)
        gate=jnp.sum(gates*onehot,axis=1,keepdims=True)
        for m in range(2):
            cot_loads[2*j+m].wait()
        cot=cots[2*j:2*j+2].reshape(2*cap,width).astype(f32)
        grads[span,:]=(gate*cot).astype(b16)
        def forward(step,carry):
            cols=pl.ds(pl.multiple_of(step*chunk,chunk),chunk)
            pre=jnp.dot(x,w1[:,cols],preferred_element_type=f32)
            a,d=gelu_pair(pre)
            act[span,cols]=a.astype(b16)
            slope[span,cols]=d.astype(b16)
            return carry
        lax.fori_loop(0,steps,forward,0)
        result=jnp.dot(act[span,:],w2[...],preferred_element_type=f32).astype(b16)
        results[2*j:2*j+2]=result.reshape(2,cap,width)
        for m in range(2):
            copy=pltpu.make_async_copy(results.at[2*j+m],result_out.at[device(-j,m)],out_sem.at[2*j+m])
            copy.start()
            outputs.append(copy)
        gate_grad=jnp.sum(cots[2*j:2*j+2].reshape(2*cap,width).astype(f32)*result.astype(f32),axis=1,keepdims=True)
        logit_grad=(gates*(onehot-gate)*gate_grad).astype(b16)
        logit_grads[span,:]=logit_grad
        def backward(step,carry):
            cols=pl.ds(pl.multiple_of(step*chunk,chunk),chunk)
            up=lax.dot_general(grads[span,:],w2[cols,:],NT,preferred_element_type=f32)
            up=up.astype(b16).astype(f32)*slope[span,cols].astype(f32)
            slope[span,cols]=up.astype(b16)
            return carry
        lax.fori_loop(0,steps,backward,0)
        back=lax.dot_general(slope[span,:],w1[...],NT,preferred_element_type=f32)
        back=back+lax.dot_general(logit_grad,router_ref[...],NT,preferred_element_type=f32)
        row_grads[2*j:2*j+2]=back.astype(b16).reshape(2,cap,width)
        for m in range(2):
            member=side if m==0 else other
            if j==0 and m==0:
                copy=pltpu.make_async_copy(row_grads.at[side],home.at[me],local_sem.at[3])
                copy.start()
                outputs.append(copy)
            else:
                launch(remote(row_grads.at[2*j+member],home.at[me],s_home.at[2*j+m],r_home.at[2*j+side],device(-j,member)))
    load1.wait()
    load2.wait()
    own_rows.wait()
    wait_slot(rows.at[other],r_rows,other)
    process(0)
    for j in visit:
        for m in range(2):
            wait_slot(rows.at[2*j+m],r_rows,2*j+m)
        process(j)
    rows_t[...]=jnp.transpose(rows[...].reshape(experts*cap,width))
    router_part[...]=jnp.dot(rows_t[...],logit_grads[...],preferred_element_type=f32)
    def weight_grads(step,carry):
        cols=pl.ds(pl.multiple_of(step*chunk,chunk),chunk)
        dw1[:,cols]=jnp.dot(rows_t[...],slope[:,cols],preferred_element_type=f32).astype(b16)
        dw2[cols,:]=lax.dot_general(act[:,cols],grads[...],TN,preferred_element_type=f32).astype(b16)
        return carry
    lax.fori_loop(0,steps,weight_grads,0)
    for j in range(pairs):
        for m in range(2):
            if j:
                wait_slot(home.at[device(j,m)],r_home,2*j+m)
    wait_slot(home.at[device(0,other)],r_home,other)
    for copy in outputs:
        copy.wait()
    for copy in started:
        copy.wait_send()

def expert_layer(send,cot,w1,w2,router,cid=20):
    experts,cap,width=send.shape
    hidden_width=w1.shape[1]
    b16=jnp.bfloat16
    block=jax.ShapeDtypeStruct((experts,cap,width),b16)
    anywhere=pl.BlockSpec(memory_space=pl.ANY)
    vmem=pl.BlockSpec(memory_space=pltpu.VMEM)
    dma=lambda n: pltpu.SemaphoreType.DMA((n,))
    blocks=pltpu.VMEM((experts,cap,width),b16)
    wide=pltpu.VMEM((experts*cap,hidden_width),b16)
    return pl.pallas_call(
        functools.partial(expert_kernel,experts,cap,width,hidden_width),
        in_specs=[anywhere]*4+[vmem],
        out_specs=[anywhere,anywhere,vmem,vmem,vmem],
        out_shape=[block,block,jax.ShapeDtypeStruct(w1.shape,b16),jax.ShapeDtypeStruct(w2.shape,b16),jax.ShapeDtypeStruct((width,128),jnp.float32)],
        scratch_shapes=[blocks,blocks,pltpu.VMEM((experts*cap,width),b16),blocks,blocks,pltpu.VMEM((experts*cap,128),b16),wide,wide,
            pltpu.VMEM(w1.shape,b16),pltpu.VMEM(w2.shape,b16),pltpu.VMEM((width,experts*cap),b16),
            dma(4)]+[dma(experts)]*6,
        compiler_params=pltpu.CompilerParams(collective_id=cid,has_side_effects=True,vmem_limit_bytes=60*MIB),
        cost_estimate=pl.CostEstimate(flops=12*experts*cap*width*hidden_width,bytes_accessed=40*MIB,transcendentals=experts*cap*hidden_width),
        name="expert_layer",
    )(send,cot,w1,w2,router)

def inverse_rms(values):
    return lax.rsqrt(jnp.mean(values*values,axis=-1,keepdims=True)+EPSILON)

def matmul(left,right,dims=NN):
    return lax.dot_general(left,right,dims,preferred_element_type=jnp.float32)

def swap_parts(values,axis):
    return lax.all_to_all(values,axis,split_axis=0,concat_axis=0,tiled=True)

def reversed_ids(ids):
    flip=np.eye(128,dtype=np.float32)[::-1]
    rows=ids.shape[0]//128
    flip_rows=np.eye(rows,dtype=np.float32)[::-1]
    grid=ids.astype(jnp.bfloat16).reshape(rows,128)
    grid=matmul(grid,jnp.asarray(flip,jnp.bfloat16)).astype(jnp.bfloat16)
    return matmul(jnp.asarray(flip_rows,jnp.bfloat16),grid).reshape(-1).astype(jnp.int32)

def offset_rows(ids,table):
    hot=(ids[None,:]==jnp.arange(table.shape[0],dtype=jnp.int32)[:,None]).astype(jnp.float32)
    return lax.dot_general(table,hot,TN,precision=lax.Precision.HIGHEST)

def shards(tokens,query_weight,key_weight,value_weight,out_weight,router_weight,attn_gain,moe_gain,bias_table,expert_in,expert_out,expert_id,slot_id,bucket_id,cotangent):
    f32,b16=jnp.float32,jnp.bfloat16
    seq_count,stretch,width=tokens.shape
    seq_devs=lax.axis_size("seq")
    experts=lax.axis_size("exp")
    devices=seq_devs*experts
    length=stretch*seq_devs
    count=seq_count*stretch
    capacity=(5*count+4*experts-1)//(4*experts)
    padded_cap=(capacity+15)//16*16
    buckets,heads=bias_table.shape
    head_dim=width//heads
    groups=seq_devs//seq_count
    own_heads=heads//groups
    per_chunk=2 if own_heads%2==0 else 1
    chunks=own_heads//per_chunk
    used=per_chunk*head_dim
    span=chunks*384
    row_block=width//devices
    place=lax.axis_index("seq")
    group=place%groups
    def by_group(weight):
        cut=weight.reshape(row_block,groups,chunks,used)
        return jnp.pad(cut,((0,0),(0,0),(0,0),(0,128-used)))
    stacked=jnp.stack([by_group(w) for w in (query_weight,key_weight,value_weight)],axis=3).reshape(row_block,groups*span)
    stacked_full=lax.all_gather(stacked,BOTH,axis=0,tiled=True)
    gains=jnp.stack([attn_gain,moe_gain],axis=1)
    small=jnp.pad(jnp.concatenate([router_weight,gains],axis=1),((0,0),(0,126-experts)))
    small_full=lax.all_gather(small,BOTH,axis=0,tiled=True)
    out_full=lax.all_gather(out_weight,BOTH,axis=0,tiled=True)
    first_full=lax.all_gather(expert_in,"seq",axis=2,tiled=True)[0]
    second_full=lax.all_gather(expert_out,"seq",axis=1,tiled=True)[0]
    copies=jnp.broadcast_to(tokens[:,None],(seq_count,groups,stretch,width)).reshape(seq_devs,stretch,width)
    own_sequence=swap_parts(copies,"seq").reshape(length,width).astype(f32)
    weight=lax.dynamic_slice_in_dim(stacked_full,group*span,span,axis=1)
    router_full=small_full[:,:experts]
    router_wide=jnp.where(jnp.arange(128)[None,:]<experts,small_full,jnp.zeros((),b16))
    attn_gain_full=small_full[:,experts].astype(f32)
    moe_gain_full=small_full[:,experts+1].astype(f32)
    zero_id=jnp.zeros((1,),jnp.int32)
    backward_ids=jnp.concatenate([zero_id,bucket_id])
    forward_ids=reversed_ids(jnp.concatenate([bucket_id,zero_id]))
    own_table=lax.dynamic_slice_in_dim(bias_table,group*own_heads,own_heads,axis=1)*LOG2E
    forward_bias=offset_rows(forward_ids,own_table)
    backward_bias=offset_rows(backward_ids,own_table)
    expert_pick=expert_id.reshape(count)
    slot_pick=slot_id.reshape(count)
    slots=experts*padded_cap
    position=jnp.where(slot_pick<capacity,expert_pick*padded_cap+slot_pick,slots)
    hot=(position[None,:]==jnp.arange(slots,dtype=jnp.int32)[:,None]).astype(b16)
    cot_rows=matmul(hot,cotangent.reshape(count,width)).astype(b16).reshape(experts,padded_cap,width)
    cot_arrived=swap_parts(cot_rows,"exp")
    normed=(own_sequence*inverse_rms(own_sequence)*attn_gain_full).astype(b16)
    projected=matmul(normed,weight).astype(b16)
    saved,attended_parts=[],[]
    for chunk in range(chunks):
        bias_rows=slice(chunk*per_chunk,(chunk+1)*per_chunk)
        out,out32,log_total=attend(projected,chunk,forward_bias[bias_rows])
        saved.append((out32,log_total))
        attended_parts.append(swap_parts(out[:,:used].reshape(seq_devs,stretch,used),"seq"))
    attended=jnp.stack(attended_parts,axis=2).reshape(seq_count,groups,stretch,own_heads*head_dim)
    attended=jnp.swapaxes(attended,1,2).reshape(count,width)
    tokens_f=tokens.astype(f32).reshape(count,width)
    hidden=tokens_f+matmul(attended,out_full)
    moe_inverse=inverse_rms(hidden)
    moe_in=(hidden*moe_inverse*moe_gain_full).astype(b16)
    send_rows=matmul(hot,moe_in).astype(b16).reshape(experts,padded_cap,width)
    home,result,first_grad,second_grad,router_part=expert_layer(send_rows,cot_arrived,first_full,second_full,router_wide)
    returned=swap_parts(result,"exp").reshape(slots,width)
    expert_in_grad=lax.psum_scatter(first_grad[None],"seq",scatter_dimension=2,tiled=True).astype(f32)
    expert_out_grad=lax.psum_scatter(second_grad[None],"seq",scatter_dimension=1,tiled=True).astype(f32)
    grad_out=cotangent.astype(f32).reshape(count,width)
    moe_in_grad=matmul(hot,home.reshape(slots,width),TN)
    weighted=moe_in_grad*moe_gain_full
    moe_gain_part=jnp.sum(moe_in_grad*hidden*moe_inverse,axis=0)
    inner=jnp.mean(weighted*hidden,axis=-1,keepdims=True)
    hidden_grad=grad_out+weighted*moe_inverse-hidden*(moe_inverse*moe_inverse*moe_inverse)*inner
    branch_grad=hidden_grad.astype(b16)
    heads_grad=matmul(branch_grad,out_full,NT).astype(b16)
    outgoing=heads_grad.reshape(seq_count,stretch,groups,chunks,used)
    outgoing=jnp.transpose(outgoing,(3,0,2,1,4))
    arriving=[swap_parts(outgoing[chunk].reshape(seq_devs,stretch,used),"seq").reshape(length,used) for chunk in range(chunks)]
    out_part=matmul(attended,branch_grad,TN)
    extra=jnp.pad(jnp.concatenate([router_part[:,:experts],moe_gain_part[:,None]],axis=1),((0,0),(0,127-experts)))
    out_piece=jnp.concatenate([out_part,extra],axis=1).astype(b16).reshape(devices,row_block,width+128)
    out_sum=jnp.sum(swap_parts(out_piece,BOTH).astype(f32),axis=0)
    logits=matmul(moe_in,router_full)
    gates=jax.nn.softmax(logits,axis=-1)
    picked=(expert_pick[:,None]==jnp.arange(experts,dtype=jnp.int32)[None,:]).astype(f32)
    gate=jnp.sum(gates*picked,axis=-1)
    output=(hidden+gate[:,None]*matmul(hot,returned,TN)).astype(b16).reshape(seq_count,stretch,width)
    diagonals,token_grads,weight_sums=[],[],[]
    hot_bucket=(backward_ids[None,:]==jnp.arange(buckets,dtype=jnp.int32)[:,None]).astype(f32)
    hot_bucket=hot_bucket*(jnp.arange(length*2)>0)[None,:]
    for chunk in range(chunks):
        bias_rows=slice(chunk*per_chunk,(chunk+1)*per_chunk)
        upstream=jnp.pad(arriving[chunk],((0,0),(0,128-used)))
        grads,diagonal=attend_back(projected,chunk,upstream,*saved[chunk],backward_bias[bias_rows])
        diagonals.append(diagonal[:per_chunk])
        token_grads.append(swap_parts(grads.reshape(seq_devs,stretch,384),"seq").reshape(seq_count,groups,stretch,384))
        piece=matmul(normed,grads,TN).astype(b16).reshape(devices,row_block,384)
        if chunk==chunks-1:
            table_part=lax.dot_general(hot_bucket,jnp.concatenate(diagonals,axis=0),NT,precision=lax.Precision.HIGHEST)
            high=table_part.astype(b16)
            low=(table_part-lax.reduce_precision(table_part,8,7)).astype(b16)
            values=jnp.concatenate([high.reshape(-1),low.reshape(-1)])
            values=jnp.pad(values,(0,row_block*128-values.shape[0])).reshape(1,row_block,128)
            piece=jnp.concatenate([piece,jnp.broadcast_to(values,(devices,row_block,128))],axis=2)
        weight_sums.append(swap_parts(piece,BOTH))
    table_values=weight_sums[-1][:,:,384:].astype(f32).reshape(devices//groups,groups,row_block*128)
    table_values=jnp.sum(table_values,axis=0)[:,:2*buckets*own_heads].reshape(groups,2,buckets,own_heads)
    bias_table_grad=jnp.transpose(jnp.sum(table_values,axis=1),(1,0,2)).reshape(buckets,heads)
    normed_grad=jnp.zeros((count,width),f32)
    for chunk in range(chunks):
        for owner in range(groups):
            start=owner*span+chunk*384
            normed_grad=normed_grad+matmul(token_grads[chunk][:,owner].reshape(count,384),stacked_full[:,start:start+384],NT)
    summed=[jnp.sum(part[:,:,:384].astype(f32).reshape(devices//groups,groups,row_block,3,128)[...,:used],axis=0) for part in weight_sums]
    summed=jnp.stack(summed,axis=1)
    weight_grads=jnp.transpose(summed,(3,2,0,1,4)).reshape(3,row_block,width)
    own_weights=jnp.stack([query_weight,key_weight,value_weight]).astype(f32)
    attn_gain_grad=jnp.sum(weight_grads*own_weights,axis=(0,2))/attn_gain.astype(f32)
    tokens_inverse=inverse_rms(tokens_f)
    weighted=normed_grad*attn_gain_full
    inner=jnp.mean(weighted*tokens_f,axis=-1,keepdims=True)
    input_grad=hidden_grad+weighted*tokens_inverse-tokens_f*(tokens_inverse*tokens_inverse*tokens_inverse)*inner
    return (
        output,
        input_grad.reshape(seq_count,stretch,width),
        weight_grads[0],weight_grads[1],weight_grads[2],
        out_sum[:,:width],
        out_sum[:,width:width+experts],
        attn_gain_grad,
        out_sum[:,width+experts],
        bias_table_grad,
        expert_in_grad,
        expert_out_grad,
    )

def solution(mesh):
    tokens=P("exp","seq",None)
    rows=P(BOTH,None)
    return jax.shard_map(
        shards,
        mesh=mesh,
        in_specs=(tokens,rows,rows,rows,rows,rows,P(BOTH),P(BOTH),P(),P("exp",None,"seq"),P("exp","seq",None),P("exp","seq"),P("exp","seq"),P(),tokens),
        out_specs=(tokens,tokens,rows,rows,rows,rows,rows,P(BOTH),P(BOTH),P(),P("exp",None,"seq"),P("exp","seq",None)),
        check_vma=False,
    )
```

time: 806 us -> 711 us (0.88)
  matrix products: 140 us -> 68 us
  waiting for transfers between devices: 146 us -> 103 us
  Pallas kernels: 208 us -> 247 us
  blocking collectives: 136 us -> 119 us
    dot_general x22 -> x19, matrix products: 139 us -> 66.2 us  [matmul(): lax.dot_general(left, right, dims, preferred_element_type=jnp.float32)]
    psum x1 -> x0, blocking collectives: 62.9 us -> none  [shards(): bias_table_grad = lax.psum(table_wide, BOTH)]
    all_to_all x0 -> x2, blocking collectives: none -> 46.5 us  [swap_parts(): return lax.all_to_all(values, axis, split_axis=0, concat_axis=0, tiled=True)]
    all_to_all x14, waiting for transfers between devices: 144 us -> 100 us  [swap_parts(): return lax.all_to_all(values, axis, split_axis=0, concat_axis=0, tiled=True)]
    pallas_call x6 -> x7, Pallas kernels: 208 us -> 247 us  [the longest x3 114 us: attend_back(): pl.pallas_call(functools.partial(backward_kernel, heads, bq, bk, srows, L...]
    unnamed x80 -> x138, local copies, waits for them, and re-layouts: 18.5 us -> 28 us
  transfers between devices with their start and end apart: 20 -> 20, of which waited for: 7 -> 8; matrix products, arithmetic and copies ran while one was open for 27% -> 17% of each run, Pallas kernels for 26% -> 22%
where the time goes in v1:
time: 711 us; the launch traced here: 704 us
  Pallas kernels  247 us (35%)
  blocking collectives  119 us (17%)
  waiting for transfers between devices  103 us (14%)
  matrix products  68 us (10%)
  local copies, waits for them, and re-layouts  67.2 us (9%)
  starting transfers between devices  56.9 us (8%)
  other arithmetic  28.1 us (4%)
  between operations  15.6 us (2%)
    pallas_call x3, Pallas kernels, attend_back(): pl.pallas_call(functools.partial(backward_kernel, heads, bq, bk, srows, L...  114 us
    all_to_all x14, waiting for transfers between devices, swap_parts(): return lax.all_to_all(values, axis, split_axis=0, concat_axis=0, tiled=True)  100 us
    pallas_call x1, Pallas kernels, expert_layer(): pl.pallas_call(functools.partial(expert_kernel, experts, cap, width, hidd...  94.4 us
    all_gather x1, blocking collectives, shards(): small_full = lax.all_gather(small, BOTH, axis=0, tiled=True)  72.8 us
    dot_general x19, matrix products, matmul(): lax.dot_general(left, right, dims, preferred_element_type=jnp.float32)  66.2 us
    all_to_all x14, starting transfers between devices, swap_parts(): return lax.all_to_all(values, axis, split_axis=0, concat_axis=0, tiled=True)  56.7 us
    all_to_all x2, blocking collectives, swap_parts(): return lax.all_to_all(values, axis, split_axis=0, concat_axis=0, tiled=True)  46.5 us
    pallas_call x3, Pallas kernels, attend(): pl.pallas_call(functools.partial(forward_kernel, heads, block, srows, LOG...  37.7 us
  transfers between devices with their start and end apart: 20, of which 8 were waited for; matrix products, arithmetic and copies ran while one was open for 17% of the time, Pallas kernels for 22%

profile of v1, /device:TPU:0, one launch (start us, length us, event | category | flops | bytes accessed | tf_op | source)
XLA Modules:
  0.0 704.5 jit_solution(10207314451842382000)
XLA Ops:
  14.2 4.4 all-to-all-start
  19.6 72.8 %all_gather.15 = bf16[768,128]{1,0:T(8,128)(2,1)S(1)} all-gather(bf16[24,128]{1,0:T(8,128)(2,1)S(1)} %fusion.64), channel_id=1, replica_groups=mesh['exp'=8,'seq'=4] {'exp','seq'}, dimensions={0}, use_global_device_ids=true | all-gather | bytes 202752 | tf_op jit(solution)/shard_map/all_gather | solution.py:421
  97.8 7.2 %convolution_convert_fusion.q_ref.k_ref.v_ref = bf16[2048,1152]{1,0:T(8,128)(2,1)S(1)} fusion(bf16[2048,768]{1,0:T(8,128)(2,1)S(1)} %fusion.1, bf16[768,2304]{1,0:T(8,128)(2,1)} %all-gather.5.cloned.1.call-done, s32[]{:T(128)S(6)} %select_n.26), kind=kOutput, calls=%fused_computation | convolution fusion | flops 3626237952 | bytes 9633796 | tf_op jit(solution)/shard_map/dot_general | solution.py:376
  105.0 12.6 %attend_forward.5 = (bf16[2048,128]{1,0:T(8,128)(2,1)S(1)}, f32[2048,128]{1,0:T(8,128)S(1)}, f32[2048,128]{1,0:T(8,128)S(1)}) custom-call(bf16[2048,1152]{1,0:T(8,128)(2,1)S(1)} %convolution_convert_fusion.q_ref.k_ref.v_ref, bf16[2048,1152]{1,0:T(8,128)(2,1)S(1)} %convolution_convert_fusion.q_ref.k_ref.v_ref, ...), custom_call_target="tpu_custom_call" | custom-call | flops 8589934592 | bytes 8388608 | tf_op jit(solution)/shard_map/attend_forward/pallas_call | solution.py:125
  126.5 12.4 %attend_forward.4 = (bf16[2048,128]{1,0:T(8,128)(2,1)S(1)}, f32[2048,128]{1,0:T(8,128)S(1)}, f32[2048,128]{1,0:T(8,128)S(1)}) custom-call(bf16[2048,1152]{1,0:T(8,128)(2,1)S(1)} %copy-done.4, bf16[2048,1152]{1,0:T(8,128)(2,1)S(1)} %copy-done.4, bf16[2048,1152]{1,0:T(8,128)(2,1)S(1)} %copy-done.4, f32[2,4096]{1,0:T(2,128)S(1)} %get-tuple-element.145.bias_ref), custom_call_target="tpu_custom_call" | custom-call | flops 8589934592 | bytes 8388608 | tf_op jit(solution)/shard_map/attend_forward/pallas_call | solution.py:125
  147.7 12.6 %attend_forward.3 = (bf16[2048,128]{1,0:T(8,128)(2,1)S(1)}, f32[2048,128]{1,0:T(8,128)S(1)}, f32[2048,128]{1,0:T(8,128)S(1)}) custom-call(bf16[2048,1152]{1,0:T(8,128)(2,1)S(1)} %copy-done.5, bf16[2048,1152]{1,0:T(8,128)(2,1)S(1)} %copy-done.5, bf16[2048,1152]{1,0:T(8,128)(2,1)S(1)} %copy-done.5, f32[2,4096]{1,0:T(2,128)S(1)} %get-tuple-element.143.bias_ref), custom_call_target="tpu_custom_call" | custom-call | flops 8589934592 | bytes 8388608 | tf_op jit(solution)/shard_map/attend_forward/pallas_call | solution.py:125
  166.8 5.1 fusion.7
  171.9 8.2 %all-to-all-done.1 = bf16[4,512,128]{1,2,0:T(8,128)(2,1)S(1)} async-done(((bf16[4,512,128]{1,2,0:T(8,128)(2,1)}), bf16[4,512,128]{1,2,0:T(8,128)(2,1)S(1)}, u32[]{:S(2)}, u32[]{:S(2)}) %all-to-all-start.1) | async-done | bytes 524320 | tf_op jit(solution)/shard_map/all_to_all | solution.py:379
  180.1 4.5 all-to-all-start.4
  201.6 28.8 %all-to-all-done.4.cot_hbm = bf16[8,160,768]{2,1,0:T(8,128)(2,1)} async-done(((bf16[8,160,768]{2,1,0:T(8,128)(2,1)}), bf16[8,160,768]{2,1,0:T(8,128)(2,1)}, u32[]{:S(2)}, u32[]{:S(2)}) %all-to-all-start.4) | async-done | bytes 1966112 | tf_op jit(solution)/shard_map/all_to_all | solution.py:379
  230.4 94.4 %expert_layer.1 = (bf16[8,160,768]{2,1,0:T(8,128)(2,1)}, bf16[8,160,768]{2,1,0:T(8,128)(2,1)}, bf16[768,3072]{1,0:T(8,128)(2,1)}, bf16[3072,768]{1,0:T(8,128)(2,1)}, f32[768,128]{1,0:T(8,128)}) custom-call(bf16[8,160,768]{2,1,0:T(8,128)(2,1)} %bitcast.182, bf16[8,160,768]{2,1,0:T(8,128)(2,1)} %all-to-all-done.4.cot_hbm, bf16[768,3072]{1,0:T(8,128)(2,1)} %bitcast.180, ...), custom_call_target="tpu_custom_call" | custom-call | flops 36238786560 | bytes 41943040 | tf_op jit(solution)/shard_map/expert_layer/pallas_call | solution.py:359
  324.8 4.6 multiply_reduce_fusion.1
  343.7 6.5 all-to-all-done.8
  350.2 4.0 all-to-all-start.10
  356.7 37.7 %attend_backward.4 = (bf16[2048,384]{1,0:T(8,128)(2,1)S(1)}, f32[8,4096]{1,0:T(8,128)S(1)}) custom-call(bf16[2048,1152]{1,0:T(8,128)(2,1)} %copy-done.3, bf16[2048,1152]{1,0:T(8,128)(2,1)} %copy-done.3, bf16[2048,1152]{1,0:T(8,128)(2,1)} %copy-done.3, bf16[2048,128]{1,0:T(8,128)(2,1)S(1)} %bitcast.131, f32[2048,128]{1,0:T(8,128)S(1)} %copy-done.15, ...), custom_call_target="tpu_custom_call" | custom-call | flops 21474836480 | bytes 12582912 | tf_op jit(solution)/shard_map/attend_backward/pallas_call | solution.py:213
  397.9 4.5 convolution_convert_fusion.3
  402.4 4.3 all-to-all-done.6
  412.2 39.2 %attend_backward.3 = (bf16[2048,384]{1,0:T(8,128)(2,1)}, f32[8,4096]{1,0:T(8,128)S(1)}) custom-call(bf16[2048,1152]{1,0:T(8,128)(2,1)} %copy-done.3, bf16[2048,1152]{1,0:T(8,128)(2,1)} %copy-done.3, bf16[2048,1152]{1,0:T(8,128)(2,1)} %copy-done.3, bf16[2048,128]{1,0:T(8,128)(2,1)S(1)} %bitcast.132, f32[2048,128]{1,0:T(8,128)S(1)} %copy-done.11, ...), custom_call_target="tpu_custom_call" | custom-call | flops 21474836480 | bytes 12582912 | tf_op jit(solution)/shard_map/attend_backward/pallas_call | solution.py:213
  451.3 4.0 convolution_convert_fusion.4
  455.4 5.9 all-to-all-start.12
  464.8 37.6 %attend_backward.5 = (bf16[2048,384]{1,0:T(8,128)(2,1)S(1)}, f32[8,4096]{1,0:T(8,128)S(1)}) custom-call(bf16[2048,1152]{1,0:T(8,128)(2,1)} %copy-done.3, bf16[2048,1152]{1,0:T(8,128)(2,1)} %copy-done.3, bf16[2048,1152]{1,0:T(8,128)(2,1)} %copy-done.3, bf16[2048,128]{1,0:T(8,128)(2,1)S(1)} %bitcast.130, f32[2048,128]{1,0:T(8,128)S(1)} %copy-done.7, ...), custom_call_target="tpu_custom_call" | custom-call | flops 21474836480 | bytes 12582912 | tf_op jit(solution)/shard_map/attend_backward/pallas_call | solution.py:213
  503.2 23.2 %all_to_all.80 = bf16[4,512,384]{2,1,0:T(8,128)(2,1)} all-to-all(bf16[4,512,384]{2,1,0:T(8,128)(2,1)S(1)} %bitcast.129), channel_id=1, replica_groups=mesh['exp'=8,'seq'=4] {'seq'}, dimensions={0} | all-to-all | bytes 3145728 | tf_op jit(solution)/shard_map/all_to_all | solution.py:379
  526.4 23.3 %all_to_all.81 = bf16[4,512,384]{2,1,0:T(8,128)(2,1)} all-to-all(bf16[4,512,384]{2,1,0:T(8,128)(2,1)S(1)} %bitcast.128), channel_id=1, replica_groups=mesh['exp'=8,'seq'=4] {'seq'}, dimensions={0} | all-to-all | bytes 3145728 | tf_op jit(solution)/shard_map/all_to_all | solution.py:379
  549.7 4.3 all-to-all-start.7
  561.5 12.7 %all-to-all-done.7 = bf16[4,512,384]{2,1,0:T(8,128)(2,1)} async-done(((bf16[4,512,384]{2,1,0:T(8,128)(2,1)}), bf16[4,512,384]{2,1,0:T(8,128)(2,1)}, u32[]{:S(2)}, u32[]{:S(2)}) %all-to-all-start.7) | async-done | bytes 1572896 | tf_op jit(solution)/shard_map/all_to_all | solution.py:379
  574.2 4.9 all-to-all-start.14
  587.5 12.2 %all-to-all-done.14 = bf16[32,24,512]{2,1,0:T(8,128)(2,1)} async-done(((bf16[32,24,512]{2,1,0:T(8,128)(2,1)}), bf16[32,24,512]{2,1,0:T(8,128)(2,1)}, u32[]{:S(2)}, u32[]{:S(2)}) %all-to-all-start.14) | async-done | bytes 786464 | tf_op jit(solution)/shard_map/all_to_all | solution.py:379
  629.3 7.4 %all-to-all-done.15 = bf16[32,24,896]{2,1,0:T(8,128)(2,1)} async-done(((bf16[32,24,896]{2,1,0:T(8,128)(2,1)}), bf16[32,24,896]{2,1,0:T(8,128)(2,1)}, u32[]{:S(2)}, u32[]{:S(2)}) %all-to-all-start.15) | async-done | bytes 1376288 | tf_op jit(solution)/shard_map/all_to_all | solution.py:379
  636.8 4.6 all-to-all-start.5
  645.9 4.1 fusion.11
  666.1 20.4 %all-to-all-done.5 = bf16[8,160,768]{2,1,0:T(8,128)(2,1)} async-done(((bf16[8,160,768]{2,1,0:T(8,128)(2,1)}), bf16[8,160,768]{2,1,0:T(8,128)(2,1)}, u32[]{:S(2)}, u32[]{:S(2)}) %all-to-all-start.5) | async-done | bytes 1966112 | tf_op jit(solution)/shard_map/all_to_all | solution.py:379
  686.5 5.2 add_convert_fusion
  (284 shorter events, 155.4 us)
Async XLA Ops:
  7.2 90.6 %all-gather.5.cloned.1.call-start = ((), (), s32[]{:S(2)}) async-start(), calls=%async_computation.18 | async-start | bytes 3649536 | tf_op jit(solution)/shard_map/all_gather | solution.py:418
  10.7 181.9 %all-gather.7.cloned.1.call-start = ((), (), s32[]{:S(2)}) async-start(), calls=%async_computation.19 | async-start | bytes 1216512 | tf_op jit(solution)/shard_map/all_gather | solution.py:422
  11.5 218.9 %all-gather.9.cloned.1.call-start = ((), (), s32[]{:S(2)}) async-start(), calls=%async_computation.20 | async-start | bytes 5898240 | tf_op jit(solution)/shard_map/all_gather | solution.py:423
  14.1 78.2 %copy-start.55 = (bf16[128,128]{1,0:T(8,128)(2,1)S(1)}, bf16[128,128]{1,0:T(8,128)(2,1)}, u32[]{:S(2)}) copy-start(bf16[128,128]{1,0:T(8,128)(2,1)} %constant.66.clone) | copy-start | bytes 98308
  14.1 78.2 %copy-start.57 = (bf16[32,32]{1,0:T(8,128)(2,1)S(1)}, bf16[32,32]{1,0:T(8,128)(2,1)}, u32[]{:S(2)}) copy-start(bf16[32,32]{1,0:T(8,128)(2,1)} %constant.67.clone) | copy-start | bytes 6148
  14.2 78.9 %copy-start.56 = (f32[32,12]{0,1:T(8,128)S(1)}, f32[32,12]{0,1:T(8,128)}, u32[]{:S(2)}) copy-start(f32[32,12]{0,1:T(8,128)} %param.25) | copy-start | bytes 4612
  14.2 79.2 %all-to-all-start = ((bf16[4,512,768]{2,1,0:T(8,128)(2,1)}), bf16[4,512,768]{2,1,0:T(8,128)(2,1)S(1)}, u32[]{:S(2)}, u32[]{:S(2)}) async-start(bf16[4,512,768]{2,1,0:T(8,128)(2,1)} %bitcast.136), calls=%async_computation | async-start | bytes 6291456 | tf_op jit(solution)/shard_map/all_to_all | solution.py:379
  18.6 211.8 %all-gather.11.cloned.1.call-start = ((), (), s32[]{:S(2)}) async-start(), calls=%async_computation.21 | async-start | bytes 5898240 | tf_op jit(solution)/shard_map/all_gather | solution.py:424
  19.5 78.2 %copy-start.51 = (s32[1,4,2,128]{3,1,2,0:T(4,128)}, s32[1,4,2,128]{3,1,2,0:T(4,128)S(1)}, u32[]{:S(2)}) copy-start(s32[1,4,2,128]{3,1,2,0:T(4,128)S(1)} %copy.143) | copy-start | bytes 12292
  92.4 93.2 %copy-start.34 = (bf16[768,128]{1,0:T(8,128)(2,1)}, bf16[768,128]{1,0:T(8,128)(2,1)S(1)}, u32[]{:S(2)}) copy-start(bf16[768,128]{1,0:T(8,128)(2,1)S(1)} %all_gather.15) | copy-start | bytes 589828
  120.7 21.3 %all-to-all-start.3 = ((bf16[4,512,128]{1,2,0:T(8,128)(2,1)}), bf16[4,512,128]{1,2,0:T(8,128)(2,1)S(1)}, u32[]{:S(2)}, u32[]{:S(2)}) async-start(bf16[4,512,128]{1,2,0:T(8,128)(2,1)} %copy.121), calls=%async_computation.3 | async-start | bytes 1048576 | tf_op jit(solution)/shard_map/all_to_all | solution.py:379
  141.9 21.4 %all-to-all-start.2 = ((bf16[4,512,128]{1,2,0:T(8,128)(2,1)}), bf16[4,512,128]{1,2,0:T(8,128)(2,1)S(1)}, u32[]{:S(2)}, u32[]{:S(2)}) async-start(bf16[4,512,128]{1,2,0:T(8,128)(2,1)} %copy.120), calls=%async_computation.2 | async-start | bytes 1048576 | tf_op jit(solution)/shard_map/all_to_all | solution.py:379
  163.4 16.8 %all-to-all-start.1 = ((bf16[4,512,128]{1,2,0:T(8,128)(2,1)}), bf16[4,512,128]{1,2,0:T(8,128)(2,1)S(1)}, u32[]{:S(2)}, u32[]{:S(2)}) async-start(bf16[4,512,128]{1,2,0:T(8,128)(2,1)} %copy.119), calls=%async_computation.1 | async-start | bytes 1048576 | tf_op jit(solution)/shard_map/all_to_all | solution.py:379
  180.1 50.3 %all-to-all-start.4 = ((bf16[8,160,768]{2,1,0:T(8,128)(2,1)}), bf16[8,160,768]{2,1,0:T(8,128)(2,1)}, u32[]{:S(2)}, u32[]{:S(2)}) async-start(bf16[8,160,768]{2,1,0:T(8,128)(2,1)} %bitcast.159), calls=%async_computation.4 | async-start | bytes 3932160 | tf_op jit(solution)/shard_map/all_to_all | solution.py:379
  230.4 94.4 %copy-start.27 = (f32[1024,768]{1,0:T(8,128)S(1)}, f32[1024,768]{1,0:T(8,128)}, u32[]{:S(2)}) copy-start(f32[1024,768]{1,0:T(8,128)} %copy-done.26) | copy-start | bytes 9437188
  337.9 12.3 %all-to-all-start.8 = ((bf16[4,512,128]{2,1,0:T(8,128)(2,1)}), bf16[4,512,128]{2,1,0:T(8,128)(2,1)S(1)}, u32[]{:S(2)}, u32[]{:S(2)}) async-start(bf16[4,512,128]{2,1,0:T(8,128)(2,1)} %bitcast.31), calls=%async_computation.8 | async-start | bytes 1048576 | tf_op jit(solution)/shard_map/all_to_all | solution.py:379
  341.4 350.3 %reduce-scatter.3.cloned.1.call-start = ((), (), s32[]{:S(2)}) async-start(), calls=%async_computation.22 | async-start | bytes 5898240 | tf_op jit(solution)/shard_map/reduce_scatter | solution.py:462
  350.2 44.2 %all-to-all-start.10 = ((bf16[4,512,128]{2,1,0:T(8,128)(2,1)}), bf16[4,512,128]{2,1,0:T(8,128)(2,1)S(1)}, u32[]{:S(2)}, u32[]{:S(2)}) async-start(bf16[4,512,128]{2,1,0:T(8,128)(2,1)} %bitcast.37), calls=%async_computation.10 | async-start | bytes 1048576 | tf_op jit(solution)/shard_map/all_to_all | solution.py:379
  394.4 12.3 %all-to-all-start.6 = ((bf16[4,512,128]{2,1,0:T(8,128)(2,1)}), bf16[4,512,128]{2,1,0:T(8,128)(2,1)S(1)}, u32[]{:S(2)}, u32[]{:S(2)}) async-start(bf16[4,512,128]{2,1,0:T(8,128)(2,1)} %bitcast.155), calls=%async_computation.6 | async-start | bytes 1048576 | tf_op jit(solution)/shard_map/all_to_all | solution.py:379
  406.7 48.7 %all-to-all-start.13 = ((bf16[32,24,384]{2,1,0:T(8,128)(2,1)}), bf16[32,24,384]{2,1,0:T(8,128)(2,1)S(1)}, u32[]{:S(2)}, u32[]{:S(2)}) async-start(bf16[32,24,384]{2,1,0:T(8,128)(2,1)} %bitcast.154), calls=%async_computation.13 | async-start | bytes 1179648 | tf_op jit(solution)/shard_map/all_to_all | solution.py:379
  412.2 39.2 %copy-start.19 = (bf16[2048,768]{1,0:T(8,128)(2,1)S(1)}, bf16[2048,768]{1,0:T(8,128)(2,1)}, u32[]{:S(2)}) copy-start(bf16[2048,768]{1,0:T(8,128)(2,1)} %copy-done.18) | copy-start | bytes 9437188
  455.4 47.8 %all-to-all-start.12 = ((bf16[32,24,384]{2,1,0:T(8,128)(2,1)}), bf16[32,24,384]{2,1,0:T(8,128)(2,1)}, u32[]{:S(2)}, u32[]{:S(2)}) async-start(bf16[32,24,384]{2,1,0:T(8,128)(2,1)} %bitcast.44), calls=%async_computation.12 | async-start | bytes 1179648 | tf_op jit(solution)/shard_map/all_to_all | solution.py:379
  549.7 24.5 %all-to-all-start.7 = ((bf16[4,512,384]{2,1,0:T(8,128)(2,1)}), bf16[4,512,384]{2,1,0:T(8,128)(2,1)}, u32[]{:S(2)}, u32[]{:S(2)}) async-start(bf16[4,512,384]{2,1,0:T(8,128)(2,1)} %bitcast.27), calls=%async_computation.7 | async-start | bytes 3145728 | tf_op jit(solution)/shard_map/all_to_all | solution.py:379
  554.0 140.5 %reduce-scatter.5.cloned.1.call-start = ((), (), s32[]{:S(2)}) async-start(), calls=%async_computation.23 | async-start | bytes 5898240 | tf_op jit(solution)/shard_map/reduce_scatter | solution.py:463
  556.7 22.4 %copy-start.23 = (bf16[2,512,768]{2,1,0:T(8,128)(2,1)S(1)}, bf16[2,512,768]{2,1,0:T(8,128)(2,1)}, u32[]{:S(2)}) copy-start(bf16[2,512,768]{2,1,0:T(8,128)(2,1)} %param.17) | copy-start | bytes 4718596
  560.5 20.4 %copy-start.32 = (bf16[128,8,2,384]{3,1,2,0:T(8,128)(2,1)S(1)}, bf16[128,8,2,384]{3,1,2,0:T(8,128)(2,1)}, u32[]{:S(2)}) copy-start(bf16[128,8,2,384]{3,1,2,0:T(8,128)(2,1)} %copy-done.31) | copy-start | bytes 4718596
  574.2 25.6 %all-to-all-start.14 = ((bf16[32,24,512]{2,1,0:T(8,128)(2,1)}), bf16[32,24,512]{2,1,0:T(8,128)(2,1)}, u32[]{:S(2)}, u32[]{:S(2)}) async-start(bf16[32,24,512]{2,1,0:T(8,128)(2,1)} %pad_maximum_fusion.2), calls=%async_computation.14 | async-start | bytes 1572864 | tf_op jit(solution)/shard_map/all_to_all | solution.py:379
  586.3 19.4 %copy-start.35 = (bf16[768,128]{1,0:T(8,128)(2,1)S(1)}, bf16[768,128]{1,0:T(8,128)(2,1)}, u32[]{:S(2)}) copy-start(bf16[768,128]{1,0:T(8,128)(2,1)} %copy-done.34) | copy-start | bytes 589828
  587.5 20.7 %copy-start.52 = (s32[1,4,2,128]{3,1,2,0:T(4,128)S(1)}, s32[1,4,2,128]{3,1,2,0:T(4,128)}, u32[]{:S(2)}) copy-start(s32[1,4,2,128]{3,1,2,0:T(4,128)} %copy-done.51) | copy-start | bytes 12292
  599.7 37.0 %all-to-all-start.15 = ((bf16[32,24,896]{2,1,0:T(8,128)(2,1)}), bf16[32,24,896]{2,1,0:T(8,128)(2,1)}, u32[]{:S(2)}, u32[]{:S(2)}) async-start(bf16[32,24,896]{2,1,0:T(8,128)(2,1)} %pad_maximum_fusion.1), calls=%async_computation.15 | async-start | bytes 2752512 | tf_op jit(solution)/shard_map/all_to_all | solution.py:379
  636.8 49.8 %all-to-all-start.5 = ((bf16[8,160,768]{2,1,0:T(8,128)(2,1)}), bf16[8,160,768]{2,1,0:T(8,128)(2,1)}, u32[]{:S(2)}, u32[]{:S(2)}) async-start(bf16[8,160,768]{2,1,0:T(8,128)(2,1)} %get-tuple-element.35), calls=%async_computation.5 | async-start | bytes 3932160 | tf_op jit(solution)/shard_map/all_to_all | solution.py:379
  654.1 32.4 %copy-start.28 = (f32[1024,768]{1,0:T(8,128)S(1)}, f32[1024,768]{1,0:T(8,128)}, u32[]{:S(2)}) copy-start(f32[1024,768]{1,0:T(8,128)} %copy-done.26) | copy-start | bytes 9437188
  (53 other events, 233.8 us)
Sparse Core Ops, SparseCore 0:
  11.5 63.9 all-gather.4
  78.4 54.0 all-gather.6
  134.1 46.5 all-gather.8
  182.1 37.2 all-gather.10
  344.4 47.3 reduce-scatter.2
  557.2 70.3 reduce-scatter.4

commit v2 on v1

--- a/solution.py
+++ b/solution.py
@@ -49,54 +49,94 @@
     strip[...]=turned[:,rows:]
 
 
-def forward_kernel(heads,block,srows,scale,q_ref,k_ref,v_ref,bias_ref,out_ref,o32_ref,lse_ref,strip,kd,va,scr):
-    length=q_ref.shape[0]
+def head_column(values,index):
+    return jnp.sum(jnp.where(lane_iota(values.shape[0])==index,values,0.0),axis=1,keepdims=True)
+
+def remote(src,dst,sent,received,target):
+    return pltpu.make_async_remote_copy(src_ref=src,dst_ref=dst,send_sem=sent,recv_sem=received,device_id=target,device_id_type=MESH)
+
+def loop(first,last,body):
+    def step(i,carry):
+        body(i)
+        return carry
+    lax.fori_loop(first,last,step,0)
+
+def forward_kernel(plan,block,srows,scale,proj_ref,bias_ref,cot_ref,att_out,o32_ref,lse_ref,cot_out,strip,kd,va,scr,outs,s_cot,r_cot,s_att,r_att,local_sem):
+    experts,seq_devs,seq_count,stretch,heads,chunks=plan
+    length=stretch*seq_devs
+    groups=seq_devs//seq_count
+    f32,b16=jnp.float32,jnp.bfloat16
+    me,place=lax.axis_index("exp"),lax.axis_index("seq")
+    sequence,group=place//groups,place%groups
+    barrier=pltpu.get_barrier_semaphore()
+    loop(1,experts,lambda i: pl.semaphore_signal(barrier,inc=1,device_id=(lax.rem(me+i,experts),place),device_id_type=MESH))
+    loop(1,seq_devs,lambda i: pl.semaphore_signal(barrier,inc=1,device_id=(me,lax.rem(place+i,seq_devs)),device_id_type=MESH))
+    own_cot=pltpu.make_async_copy(cot_ref.at[me],cot_out.at[me],local_sem.at[0])
+    own_cot.start()
+    pl.semaphore_wait(barrier,experts+seq_devs-2)
+    def send_cot(i):
+        target=lax.rem(me+i,experts)
+        return remote(cot_ref.at[target],cot_out.at[me],s_cot.at[i],r_cot.at[i],(target,place))
+    loop(1,experts,lambda i: send_cot(i).start())
+    def lanes_of(owner_group,c,size):
+        return pl.ds(pl.multiple_of((owner_group*chunks+c)*size,128),size)
+    def send_att(c,i):
+        target=lax.rem(place+i,seq_devs)
+        rows=pl.ds(pl.multiple_of(target*stretch,128),stretch)
+        return remote(outs.at[c,rows],att_out.at[sequence,:,lanes_of(group,c,128)],s_att.at[c,i],r_att.at[c,i],(me,target))
+    def own_att(c):
+        rows=pl.ds(pl.multiple_of(place*stretch,128),stretch)
+        return pltpu.make_async_copy(outs.at[c,rows],att_out.at[sequence,:,lanes_of(group,c,128)],local_sem.at[1+c])
     width=strip.shape[1]
     wide=256
     blocks=length//block
     pieces=length//wide
     lanes=lane_iota(length)
     block_lanes=lane_iota(block)
-    for head in range(heads):
-        fill_strip(strip,bias_ref[head:head+1,:],srows,width)
-        kd[...]=dup_head(k_ref[...],head).astype(jnp.bfloat16)
-        va[...]=jnp.where(lanes<64,dup_head(v_ref[...],head),jnp.where(lanes==64,1.0,0.0)).astype(jnp.bfloat16)
+    lse_ref[...]=jnp.zeros_like(lse_ref)
+    def attend_head(c,head):
+        index=c*heads+head
+        base=c*384
+        def columns(which):
+            return pl.ds(pl.multiple_of(base+which*128,128),128)
+        own=pl.ds(pl.multiple_of(c*128,128),128)
+        fill_strip(strip,bias_ref[pl.ds(index,1),:],srows,width)
+        kd[...]=dup_head(proj_ref[:,columns(1)],head).astype(b16)
+        va[...]=jnp.where(lanes<64,dup_head(proj_ref[:,columns(2)],head),jnp.where(lanes==64,1.0,0.0)).astype(b16)
         def rows_of(step):
             return pl.ds(pl.multiple_of(step*block,block),block)
-        def score_piece(step,qa,c,slot,top):
-            raw=lax.dot_general(qa,kd[c*wide:(c+1)*wide,:],NT,preferred_element_type=jnp.float32)
+        def score_piece(step,qa,p,slot,top):
+            raw=lax.dot_general(qa,kd[p*wide:(p+1)*wide,:],NT,preferred_element_type=f32)
             parts=[]
             for part in range(block//srows):
-                start=pl.multiple_of(length-srows-step*block-part*srows+c*wide,128)
+                start=pl.multiple_of(length-srows-step*block-part*srows+p*wide,128)
                 parts.append(raw[part*srows:(part+1)*srows]+strip[:,pl.ds(start,wide)])
             scores=jnp.concatenate(parts,axis=0)
-            scr[slot,:,c*wide:(c+1)*wide]=scores
+            scr[slot,:,p*wide:(p+1)*wide]=scores
             for j in range(wide//128):
                 top=jnp.maximum(top,scores[:,j*128:(j+1)*128])
             return top
-        def mix_piece(slot,c,top,total):
-            weights=jnp.exp2(scr[slot,:,c*wide:(c+1)*wide]-top).astype(jnp.bfloat16)
-            return total+jnp.dot(weights,va[c*wide:(c+1)*wide,:],preferred_element_type=jnp.float32)
+        def mix_piece(slot,p,top,total):
+            weights=jnp.exp2(scr[slot,:,p*wide:(p+1)*wide]-top).astype(b16)
+            return total+jnp.dot(weights,va[p*wide:(p+1)*wide,:],preferred_element_type=f32)
         def finish(step,top,mixed):
             rows=rows_of(step)
             total=mixed[:,64:65]
             result=mixed/total
-            log_total=top+jnp.log2(total)
+            lse_ref[rows,:]=jnp.where(block_lanes==index,top+jnp.log2(total),lse_ref[rows,:])
             if head==0:
-                lse_ref[rows,:]=jnp.broadcast_to(log_total,(block,128))
-                o32_ref[rows,:]=result
+                o32_ref[rows,own]=result
             else:
-                lse_ref[rows,:]=jnp.where(block_lanes==head,log_total,lse_ref[rows,:])
-                o32_ref[rows,:]=jnp.where(block_lanes<64,o32_ref[rows,:],pltpu.roll(result,64,1))
+                o32_ref[rows,own]=jnp.where(block_lanes<64,o32_ref[rows,own],pltpu.roll(result,64,1))
         def advance(step,slot,top):
             mixing=top is not None
-            qa=split_query(q_ref[rows_of(step),:],head,scale)
-            new=jnp.full((block,128),-jnp.inf,jnp.float32)
-            mixed=jnp.zeros((block,128),jnp.float32)
-            for c in range(pieces):
-                new=score_piece(step,qa,c,slot,new)
+            qa=split_query(proj_ref[rows_of(step),columns(0)],head,scale)
+            new=jnp.full((block,128),-jnp.inf,f32)
+            mixed=jnp.zeros((block,128),f32)
+            for p in range(pieces):
+                new=score_piece(step,qa,p,slot,new)
                 if mixing:
-                    mixed=mix_piece(1-slot,c,top,mixed)
+                    mixed=mix_piece(1-slot,p,top,mixed)
             if mixing:
                 finish(step-1,top,mixed)
             return jnp.max(new,axis=1,keepdims=True)
@@ -109,59 +149,140 @@
         if blocks%2==0:
             top=advance(blocks-1,1,top)
             last=1
-        mixed=jnp.zeros((block,128),jnp.float32)
-        for c in range(pieces):
-            mixed=mix_piece(last,c,top,mixed)
+        mixed=jnp.zeros((block,128),f32)
+        for p in range(pieces):
+            mixed=mix_piece(last,p,top,mixed)
         finish(blocks-1,top,mixed)
-    out_ref[...]=o32_ref[...].astype(jnp.bfloat16)
-
-def attend(projected,chunk,bias_vec,block=512,srows=128):
-    length=projected.shape[0]
-    heads=bias_vec.shape[0]
+    def one_chunk(c):
+        for head in range(heads):
+            attend_head(c,head)
+        outs[c]=o32_ref[:,pl.ds(pl.multiple_of(c*128,128),128)].astype(b16)
+        loop(1,seq_devs,lambda i: send_att(c,i).start())
+        own_att(c).start()
+    loop(0,chunks,one_chunk)
+    def land_att(c,i):
+        source=lax.rem(place-i+seq_devs,seq_devs)
+        landing=att_out.at[source//groups,:,lanes_of(source%groups,c,128)]
+        remote(landing,landing,s_att.at[c,i],r_att.at[c,i],(me,place)).wait_recv()
+    def finish_chunk(c):
+        own_att(c).wait()
+        loop(1,seq_devs,lambda i: land_att(c,i))
+        loop(1,seq_devs,lambda i: send_att(c,i).wait_send())
+    loop(0,chunks,finish_chunk)
+    def land_cot(i):
+        landing=cot_out.at[lax.rem(me-i+experts,experts)]
+        remote(landing,landing,s_cot.at[i],r_cot.at[i],(me,place)).wait_recv()
+    loop(1,experts,land_cot)
+    loop(1,experts,lambda i: send_cot(i).wait_send())
+    own_cot.wait()
+
+def attend(plan,projected,bias_vec,cot_rows,block=512,srows=128):
+    experts,seq_devs,seq_count,stretch,heads,chunks=plan
+    length=stretch*seq_devs
+    groups=seq_devs//seq_count
     f32,b16=jnp.float32,jnp.bfloat16
-    spec=lambda c: pl.BlockSpec((length,128),lambda i,c=c:(0,c))
-    full=pl.BlockSpec((length,128),lambda i:(0,0))
-    shape=lambda kind: jax.ShapeDtypeStruct((length,128),kind)
+    vmem=pl.BlockSpec(memory_space=pltpu.VMEM)
+    anywhere=pl.BlockSpec(memory_space=pl.ANY)
+    dma=lambda *shape: pltpu.SemaphoreType.DMA(shape)
     return pl.pallas_call(
-        functools.partial(forward_kernel,heads,block,srows,LOG2E/8),
-        grid=(1,),
-        in_specs=[spec(3*chunk),spec(3*chunk+1),spec(3*chunk+2),pl.BlockSpec(bias_vec.shape,lambda i:(0,0))],
-        out_specs=[full]*3,
-        out_shape=[shape(b16),shape(f32),shape(f32)],
-        scratch_shapes=[pltpu.VMEM((srows,2*length-srows),f32),pltpu.VMEM((length,128),b16),pltpu.VMEM((length,128),b16),pltpu.VMEM((2,block,length),f32)],
-        compiler_params=pltpu.CompilerParams(vmem_limit_bytes=40*MIB),
-        cost_estimate=pl.CostEstimate(flops=16*heads*length*length*64,bytes_accessed=8*MIB,transcendentals=heads*length*length),
+        functools.partial(forward_kernel,plan,block,srows,LOG2E/8),
+        in_specs=[vmem,vmem,anywhere],
+        out_specs=[anywhere,vmem,vmem,anywhere],
+        out_shape=[jax.ShapeDtypeStruct((seq_count,stretch,groups*chunks*128),b16),jax.ShapeDtypeStruct((length,chunks*128),f32),jax.ShapeDtypeStruct((length,128),f32),jax.ShapeDtypeStruct(cot_rows.shape,b16)],
+        scratch_shapes=[pltpu.VMEM((srows,2*length-srows),f32),pltpu.VMEM((length,128),b16),pltpu.VMEM((length,128),b16),pltpu.VMEM((2,block,length),f32),pltpu.VMEM((chunks,length,128),b16),
+            dma(experts),dma(experts),dma(chunks,seq_devs),dma(chunks,seq_devs),dma(1+chunks)],
+        compiler_params=pltpu.CompilerParams(collective_id=1,has_side_effects=True,vmem_limit_bytes=48*MIB),
+        cost_estimate=pl.CostEstimate(flops=16*heads*chunks*length*length*64,bytes_accessed=16*MIB,transcendentals=heads*chunks*length*length),
         name="attend_forward",
-    )(projected,projected,projected,bias_vec)
-
-def backward_kernel(heads,bq,bk,srows,scale,q_ref,k_ref,v_ref,do_ref,o32_ref,lse_ref,bias_ref,out_ref,diag_ref,strip,grads,ka,va,kt,qa,da,dd,qd,dk_acc,dv_acc):
-    length=q_ref.shape[0]
+    )(projected,bias_vec,cot_rows)
+
+def backward_kernel(plan,inside,bq,bk,srows,scale,proj_ref,o32_ref,lse_ref,bias_ref,normed_t,bucket_ref,up_ref,res_ref,piece_ref,
+                    grad_out,ret_out,piece_out,weight_out,table_out,
+                    strip,grads,ka,va,kt,qa,da,dd,qd,dk_acc,dv_acc,ups,outs,weight_parts,diag,table,
+                    s_up,r_up,s_res,r_res,s_piece,r_piece,s_grad,r_grad,s_weight,r_weight,s_table,r_table,local_sem,own_sem):
+    experts,seq_devs,seq_count,stretch,heads,chunks=plan
+    length=stretch*seq_devs
+    groups=seq_devs//seq_count
+    devices=experts*seq_devs
+    f32,b16=jnp.float32,jnp.bfloat16
+    me,place=lax.axis_index("exp"),lax.axis_index("seq")
+    sequence,group=place//groups,place%groups
+    rank=me*seq_devs+place
+    def other(i):
+        target=lax.rem(rank+i,devices)
+        return target,(target//seq_devs,target%seq_devs)
+    barrier=pltpu.get_barrier_semaphore()
+    loop(1,devices,lambda i: pl.semaphore_signal(barrier,inc=1,device_id=other(i)[1],device_id_type=MESH))
+    def lanes_of(owner_group,c,size):
+        return pl.ds(pl.multiple_of((owner_group*chunks+c)*size,128),size)
+    def rows_of(owner):
+        return pl.ds(pl.multiple_of(owner*stretch,128),stretch)
+    def send_up(c,i):
+        target=lax.rem(place+i,seq_devs)
+        return remote(up_ref.at[target//groups,:,lanes_of(target%groups,c,128)],ups.at[c,rows_of(place)],s_up.at[c,i],r_up.at[c,i],(me,target))
+    def own_up(c):
+        return pltpu.make_async_copy(up_ref.at[sequence,:,lanes_of(group,c,128)],ups.at[c,rows_of(place)],local_sem.at[0,c])
+    def send_res(i):
+        target=lax.rem(me+i,experts)
+        return remote(res_ref.at[target],ret_out.at[me],s_res.at[i],r_res.at[i],(target,place))
+    def send_piece(i):
+        target,where=other(i)
+        return remote(piece_ref.at[target],piece_out.at[rank],s_piece.at[i],r_piece.at[i],where)
+    def send_grad(c,i):
+        target=lax.rem(place+i,seq_devs)
+        return remote(outs.at[c,rows_of(target)],grad_out.at[sequence,:,lanes_of(group,c,384)],s_grad.at[c,i],r_grad.at[c,i],(me,target))
+    def own_grad(c):
+        return pltpu.make_async_copy(outs.at[c,rows_of(place)],grad_out.at[sequence,:,lanes_of(group,c,384)],local_sem.at[1,c])
+    def send_weight(c,i):
+        target,where=other(i)
+        return remote(weight_parts.at[c,target],weight_out.at[c,rank],s_weight.at[c,i],r_weight.at[c,i],where)
+    def own_weight(c):
+        return pltpu.make_async_copy(weight_parts.at[c,rank],weight_out.at[c,rank],local_sem.at[2,c])
+    def send_table(i):
+        return remote(table,table_out.at[rank],s_table.at[i],r_table.at[i],other(i)[1])
+    own_table=pltpu.make_async_copy(table,table_out.at[rank],own_sem.at[0])
+    own_res=pltpu.make_async_copy(res_ref.at[me],ret_out.at[me],own_sem.at[1])
+    own_piece=pltpu.make_async_copy(piece_ref.at[rank],piece_out.at[rank],own_sem.at[2])
+    def landed(landing,received):
+        remote(landing,landing,own_sem.at[3],received,(me,place)).wait_recv()
+    own_res.start()
+    own_piece.start()
+    loop(0,chunks,lambda c: own_up(c).start())
+    pl.semaphore_wait(barrier,devices-1)
+    loop(0,chunks,lambda c: loop(1,seq_devs,lambda i: send_up(c,i).start()))
     width=strip.shape[1]
     full_width=2*length
     lanes=lane_iota(length)
-    f32,b16=jnp.float32,jnp.bfloat16
     count=length//bk
-    for head in range(heads):
-        fill_strip(strip,bias_ref[head:head+1,:],srows,width)
+    if inside:
+        weight_parts[...]=jnp.zeros_like(weight_parts)
+    diag[...]=jnp.zeros_like(diag)
+    def head_back(c,head):
+        index=c*heads+head
+        def columns(which):
+            return pl.ds(pl.multiple_of(c*384+which*128,128),128)
+        query,key,value=[proj_ref[:,columns(which)] for which in range(3)]
+        fill_strip(strip,bias_ref[pl.ds(index,1),:],srows,width)
         grads[...]=jnp.zeros_like(grads)
-        kd=dup_head(k_ref[...],head)
+        kd=dup_head(key,head)
         ka[:,:128]=kd.astype(b16)
         ka[:,128:]=jnp.where(lanes<3,1.0,0.0).astype(b16)
         kt[...]=jnp.transpose(kd).astype(b16)
-        va[...]=jnp.where(lanes<64,dup_head(v_ref[...],head),jnp.where(lanes<67,1.0,0.0)).astype(b16)
-        qa[:,:128]=split_query(q_ref[...],head,scale)
-        qa[:,128:]=columns_at(lanes,0,three_parts(-lse_ref[:,head:head+1]),0.0).astype(b16)
-        qd[...]=dup_head(q_ref[...],head).astype(b16)
-        upstream=dup_head(do_ref[...],head)
+        va[...]=jnp.where(lanes<64,dup_head(value,head),jnp.where(lanes<67,1.0,0.0)).astype(b16)
+        qa[:,:128]=split_query(query,head,scale)
+        qa[:,128:]=columns_at(lanes,0,three_parts(-head_column(lse_ref[...],index)),0.0).astype(b16)
+        qd[...]=dup_head(query,head).astype(b16)
+        upstream=dup_head(ups[c],head)
         dd[...]=upstream.astype(b16)
-        delta=0.5*jnp.sum(upstream*dup_head(o32_ref[...],head),axis=1,keepdims=True)
+        delta=0.5*jnp.sum(upstream*dup_head(o32_ref[:,pl.ds(pl.multiple_of(c*128,128),128)],head),axis=1,keepdims=True)
         da[...]=columns_at(lanes,64,three_parts(-delta),jnp.where(lanes<64,upstream,0.0)).astype(b16)
         dk_acc[...]=jnp.zeros_like(dk_acc)
         dv_acc[...]=jnp.zeros_like(dv_acc)
-        def keep(columns,rows,values):
-            held=out_ref[rows,columns].astype(f32)
-            out_ref[rows,columns]=(jnp.where(lane_iota(values.shape[0])<64,held,values) if head else values).astype(b16)
-        def query_block(qb,carry):
+        def keep(part,rows,values):
+            if head:
+                values=jnp.where(lane_iota(values.shape[0])<64,outs[c,rows,part].astype(f32),values)
+            outs[c,rows,part]=values.astype(b16)
+        def query_block(qb):
             qs=pl.ds(pl.multiple_of(qb*bq,bq),bq)
             def products(kb):
                 ks=slice(kb*bk,(kb+1)*bk)
@@ -190,8 +311,7 @@
                 dq=consume(kb,*ready,dq)
                 ready=following
             keep(slice(0,128),qs,jnp.transpose(dq)*0.125)
-            return carry
-        lax.fori_loop(0,length//bq,query_block,0)
+        loop(0,length//bq,query_block)
         every=slice(0,length)
         keep(slice(128,256),every,dk_acc[...]*0.125)
         keep(slice(256,384),every,dv_acc[...])
@@ -201,27 +321,92 @@
         row=lax.broadcasted_iota(jnp.int32,(8,full_width),0)
         for part in range(1,8):
             total=jnp.where(row==part,pltpu.roll(total,full_width-part,1),total)
-        diag_ref[head:head+1,:]=jnp.sum(total,axis=0,keepdims=True)
-
-def attend_back(projected,chunk,upstream,o32,lse,bias_vec,bq=512,bk=512,srows=128):
-    length=projected.shape[0]
-    heads=bias_vec.shape[0]
+        diag[pl.ds(index,1),:]=jnp.sum(total,axis=0,keepdims=True)
+    def one_chunk(c):
+        loop(1,seq_devs,lambda i: landed(ups.at[c,rows_of(lax.rem(place-i+seq_devs,seq_devs))],r_up.at[c,i]))
+        own_up(c).wait()
+        @pl.when(c==0)
+        def _():
+            loop(1,experts,lambda i: send_res(i).start())
+            loop(1,devices,lambda i: send_piece(i).start())
+        for head in range(heads):
+            head_back(c,head)
+        loop(1,seq_devs,lambda i: send_grad(c,i).start())
+        own_grad(c).start()
+        if inside:
+            part=jnp.dot(normed_t[...],outs[c],preferred_element_type=f32)
+            block=normed_t.shape[0]//devices
+            weight_parts[c,:,:block,:]=part.reshape(devices,block,384).astype(b16)
+            loop(1,devices,lambda i: send_weight(c,i).start())
+            own_weight(c).start()
+    loop(0,chunks,one_chunk)
+    table[...]=lax.dot_general(bucket_ref[...],diag[...],NT,precision=lax.Precision.HIGHEST,preferred_element_type=f32)
+    loop(1,devices,lambda i: send_table(i).start())
+    own_table.start()
+    def back(i,total):
+        return lax.rem(i[0]-i[1]+total,total)
+    def finish_chunk(c):
+        def grad_landed(i):
+            source=lax.rem(place-i+seq_devs,seq_devs)
+            landed(grad_out.at[source//groups,:,lanes_of(source%groups,c,384)],r_grad.at[c,i])
+            send_grad(c,i).wait_send()
+            send_up(c,i).wait_send()
+        loop(1,seq_devs,grad_landed)
+        own_grad(c).wait()
+        if inside:
+            def weight_landed(i):
+                landed(weight_out.at[c,lax.rem(rank-i+devices,devices)],r_weight.at[c,i])
+                send_weight(c,i).wait_send()
+            loop(1,devices,weight_landed)
+            own_weight(c).wait()
+    loop(0,chunks,finish_chunk)
+    def res_landed(i):
+        landed(ret_out.at[lax.rem(me-i+experts,experts)],r_res.at[i])
+        send_res(i).wait_send()
+    loop(1,experts,res_landed)
+    def piece_landed(i):
+        source=lax.rem(rank-i+devices,devices)
+        landed(piece_out.at[source],r_piece.at[i])
+        send_piece(i).wait_send()
+        landed(table_out.at[source],r_table.at[i])
+        send_table(i).wait_send()
+    loop(1,devices,piece_landed)
+    own_res.wait()
+    own_piece.wait()
+    own_table.wait()
+
+def attend_back(plan,projected,o32,lse,bias_vec,normed_t,buckets,upstream,result,piece,bq=512,bk=512,srows=128):
+    experts,seq_devs,seq_count,stretch,heads,chunks=plan
+    length=stretch*seq_devs
+    groups=seq_devs//seq_count
+    devices=experts*seq_devs
+    block=normed_t.shape[0]//devices
+    inside=block%8==0
+    rows=(block+15)//16*16
     f32,b16=jnp.float32,jnp.bfloat16
-    spec=lambda c: pl.BlockSpec((length,128),lambda i,c=c:(0,c))
-    full=pl.BlockSpec((length,128),lambda i:(0,0))
     vm=lambda kind,*shape: pltpu.VMEM(shape,kind)
+    vmem=pl.BlockSpec(memory_space=pltpu.VMEM)
+    anywhere=pl.BlockSpec(memory_space=pl.ANY)
+    dma=lambda *shape: pltpu.SemaphoreType.DMA(shape)
+    shape=lambda kind,*dims: jax.ShapeDtypeStruct(dims,kind)
+    weight_shape=(chunks,devices,rows,384) if inside else (1,1,16,128)
     return pl.pallas_call(
-        functools.partial(backward_kernel,heads,bq,bk,srows,LOG2E/8),
-        grid=(1,),
-        in_specs=[spec(3*chunk),spec(3*chunk+1),spec(3*chunk+2),full,full,full,pl.BlockSpec(bias_vec.shape,lambda i:(0,0))],
-        out_specs=[pl.BlockSpec((length,384),lambda i:(0,0)),pl.BlockSpec((8,2*length),lambda i:(0,0))],
-        out_shape=[jax.ShapeDtypeStruct((length,384),b16),jax.ShapeDtypeStruct((8,2*length),f32)],
+        functools.partial(backward_kernel,plan,inside,bq,bk,srows,LOG2E/8),
+        in_specs=[vmem]*6+[anywhere]*3,
+        out_specs=[anywhere]*5,
+        out_shape=[shape(b16,seq_count,stretch,groups*chunks*384),shape(b16,*result.shape),shape(b16,*piece.shape),shape(b16,*weight_shape),shape(f32,devices,buckets.shape[0],diag_rows(plan))],
         scratch_shapes=[vm(f32,srows,2*length-srows),vm(f32,srows,2*length),vm(b16,length,256),vm(b16,length,128),vm(b16,128,length),
-            vm(b16,length,256),vm(b16,length,128),vm(b16,length,128),vm(b16,length,128),vm(f32,length,128),vm(f32,length,128)],
-        compiler_params=pltpu.CompilerParams(vmem_limit_bytes=48*MIB),
-        cost_estimate=pl.CostEstimate(flops=40*heads*length*length*64,bytes_accessed=12*MIB,transcendentals=heads*length*length),
+            vm(b16,length,256),vm(b16,length,128),vm(b16,length,128),vm(b16,length,128),vm(f32,length,128),vm(f32,length,128),
+            vm(b16,chunks,length,128),vm(b16,chunks,length,384),vm(b16,*weight_shape),vm(f32,diag_rows(plan),2*length),vm(f32,buckets.shape[0],diag_rows(plan)),
+            dma(chunks,seq_devs),dma(chunks,seq_devs),dma(experts),dma(experts),dma(devices),dma(devices),dma(chunks,seq_devs),dma(chunks,seq_devs),
+            dma(chunks,devices),dma(chunks,devices),dma(devices),dma(devices),dma(3,chunks),dma(4)],
+        compiler_params=pltpu.CompilerParams(collective_id=2,has_side_effects=True,vmem_limit_bytes=58*MIB),
+        cost_estimate=pl.CostEstimate(flops=40*heads*chunks*length*length*64,bytes_accessed=24*MIB,transcendentals=heads*chunks*length*length),
         name="attend_backward",
-    )(projected,projected,projected,upstream,o32,lse,bias_vec)
+    )(projected,o32,lse,bias_vec,normed_t,buckets,upstream,result,piece)
+
+def diag_rows(plan):
+    return 128
 
 def gelu_pair(u):
     c=0.7978845608028654
@@ -408,6 +593,7 @@
     chunks=own_heads//per_chunk
     used=per_chunk*head_dim
     span=chunks*384
+    heads_width=groups*chunks*128
     row_block=width//devices
     place=lax.axis_index("seq")
     group=place%groups
@@ -420,6 +606,7 @@
     small=jnp.pad(jnp.concatenate([router_weight,gains],axis=1),((0,0),(0,126-experts)))
     small_full=lax.all_gather(small,BOTH,axis=0,tiled=True)
     out_full=lax.all_gather(out_weight,BOTH,axis=0,tiled=True)
+    out_full=jnp.pad(out_full.reshape(groups*chunks,used,width),((0,0),(0,128-used),(0,0))).reshape(heads_width,width)
     first_full=lax.all_gather(expert_in,"seq",axis=2,tiled=True)[0]
     second_full=lax.all_gather(expert_out,"seq",axis=1,tiled=True)[0]
     copies=jnp.broadcast_to(tokens[:,None],(seq_count,groups,stretch,width)).reshape(seq_devs,stretch,width)
@@ -441,24 +628,17 @@
     position=jnp.where(slot_pick<capacity,expert_pick*padded_cap+slot_pick,slots)
     hot=(position[None,:]==jnp.arange(slots,dtype=jnp.int32)[:,None]).astype(b16)
     cot_rows=matmul(hot,cotangent.reshape(count,width)).astype(b16).reshape(experts,padded_cap,width)
-    cot_arrived=swap_parts(cot_rows,"exp")
+    plan=(experts,seq_devs,seq_count,stretch,per_chunk,chunks)
     normed=(own_sequence*inverse_rms(own_sequence)*attn_gain_full).astype(b16)
     projected=matmul(normed,weight).astype(b16)
-    saved,attended_parts=[],[]
-    for chunk in range(chunks):
-        bias_rows=slice(chunk*per_chunk,(chunk+1)*per_chunk)
-        out,out32,log_total=attend(projected,chunk,forward_bias[bias_rows])
-        saved.append((out32,log_total))
-        attended_parts.append(swap_parts(out[:,:used].reshape(seq_devs,stretch,used),"seq"))
-    attended=jnp.stack(attended_parts,axis=2).reshape(seq_count,groups,stretch,own_heads*head_dim)
-    attended=jnp.swapaxes(attended,1,2).reshape(count,width)
+    attended,out32,log_total,cot_arrived=attend(plan,projected,forward_bias,cot_rows)
+    attended=attended.reshape(count,heads_width)
     tokens_f=tokens.astype(f32).reshape(count,width)
     hidden=tokens_f+matmul(attended,out_full)
     moe_inverse=inverse_rms(hidden)
     moe_in=(hidden*moe_inverse*moe_gain_full).astype(b16)
     send_rows=matmul(hot,moe_in).astype(b16).reshape(experts,padded_cap,width)
     home,result,first_grad,second_grad,router_part=expert_layer(send_rows,cot_arrived,first_full,second_full,router_wide)
-    returned=swap_parts(result,"exp").reshape(slots,width)
     expert_in_grad=lax.psum_scatter(first_grad[None],"seq",scatter_dimension=2,tiled=True).astype(f32)
     expert_out_grad=lax.psum_scatter(second_grad[None],"seq",scatter_dimension=1,tiled=True).astype(f32)
     grad_out=cotangent.astype(f32).reshape(count,width)
@@ -469,47 +649,32 @@
     hidden_grad=grad_out+weighted*moe_inverse-hidden*(moe_inverse*moe_inverse*moe_inverse)*inner
     branch_grad=hidden_grad.astype(b16)
     heads_grad=matmul(branch_grad,out_full,NT).astype(b16)
-    outgoing=heads_grad.reshape(seq_count,stretch,groups,chunks,used)
-    outgoing=jnp.transpose(outgoing,(3,0,2,1,4))
-    arriving=[swap_parts(outgoing[chunk].reshape(seq_devs,stretch,used),"seq").reshape(length,used) for chunk in range(chunks)]
-    out_part=matmul(attended,branch_grad,TN)
+    out_part=matmul(attended,branch_grad,TN).reshape(groups*chunks,128,width)[:,:used].reshape(width,width)
     extra=jnp.pad(jnp.concatenate([router_part[:,:experts],moe_gain_part[:,None]],axis=1),((0,0),(0,127-experts)))
     out_piece=jnp.concatenate([out_part,extra],axis=1).astype(b16).reshape(devices,row_block,width+128)
-    out_sum=jnp.sum(swap_parts(out_piece,BOTH).astype(f32),axis=0)
+    out_piece=jnp.pad(out_piece,((0,0),(0,-row_block%16),(0,0)))
+    hot_bucket=(backward_ids[None,:]==jnp.arange(buckets,dtype=jnp.int32)[:,None]).astype(f32)
+    hot_bucket=hot_bucket*(jnp.arange(length*2)>0)[None,:]
+    normed_t=jnp.transpose(normed)
+    token_grads,returned,out_pieces,weight_pieces,tables=attend_back(plan,projected,out32,log_total,backward_bias,normed_t,hot_bucket,heads_grad.reshape(seq_count,stretch,heads_width),result,out_piece)
+    out_sum=jnp.sum(out_pieces[:,:row_block].astype(f32),axis=0)
     logits=matmul(moe_in,router_full)
     gates=jax.nn.softmax(logits,axis=-1)
     picked=(expert_pick[:,None]==jnp.arange(experts,dtype=jnp.int32)[None,:]).astype(f32)
     gate=jnp.sum(gates*picked,axis=-1)
-    output=(hidden+gate[:,None]*matmul(hot,returned,TN)).astype(b16).reshape(seq_count,stretch,width)
-    diagonals,token_grads,weight_sums=[],[],[]
-    hot_bucket=(backward_ids[None,:]==jnp.arange(buckets,dtype=jnp.int32)[:,None]).astype(f32)
-    hot_bucket=hot_bucket*(jnp.arange(length*2)>0)[None,:]
-    for chunk in range(chunks):
-        bias_rows=slice(chunk*per_chunk,(chunk+1)*per_chunk)
-        upstream=jnp.pad(arriving[chunk],((0,0),(0,128-used)))
-        grads,diagonal=attend_back(projected,chunk,upstream,*saved[chunk],backward_bias[bias_rows])
-        diagonals.append(diagonal[:per_chunk])
-        token_grads.append(swap_parts(grads.reshape(seq_devs,stretch,384),"seq").reshape(seq_count,groups,stretch,384))
-        piece=matmul(normed,grads,TN).astype(b16).reshape(devices,row_block,384)
-        if chunk==chunks-1:
-            table_part=lax.dot_general(hot_bucket,jnp.concatenate(diagonals,axis=0),NT,precision=lax.Precision.HIGHEST)
-            high=table_part.astype(b16)
-            low=(table_part-lax.reduce_precision(table_part,8,7)).astype(b16)
-            values=jnp.concatenate([high.reshape(-1),low.reshape(-1)])
-            values=jnp.pad(values,(0,row_block*128-values.shape[0])).reshape(1,row_block,128)
-            piece=jnp.concatenate([piece,jnp.broadcast_to(values,(devices,row_block,128))],axis=2)
-        weight_sums.append(swap_parts(piece,BOTH))
-    table_values=weight_sums[-1][:,:,384:].astype(f32).reshape(devices//groups,groups,row_block*128)
-    table_values=jnp.sum(table_values,axis=0)[:,:2*buckets*own_heads].reshape(groups,2,buckets,own_heads)
-    bias_table_grad=jnp.transpose(jnp.sum(table_values,axis=1),(1,0,2)).reshape(buckets,heads)
-    normed_grad=jnp.zeros((count,width),f32)
-    for chunk in range(chunks):
-        for owner in range(groups):
-            start=owner*span+chunk*384
-            normed_grad=normed_grad+matmul(token_grads[chunk][:,owner].reshape(count,384),stacked_full[:,start:start+384],NT)
-    summed=[jnp.sum(part[:,:,:384].astype(f32).reshape(devices//groups,groups,row_block,3,128)[...,:used],axis=0) for part in weight_sums]
-    summed=jnp.stack(summed,axis=1)
-    weight_grads=jnp.transpose(summed,(3,2,0,1,4)).reshape(3,row_block,width)
+    output=(hidden+gate[:,None]*matmul(hot,returned.reshape(slots,width),TN)).astype(b16).reshape(seq_count,stretch,width)
+    tables=jnp.sum(tables.reshape(devices//groups,groups,buckets,-1),axis=0)[:,:,:own_heads]
+    bias_table_grad=jnp.transpose(tables,(1,0,2)).reshape(buckets,heads)
+    token_grads=token_grads.reshape(count,groups*span)
+    normed_grad=matmul(token_grads,stacked_full,NT)
+    if row_block%8:
+        normed_own=(tokens_f*inverse_rms(tokens_f)*attn_gain_full).astype(b16)
+        parts=matmul(normed_own,token_grads,TN).astype(b16).reshape(devices,row_block,groups,chunks,3,128)
+        summed=jnp.sum(swap_parts(parts,BOTH).astype(f32),axis=0)
+    else:
+        parts=weight_pieces[:,:,:row_block].astype(f32).reshape(chunks,devices//groups,groups,row_block,3,128)
+        summed=jnp.transpose(jnp.sum(parts,axis=1),(2,1,0,3,4))
+    weight_grads=jnp.transpose(summed[...,:used],(3,0,1,2,4)).reshape(3,row_block,width)
     own_weights=jnp.stack([query_weight,key_weight,value_weight]).astype(f32)
     attn_gain_grad=jnp.sum(weight_grads*own_weights,axis=(0,2))/attn_gain.astype(f32)
     tokens_inverse=inverse_rms(tokens_f)

time: 711 us -> 580 us (0.82)
  Pallas kernels: 247 us -> 312 us
  waiting for transfers between devices: 103 us -> 51.1 us
  starting transfers between devices: 56.9 us -> 5.06 us
  blocking collectives: 119 us -> 74.1 us
  local copies, waits for them, and re-layouts: 67.2 us -> 31.5 us
  matrix products: 68 us -> 46.6 us
  other arithmetic: 28.1 us -> 35.7 us
    all_to_all x14 -> x1, waiting for transfers between devices: 100 us -> 0.01 us  [swap_parts(): return lax.all_to_all(values, axis, split_axis=0, concat_axis=0, tiled=True)]
    pallas_call x6 -> x2, Pallas kernels: 152 us -> 217 us  [the longest x1 163 us: attend_back(): pl.pallas_call(functools.partial(backward_kernel, plan, inside, bq, bk, s...]
    all_to_all x14 -> x1, starting transfers between devices: 56.7 us -> 4.82 us  [swap_parts(): return lax.all_to_all(values, axis, split_axis=0, concat_axis=0, tiled=True)]
    all_to_all x2 -> x0, blocking collectives: 46.5 us -> none  [swap_parts(): return lax.all_to_all(values, axis, split_axis=0, concat_axis=0, tiled=True)]
    all_gather x1, waiting for transfers between devices: 0.01 us -> 38.9 us  [shards(): second_full = lax.all_gather(expert_out, 'seq', axis=1, tiled=True)[0]]
    dot_general x19 -> x11, matrix products: 66.2 us -> 45.4 us  [matmul(): lax.dot_general(left, right, dims, preferred_element_type=jnp.float32)]
    unnamed x138 -> x92, local copies, waits for them, and re-layouts: 28 us -> 9.22 us
    all_gather x1, waiting for transfers between devices: 0.01 us -> 10.2 us  [shards(): first_full = lax.all_gather(expert_in, 'seq', axis=2, tiled=True)[0]]
  transfers between devices with their start and end apart: 20 -> 7, of which waited for: 8 -> 2; matrix products, arithmetic and copies ran while one was open for 17% -> 17% of each run, Pallas kernels for 22% -> 38%
where the time goes in v2:
time: 580 us; the launch traced here: 571 us
  Pallas kernels  312 us (54%)
  blocking collectives  74.1 us (13%)
  waiting for transfers between devices  51.1 us (9%)
  matrix products  46.6 us (8%)
  other arithmetic  35.7 us (6%)
  local copies, waits for them, and re-layouts  31.5 us (5%)
  between operations  15.1 us (3%)
    pallas_call x1, Pallas kernels, attend_back(): pl.pallas_call(functools.partial(backward_kernel, plan, inside, bq, bk, s...  163 us
    pallas_call x1, Pallas kernels, expert_layer(): pl.pallas_call(functools.partial(expert_kernel, experts, cap, width, hidd...  95.4 us
    all_gather x1, blocking collectives, shards(): small_full = lax.all_gather(small, BOTH, axis=0, tiled=True)  74.1 us
    pallas_call x1, Pallas kernels, attend(): pl.pallas_call(functools.partial(forward_kernel, plan, block, srows, LOG2...  53.5 us
    dot_general x11, matrix products, matmul(): lax.dot_general(left, right, dims, preferred_element_type=jnp.float32)  45.4 us
    all_gather x1, waiting for transfers between devices, shards(): second_full = lax.all_gather(expert_out, 'seq', axis=1, tiled=True)[0]  38.9 us
  transfers between devices with their start and end apart: 7, of which 2 were waited for; matrix products, arithmetic and copies ran while one was open for 17% of the time, Pallas kernels for 38%

profile of v2, /device:TPU:0, one launch (start us, length us, event | category | flops | bytes accessed | tf_op | source)
XLA Modules:
  0.0 571.3 jit_solution(15264222752601422166)
XLA Ops:
  12.9 1.9 broadcast_in_dim.25
  15.0 4.8 all-to-all-start
  20.9 74.1 %all_gather.15 = bf16[768,128]{1,0:T(8,128)(2,1)S(1)} all-gather(bf16[24,128]{1,0:T(8,128)(2,1)S(1)} %fusion.44), channel_id=1, replica_groups=mesh['exp'=8,'seq'=4] {'exp','seq'}, dimensions={0}, use_global_device_ids=true | all-gather | bytes 202752 | tf_op jit(solution)/shard_map/all_gather | solution.py:607
  96.6 3.7 fusion.7
  100.3 2.8 convert_bitcast_fusion
  103.1 3.4 copy.78
  106.5 2.5 fusion
  109.1 9.8 %convolution_convert_fusion.proj_ref = bf16[2048,1152]{1,0:T(8,128)(2,1)} fusion(bf16[768,2304]{1,0:T(8,128)(2,1)} %all-gather.5.cloned.1.call-done, s32[]{:T(128)S(6)} %select_n.26, f32[2048,768]{0,1:T(8,128)} %bitcast.82, f32[768]{0:T(1024)S(1)} %get-tuple-element.91, f32[2048]{0:T(1024)S(1)} %bitcast.97), kind=kOutput, calls=%fused_computation.2 | convolution fusion | flops 3630956544 | bytes 12790788 | tf_op jit(solution)/shard_map/dot_general | solution.py:561
  118.9 53.5 %attend_forward.1 = (bf16[2,512,768]{2,1,0:T(8,128)(2,1)S(1)}, f32[2048,384]{1,0:T(8,128)}, f32[2048,128]{1,0:T(8,128)S(1)}, bf16[8,160,768]{2,1,0:T(8,128)(2,1)S(1)}) custom-call(bf16[2048,1152]{1,0:T(8,128)(2,1)} %convolution_convert_fusion.proj_ref, f32[6,4096]{1,0:T(8,128)S(1)} %fusion.29.bias_ref, bf16[8,160,768]{2,1,0:T(8,128)(2,1)} %bitcast.109), custom_call_target="tpu_custom_call" | custom-call | flops 25769803776 | bytes 16777216 | tf_op jit(solution)/shard_map/attend_forward/pallas_call | solution.py:187
  174.7 2.8 multiply_reduce_fusion.2
  179.1 3.9 fusion.8
  183.0 10.2 %all-gather.9.cloned.1.call-done = bf16[1,768,3072]{2,1,0:T(8,128)(2,1)} async-done(((bf16[1,768,768]{2,1,0:T(8,128)(2,1)}), bf16[1,768,3072]{2,1,0:T(8,128)(2,1)}) %all-gather.9.cloned.1.call-update) | async-done | bytes 4718608 | tf_op jit(solution)/shard_map/all_gather | solution.py:610
  193.2 38.9 %all-gather.11.cloned.1.call-done = bf16[1,3072,768]{2,1,0:T(8,128)(2,1)} async-done(((bf16[1,768,768]{2,1,0:T(8,128)(2,1)}), bf16[1,3072,768]{2,1,0:T(8,128)(2,1)}) %all-gather.11.cloned.1.call-update) | async-done | bytes 4718608 | tf_op jit(solution)/shard_map/all_gather | solution.py:611
  232.1 95.4 %expert_layer.1 = (bf16[8,160,768]{2,1,0:T(8,128)(2,1)}, bf16[8,160,768]{2,1,0:T(8,128)(2,1)}, bf16[768,3072]{1,0:T(8,128)(2,1)}, bf16[3072,768]{1,0:T(8,128)(2,1)}, f32[768,128]{1,0:T(8,128)}) custom-call(bf16[8,160,768]{2,1,0:T(8,128)(2,1)} %bitcast.110, bf16[8,160,768]{2,1,0:T(8,128)(2,1)} %copy-done, bf16[768,3072]{1,0:T(8,128)(2,1)} %bitcast.104, ...), custom_call_target="tpu_custom_call" | custom-call | flops 36238786560 | bytes 41943040 | tf_op jit(solution)/shard_map/expert_layer/pallas_call | solution.py:544
  334.8 5.8 %fusion.54.normed_t = bf16[768,2048]{1,0:T(8,128)(2,1)} fusion(f32[768]{0:T(1024)S(1)} %get-tuple-element.91, f32[2048,768]{0,1:T(8,128)} %bitcast.83, f32[2048]{0:T(1024)S(1)} %bitcast.98), kind=kLoop, calls=%fused_computation.99 | loop fusion | flops 4718592 | bytes 9448448 | tf_op jit(solution)/shard_map/transpose | solution.py:658
  340.7 1.6 copy.66
  342.3 2.7 fusion.56
  345.6 6.3 %multiply_reduce_fusion = (bf16[768]{0:T(1024)(128)(2,1)S(1)}, f32[1024]{0:T(1024)S(1)}, f32[1024,768]{1,0:T(8,128)}) fusion(f32[1024,768]{1,0:T(8,128)S(1)} %copy-done.5, f32[1024]{0:T(1024)S(1)} %get-tuple-element.96, f32[768]{0:T(1024)S(1)} %get-tuple-element.90, bf16[1280,768]{1,0:T(8,128)(2,1)} %bitcast.108, s32[1024]{0:T(1024)S(1)} %copy-done.32), kind=kOutput, calls=%fused_computation.24 | convolution fusion | flops 2019293440 | bytes 8274432 | tf_op jit(solution)/shard_map/dot_general | solution.py:561
  352.3 2.9 multiply_subtract_fusion
  355.3 1.4 fusion.21
  358.4 1.9 copy-done.8
  360.2 3.8 convolution_convert_fusion.1
  364.1 163.2 %attend_backward.1 = (bf16[2,512,2304]{2,1,0:T(8,128)(2,1)}, bf16[8,160,768]{2,1,0:T(8,128)(2,1)}, bf16[32,32,896]{2,1,0:T(8,128)(2,1)}, bf16[3,32,32,384]{3,2,1,0:T(8,128)(2,1)}, f32[32,32,128]{2,1,0:T(8,128)}) custom-call(bf16[2048,1152]{1,0:T(8,128)(2,1)} %convolution_convert_fusion.proj_ref, f32[2048,384]{1,0:T(8,128)} %get-tuple-element.27.o32_ref, ...), custom_call_target="tpu_custom_call" | custom-call | flops 64424509440 | bytes 25165824 | tf_op jit(solution)/shard_map/attend_backward/pallas_call | solution.py:393
  527.3 1.5 convert_reduce_fusion
  529.5 1.7 slice_convert_fusion
  531.3 3.7 reshape.258
  535.0 3.6 reduce_sum.116
  544.0 7.1 %fusion.12 = (f32[1024]{0:T(1024)S(1)}, f32[1024,768]{1,0:T(8,128)S(1)}) fusion(bf16[2,512,768]{2,1,0:T(8,128)(2,1)S(1)} %copy-done.3, f32[768]{0:T(1024)S(1)} %get-tuple-element.91, bf16[1024,2304]{1,0:T(8,128)(2,1)} %bitcast.106, bf16[768,2304]{1,0:T(8,128)(2,1)} %all-gather.5.cloned.1.call-done), kind=kOutput, calls=%fused_computation.22 | convolution fusion | flops 3627023360 | bytes 12983296 | tf_op jit(solution)/shard_map/dot_general | solution.py:561
  551.2 2.2 fusion.11
  554.8 3.6 add_convert_fusion
  558.4 2.8 convert_element_type.141
  561.2 2.8 convert_element_type.142
  (166 shorter events, 29.6 us)
Async XLA Ops:
  7.2 101.9 %all-gather.5.cloned.1.call-start = ((), (), s32[]{:S(2)}) async-start(), calls=%async_computation.3 | async-start | bytes 3649536 | tf_op jit(solution)/shard_map/all_gather | solution.py:604
  10.7 163.9 %all-gather.7.cloned.1.call-start = ((), (), s32[]{:S(2)}) async-start(), calls=%async_computation.4 | async-start | bytes 1216512 | tf_op jit(solution)/shard_map/all_gather | solution.py:608
  11.5 181.7 %all-gather.9.cloned.1.call-start = ((), (), s32[]{:S(2)}) async-start(), calls=%async_computation.5 | async-start | bytes 5898240 | tf_op jit(solution)/shard_map/all_gather | solution.py:610
  14.9 5.6 copy-start.39
  14.9 5.7 %copy-start.37 = (bf16[24,8]{0,1:T(8,128)(2,1)S(1)}, bf16[24,8]{0,1:T(8,128)(2,1)}, u32[]{:S(2)}) copy-start(bf16[24,8]{0,1:T(8,128)(2,1)} %param.22) | copy-start | bytes 1156
  14.9 5.9 %copy-start.20 = (s32[4095]{0:T(1024)S(1)}, s32[4095]{0:T(1024)}, u32[]{:S(2)}) copy-start(s32[4095]{0:T(1024)} %param.30) | copy-start | bytes 49144
  14.9 5.9 %copy-start.35 = (s32[2,512]{1,0:T(2,128)S(1)}, s32[2,512]{1,0:T(2,128)}, u32[]{:S(2)}) copy-start(s32[2,512]{1,0:T(2,128)} %param.29) | copy-start | bytes 12292
  14.9 5.9 %copy-start.36 = (s32[2,512]{1,0:T(2,128)S(1)}, s32[2,512]{1,0:T(2,128)}, u32[]{:S(2)}) copy-start(s32[2,512]{1,0:T(2,128)} %param.28) | copy-start | bytes 12292
  14.9 80.1 %copy-start.25 = (bf16[128,128]{1,0:T(8,128)(2,1)S(1)}, bf16[128,128]{1,0:T(8,128)(2,1)}, u32[]{:S(2)}) copy-start(bf16[128,128]{1,0:T(8,128)(2,1)} %constant.66.clone) | copy-start | bytes 98308
  14.9 80.1 %copy-start.30 = (bf16[32,32]{1,0:T(8,128)(2,1)S(1)}, bf16[32,32]{1,0:T(8,128)(2,1)}, u32[]{:S(2)}) copy-start(bf16[32,32]{1,0:T(8,128)(2,1)} %constant.67.clone) | copy-start | bytes 6148
  14.9 80.7 %copy-start.28 = (f32[32,12]{0,1:T(8,128)S(1)}, f32[32,12]{0,1:T(8,128)}, u32[]{:S(2)}) copy-start(f32[32,12]{0,1:T(8,128)} %param.25) | copy-start | bytes 4612
  14.9 81.7 %copy-start.11 = (bf16[2,512,768]{2,1,0:T(8,128)(2,1)S(1)}, bf16[2,512,768]{2,1,0:T(8,128)(2,1)}, u32[]{:S(2)}) copy-start(bf16[2,512,768]{2,1,0:T(8,128)(2,1)} %param.31) | copy-start | bytes 4718596
  15.0 85.4 %all-to-all-start = ((bf16[4,512,768]{1,2,0:T(8,128)(2,1)}), bf16[4,512,768]{1,2,0:T(8,128)(2,1)}, u32[]{:S(2)}, u32[]{:S(2)}) async-start(bf16[4,512,768]{1,2,0:T(8,128)(2,1)} %bitcast.84), calls=%async_computation | async-start | bytes 6291456 | tf_op jit(solution)/shard_map/all_to_all | solution.py:564
  19.8 212.3 %all-gather.11.cloned.1.call-start = ((), (), s32[]{:S(2)}) async-start(), calls=%async_computation.6 | async-start | bytes 5898240 | tf_op jit(solution)/shard_map/all_gather | solution.py:611
  20.4 538.0 %reduce-scatter.3.cloned.1.call-start = ((), (), s32[]{:S(2)}) async-start(), calls=%async_computation.7 | async-start | bytes 5898240 | tf_op jit(solution)/shard_map/reduce_scatter | solution.py:642
  20.9 79.5 %copy-start.21 = (s32[1,4,2,128]{3,1,2,0:T(4,128)}, s32[1,4,2,128]{3,1,2,0:T(4,128)S(1)}, u32[]{:S(2)}) copy-start(s32[1,4,2,128]{3,1,2,0:T(4,128)S(1)} %copy.81) | copy-start | bytes 12292
  95.6 82.5 %copy-start.31 = (s32[1024]{0:T(1024)}, s32[1024]{0:T(1024)S(1)}, u32[]{:S(2)}) copy-start(s32[1024]{0:T(1024)S(1)} %add_select_fusion) | copy-start | bytes 12292
  109.0 9.9 %copy-start.23 = (f32[1,4,4,128]{3,1,2,0:T(4,128)}, f32[1,4,4,128]{3,1,2,0:T(4,128)S(1)}, u32[]{:S(2)}) copy-start(f32[1,4,4,128]{3,1,2,0:T(4,128)S(1)} %copy.79) | copy-start | bytes 24580
  327.5 7.3 %copy-start.24 = (f32[1,4,4,128]{3,1,2,0:T(4,128)S(1)}, f32[1,4,4,128]{3,1,2,0:T(4,128)}, u32[]{:S(2)}) copy-start(f32[1,4,4,128]{3,1,2,0:T(4,128)} %copy-done.23) | copy-start | bytes 24580
  327.6 233.7 %reduce-scatter.5.cloned.1.call-start = ((), (), s32[]{:S(2)}) async-start(), calls=%async_computation.8 | async-start | bytes 5898240 | tf_op jit(solution)/shard_map/reduce_scatter | solution.py:643
  345.6 6.3 %copy-start.19 = (f32[768,128]{1,0:T(8,128)S(1)}, f32[768,128]{1,0:T(8,128)}, u32[]{:S(2)}) copy-start(f32[768,128]{1,0:T(8,128)} %get-tuple-element.32) | copy-start | bytes 1179652
  345.6 6.7 %copy-start.26 = (f32[1024]{0:T(1024)S(1)}, f32[1024]{0:T(1024)}, u32[]{:S(2)}) copy-start(f32[1024]{0:T(1024)} %get-tuple-element.95) | copy-start | bytes 12292
  534.9 6.0 %slice-start = ((f32[24,896]{1,0:T(8,128)}), f32[24,8]{1,0:T(8,128)S(1)}, s32[]{:S(2)}) async-start(f32[24,896]{1,0:T(8,128)} %copy-done.13), calls=%async_computation.9 | async-start | bytes 24576 | tf_op jit(solution)/shard_map/slice | solution.py:689
  534.9 6.7 %copy-start.12 = (f32[32,32,128]{2,1,0:T(8,128)S(1)}, f32[32,32,128]{2,1,0:T(8,128)}, u32[]{:S(2)}) copy-start(f32[32,32,128]{2,1,0:T(8,128)} %get-tuple-element.37) | copy-start | bytes 1572868
  534.9 7.4 %copy-start.14 = (f32[24,896]{1,0:T(8,128)S(1)}, f32[24,896]{1,0:T(8,128)}, u32[]{:S(2)}) copy-start(f32[24,896]{1,0:T(8,128)} %copy-done.13) | copy-start | bytes 258052
  534.9 8.1 %copy-start.15 = (bf16[1,24,2,3,128]{4,0,1,2,3:T(2,128)(2,1)S(1)}, bf16[1,24,2,3,128]{4,0,1,2,3:T(2,128)(2,1)}, u32[]{:S(2)}) copy-start(bf16[1,24,2,3,128]{4,0,1,2,3:T(2,128)(2,1)} %copy.74) | copy-start | bytes 110596
  534.9 8.1 %copy-start.16 = (bf16[1,24,2,3,128]{4,0,1,2,3:T(2,128)(2,1)S(1)}, bf16[1,24,2,3,128]{4,0,1,2,3:T(2,128)(2,1)}, u32[]{:S(2)}) copy-start(bf16[1,24,2,3,128]{4,0,1,2,3:T(2,128)(2,1)} %copy.73) | copy-start | bytes 110596
  535.0 8.1 %copy-start.17 = (bf16[1,24,2,3,128]{4,0,1,2,3:T(2,128)(2,1)S(1)}, bf16[1,24,2,3,128]{4,0,1,2,3:T(2,128)(2,1)}, u32[]{:S(2)}) copy-start(bf16[1,24,2,3,128]{4,0,1,2,3:T(2,128)(2,1)} %copy.72) | copy-start | bytes 110596
  535.0 8.5 %copy-start.40 = (bf16[24]{0:T(256)(128)(2,1)S(1)}, bf16[24]{0:T(256)(128)(2,1)}, u32[]{:S(2)}) copy-start(bf16[24]{0:T(256)(128)(2,1)} %param.23) | copy-start | bytes 148
  535.0 9.0 %copy-start.3 = (bf16[2,512,768]{2,1,0:T(8,128)(2,1)S(1)}, bf16[2,512,768]{2,1,0:T(8,128)(2,1)}, u32[]{:S(2)}) copy-start(bf16[2,512,768]{2,1,0:T(8,128)(2,1)} %param.17) | copy-start | bytes 4718596
  544.0 7.1 %copy-start.9 = (f32[1024,768]{1,0:T(8,128)S(1)}, f32[1024,768]{1,0:T(8,128)}, u32[]{:S(2)}) copy-start(f32[1024,768]{1,0:T(8,128)} %copy-done.7) | copy-start | bytes 9437188
  544.0 7.1 %copy-start.27 = (f32[1024]{0:T(1024)S(1)}, f32[1024]{0:T(1024)}, u32[]{:S(2)}) copy-start(f32[1024]{0:T(1024)} %multiply_multiply_fusion) | copy-start | bytes 12292
  (18 other events, 52.6 us)
Sparse Core Ops, SparseCore 0:
  11.5 64.6 all-gather.4
  79.1 72.2 all-gather.6
  153.0 40.1 all-gather.8
  194.6 37.4 all-gather.10
  327.7 46.8 reduce-scatter.2
  377.1 89.4 reduce-scatter.4

commit v3 on v2

--- a/solution.py
+++ b/solution.py
@@ -61,7 +61,166 @@
         return carry
     lax.fori_loop(first,last,step,0)
 
-def forward_kernel(plan,block,srows,scale,proj_ref,bias_ref,cot_ref,att_out,o32_ref,lse_ref,cot_out,strip,kd,va,scr,outs,s_cot,r_cot,s_att,r_att,local_sem):
+class Spread:
+    def __init__(self,axes,seq_count,groups,source,slot,direct,passed,received,own):
+        self.me,self.place=axes
+        self.counts=(seq_count,groups)
+        self.source,self.slot=source,slot
+        self.direct,self.passed,self.received,self.own=direct,passed,received,own
+        self.sequence,self.group=self.place//groups,self.place%groups
+    def at(self,sequence_step,group_step):
+        seq_count,groups=self.counts
+        return lax.rem(self.sequence+sequence_step,seq_count)*groups+lax.rem(self.group+group_step,groups)
+    def copies(self):
+        seq_count,groups=self.counts
+        targets=[self.at(i,0) for i in range(1,seq_count)]+[self.at(0,i) for i in range(1,groups)]
+        return [remote(self.source(target//groups),self.slot(self.place),self.direct.at[i],self.received.at[self.place],(self.me,target)) for i,target in enumerate(targets)]
+    def local(self):
+        return pltpu.make_async_copy(self.source(self.sequence),self.slot(self.place),self.own)
+    def landed(self,place):
+        landing=self.slot(place)
+        remote(landing,landing,self.own,self.received.at[place],(self.me,self.place)).wait_recv()
+    def relays(self):
+        seq_count,groups=self.counts
+        out=[]
+        for i in range(1,seq_count):
+            part=self.at(i,0)
+            for j in range(1,groups):
+                index=(i-1)*(groups-1)+j-1
+                out.append(remote(self.slot(part),self.slot(part),self.passed.at[index],self.received.at[part],(self.me,self.at(0,j))))
+        return out
+    def start(self):
+        self.local().start()
+        for copy in self.copies():
+            copy.start()
+    def relay(self):
+        seq_count,groups=self.counts
+        for i in range(1,seq_count):
+            self.landed(self.at(i,0))
+        for copy in self.relays():
+            copy.start()
+    def finish(self):
+        seq_count,groups=self.counts
+        for j in range(1,groups):
+            for i in range(seq_count):
+                self.landed(self.at(i,j))
+        for copy in self.copies()+self.relays():
+            copy.wait_send()
+        self.local().wait()
+
+def spread_semaphores(seq_count,groups):
+    dma=lambda n: pltpu.SemaphoreType.DMA((n,))
+    return [dma(seq_count+groups-2),dma(max((seq_count-1)*(groups-1),1)),dma(seq_count*groups),pltpu.SemaphoreType.DMA]
+
+def start_kernel(plan,rows,span,token_ref,unit_ref,w1_ref,proj_ref,normed_ref,own_out,w1_out,
+                 tok,scaled,units,land,s_unit,r_unit,s_block,r_block,s_pass,own_sem,*spread_sems):
+    experts,seq_devs,seq_count,stretch,heads,chunks=plan
+    groups=seq_devs//seq_count
+    length=stretch*seq_devs
+    f32,b16=jnp.float32,jnp.bfloat16
+    me,place=lax.axis_index("exp"),lax.axis_index("seq")
+    pairs=experts//2
+    pair,side=me//2,me%2
+    other=1-side
+    block=seq_devs*rows
+    quarter=w1_ref.shape[2]
+    def device(offset,member):
+        return lax.rem(pair+offset+pairs,pairs)*2+member
+    barrier=pltpu.get_barrier_semaphore()
+    for i in range(1,experts):
+        pl.semaphore_signal(barrier,inc=1,device_id=(lax.rem(me+i,experts),place),device_id_type=MESH)
+    for i in range(1,seq_devs):
+        pl.semaphore_signal(barrier,inc=1,device_id=(me,lax.rem(place+i,seq_devs)),device_id_type=MESH)
+    def stretch_of(owner):
+        return tok.at[pl.ds(pl.multiple_of(owner*stretch,128),stretch)]
+    def part_of(owner):
+        return w1_out.at[:,pl.ds(pl.multiple_of(owner*quarter,128),quarter)]
+    tokens=Spread((me,place),seq_count,groups,lambda n: token_ref.at[n],stretch_of,*spread_sems[:4])
+    firsts=Spread((me,place),seq_count,groups,lambda n: w1_ref.at[0],part_of,*spread_sems[4:])
+    own_unit=pltpu.make_async_copy(unit_ref.at[place%groups],units.at[place],own_sem.at[0])
+    own_unit.start()
+    pl.semaphore_wait(barrier,experts+seq_devs-2)
+    def send_unit(i):
+        target=lax.rem(place+i,seq_devs)
+        return remote(unit_ref.at[target%groups],units.at[place],s_unit.at[i],r_unit.at[place],(me,target))
+    for i in range(1,seq_devs):
+        send_unit(i).start()
+    tokens.start()
+    firsts.start()
+    def landed(landing,received):
+        remote(landing,landing,own_sem.at[1],received,(me,place)).wait_recv()
+    own_unit.wait()
+    for i in range(1,seq_devs):
+        source=lax.rem(place+i,seq_devs)
+        landed(units.at[source],r_unit.at[source])
+    def block_of(owner):
+        return land.at[pl.ds(pl.multiple_of(owner*block,16),block)]
+    joined=jnp.concatenate([units[i].astype(f32)[:rows] for i in range(seq_devs)],axis=0)
+    land[pl.ds(pl.multiple_of(me*block,16),block),:]=joined.astype(b16)
+    visit=[j for step in range(1,pairs//2+1) for j in sorted({step,pairs-step})]
+    def send_block(j,member,index):
+        return remote(block_of(me),block_of(me),s_block.at[index],r_block.at[me],(device(j,member),place))
+    sends=[send_block(0,other,0)]+[send_block(j,side,j) for j in visit]
+    for copy in sends:
+        copy.start()
+    passes=[remote(block_of(device(j,side)),block_of(device(j,side)),s_pass.at[j],r_block.at[device(j,side)],(device(0,other),place)) for j in visit]
+    for j,copy in zip(visit,passes):
+        landed(block_of(device(j,side)),r_block.at[device(j,side)])
+        copy.start()
+    piece=512 if length%512==0 else 128
+    tokens.relay()
+    tokens.finish()
+    def scale_rows(step):
+        part=pl.ds(pl.multiple_of(step*piece,piece),piece)
+        x=tok[part,:].astype(f32)
+        scaled[part,:]=x*lax.rsqrt(jnp.mean(x*x,axis=-1,keepdims=True)+EPSILON)
+    loop(0,length//piece,scale_rows)
+    for j in [0]+visit:
+        landed(block_of(device(j,other)),r_block.at[device(j,other)])
+    own_copy=pltpu.make_async_copy(land,own_out,own_sem.at[2])
+    own_copy.start()
+    gain=jnp.transpose(land[:,span:].astype(f32))[experts:experts+1,:]
+    def project(step):
+        part=pl.ds(pl.multiple_of(step*piece,piece),piece)
+        normed=(scaled[part,:]*gain).astype(b16)
+        normed_ref[part,:]=normed
+        proj_ref[part,:]=jnp.dot(normed,land[:,:span],preferred_element_type=f32).astype(b16)
+    loop(0,length//piece,project)
+    firsts.relay()
+    own_copy.wait()
+    firsts.finish()
+    for copy in sends+passes:
+        copy.wait_send()
+    for i in range(1,seq_devs):
+        send_unit(i).wait_send()
+
+def gather_start(plan,rows,tokens,units,expert_in):
+    experts,seq_devs,seq_count,stretch,heads,chunks=plan
+    groups=seq_devs//seq_count
+    length=stretch*seq_devs
+    width=tokens.shape[2]
+    span=chunk_span(heads)*chunks
+    b16=jnp.bfloat16
+    vmem=pl.BlockSpec(memory_space=pltpu.VMEM)
+    anywhere=pl.BlockSpec(memory_space=pl.ANY)
+    dma=lambda n: pltpu.SemaphoreType.DMA((n,))
+    shape=lambda *dims: jax.ShapeDtypeStruct(dims,b16)
+    return pl.pallas_call(
+        functools.partial(start_kernel,plan,rows,span),
+        in_specs=[anywhere,anywhere,vmem],
+        out_specs=[vmem,vmem,anywhere,anywhere],
+        out_shape=[shape(length,span),shape(length,width),shape(width,span+128),shape(width,expert_in.shape[2]*seq_devs)],
+        scratch_shapes=[pltpu.VMEM((length,width),b16),pltpu.VMEM((length,width),jnp.float32),pltpu.VMEM((seq_devs,)+units.shape[1:],b16),pltpu.VMEM((width,span+128),b16),
+            dma(seq_devs),dma(seq_devs),dma(experts),dma(experts),dma(experts),dma(3)]+spread_semaphores(seq_count,groups)*2,
+        compiler_params=pltpu.CompilerParams(collective_id=3,has_side_effects=True,vmem_limit_bytes=40*MIB),
+        cost_estimate=pl.CostEstimate(flops=2*length*width*span,bytes_accessed=24*MIB,transcendentals=0),
+        name="gather_start",
+    )(tokens,units,expert_in)
+
+def chunk_span(heads):
+    return 128*(1+heads)
+
+def forward_kernel(plan,block,srows,scale,proj_ref,bias_ref,cot_ref,own_ref,w2_ref,att_out,o32_ref,lse_ref,cot_out,all_out,w2_out,strip,kd,va,scr,outs,s_cot,r_cot,s_att,r_att,s_all,r_all,local_sem,*spread_sems):
     experts,seq_devs,seq_count,stretch,heads,chunks=plan
     length=stretch*seq_devs
     groups=seq_devs//seq_count
@@ -73,7 +232,15 @@
     loop(1,seq_devs,lambda i: pl.semaphore_signal(barrier,inc=1,device_id=(me,lax.rem(place+i,seq_devs)),device_id_type=MESH))
     own_cot=pltpu.make_async_copy(cot_ref.at[me],cot_out.at[me],local_sem.at[0])
     own_cot.start()
+    own_all=pltpu.make_async_copy(own_ref,all_out.at[group],local_sem.at[1+chunks])
+    own_all.start()
+    deep=w2_ref.shape[1]
+    seconds=Spread((me,place),seq_count,groups,lambda n: w2_ref.at[0],lambda owner: w2_out.at[pl.ds(pl.multiple_of(owner*deep,128),deep)],*spread_sems)
     pl.semaphore_wait(barrier,experts+seq_devs-2)
+    seconds.start()
+    def send_all(i):
+        return remote(own_ref,all_out.at[group],s_all.at[i],r_all.at[i],(me,sequence*groups+lax.rem(group+i,groups)))
+    loop(1,groups,lambda i: send_all(i).start())
     def send_cot(i):
         target=lax.rem(me+i,experts)
         return remote(cot_ref.at[target],cot_out.at[me],s_cot.at[i],r_cot.at[i],(target,place))
@@ -96,20 +263,19 @@
     lse_ref[...]=jnp.zeros_like(lse_ref)
     def attend_head(c,head):
         index=c*heads+head
-        base=c*384
         def columns(which):
-            return pl.ds(pl.multiple_of(base+which*128,128),128)
-        own=pl.ds(pl.multiple_of(c*128,128),128)
-        fill_strip(strip,bias_ref[pl.ds(index,1),:],srows,width)
-        kd[...]=dup_head(proj_ref[:,columns(1)],head).astype(b16)
-        va[...]=jnp.where(lanes<64,dup_head(proj_ref[:,columns(2)],head),jnp.where(lanes==64,1.0,0.0)).astype(b16)
+            return slice(c*chunk_span(heads)+which*128,c*chunk_span(heads)+(which+1)*128)
+        own=slice(c*128,(c+1)*128)
+        fill_strip(strip,bias_ref[index:index+1,:],srows,width)
+        kd[...]=dup_head(proj_ref[:,columns(1+head)],0).astype(b16)
+        va[...]=jnp.where(lanes<64,dup_head(proj_ref[:,columns(1+head)],1),jnp.where(lanes==64,1.0,0.0)).astype(b16)
         def rows_of(step):
-            return pl.ds(pl.multiple_of(step*block,block),block)
+            return slice(step*block,(step+1)*block)
         def score_piece(step,qa,p,slot,top):
             raw=lax.dot_general(qa,kd[p*wide:(p+1)*wide,:],NT,preferred_element_type=f32)
             parts=[]
             for part in range(block//srows):
-                start=pl.multiple_of(length-srows-step*block-part*srows+p*wide,128)
+                start=length-srows-step*block-part*srows+p*wide
                 parts.append(raw[part*srows:(part+1)*srows]+strip[:,pl.ds(start,wide)])
             scores=jnp.concatenate(parts,axis=0)
             scr[slot,:,p*wide:(p+1)*wide]=scores
@@ -124,10 +290,20 @@
             total=mixed[:,64:65]
             result=mixed/total
             lse_ref[rows,:]=jnp.where(block_lanes==index,top+jnp.log2(total),lse_ref[rows,:])
-            if head==0:
-                o32_ref[rows,own]=result
-            else:
-                o32_ref[rows,own]=jnp.where(block_lanes<64,o32_ref[rows,own],pltpu.roll(result,64,1))
+            if head:
+                result=jnp.where(block_lanes<64,o32_ref[rows,own],pltpu.roll(result,64,1))
+            o32_ref[rows,own]=result
+            if head==heads-1:
+                outs[c,rows]=result.astype(b16)
+        def send_steps(first,last):
+            for part in range(first*block//stretch,last*block//stretch):
+                distance=lax.rem(part-place+seq_devs,seq_devs)
+                @pl.when(distance==0)
+                def _():
+                    own_att(c).start()
+                @pl.when(distance!=0)
+                def _():
+                    send_att(c,distance).start()
         def advance(step,slot,top):
             mixing=top is not None
             qa=split_query(proj_ref[rows_of(step),columns(0)],head,scale)
@@ -140,26 +316,21 @@
             if mixing:
                 finish(step-1,top,mixed)
             return jnp.max(new,axis=1,keepdims=True)
-        def body(i,top):
-            top=advance(2*i+1,1,top)
-            return advance(2*i+2,0,top)
-        top=advance(0,0,None)
-        top=lax.fori_loop(0,(blocks-1)//2,body,top)
-        last=0
-        if blocks%2==0:
-            top=advance(blocks-1,1,top)
-            last=1
+        top=None
+        for step in range(blocks):
+            top=advance(step,step%2,top)
+        if head==heads-1:
+            send_steps(0,blocks-1)
         mixed=jnp.zeros((block,128),f32)
         for p in range(pieces):
-            mixed=mix_piece(last,p,top,mixed)
+            mixed=mix_piece((blocks-1)%2,p,top,mixed)
         finish(blocks-1,top,mixed)
-    def one_chunk(c):
+        if head==heads-1:
+            send_steps(blocks-1,blocks)
+    for c in range(chunks):
         for head in range(heads):
             attend_head(c,head)
-        outs[c]=o32_ref[:,pl.ds(pl.multiple_of(c*128,128),128)].astype(b16)
-        loop(1,seq_devs,lambda i: send_att(c,i).start())
-        own_att(c).start()
-    loop(0,chunks,one_chunk)
+    seconds.relay()
     def land_att(c,i):
         source=lax.rem(place-i+seq_devs,seq_devs)
         landing=att_out.at[source//groups,:,lanes_of(source%groups,c,128)]
@@ -174,9 +345,16 @@
         remote(landing,landing,s_cot.at[i],r_cot.at[i],(me,place)).wait_recv()
     loop(1,experts,land_cot)
     loop(1,experts,lambda i: send_cot(i).wait_send())
+    def land_all(i):
+        landing=all_out.at[lax.rem(group-i+groups,groups)]
+        remote(landing,landing,s_all.at[i],r_all.at[i],(me,place)).wait_recv()
+        send_all(i).wait_send()
+    loop(1,groups,land_all)
+    own_all.wait()
     own_cot.wait()
-
-def attend(plan,projected,bias_vec,cot_rows,block=512,srows=128):
+    seconds.finish()
+
+def attend(plan,projected,bias_vec,cot_rows,own_weight,expert_out,block=512,srows=128):
     experts,seq_devs,seq_count,stretch,heads,chunks=plan
     length=stretch*seq_devs
     groups=seq_devs//seq_count
@@ -186,19 +364,19 @@
     dma=lambda *shape: pltpu.SemaphoreType.DMA(shape)
     return pl.pallas_call(
         functools.partial(forward_kernel,plan,block,srows,LOG2E/8),
-        in_specs=[vmem,vmem,anywhere],
-        out_specs=[anywhere,vmem,vmem,anywhere],
-        out_shape=[jax.ShapeDtypeStruct((seq_count,stretch,groups*chunks*128),b16),jax.ShapeDtypeStruct((length,chunks*128),f32),jax.ShapeDtypeStruct((length,128),f32),jax.ShapeDtypeStruct(cot_rows.shape,b16)],
+        in_specs=[vmem,vmem,anywhere,vmem,vmem],
+        out_specs=[anywhere,vmem,vmem]+[anywhere]*3,
+        out_shape=[jax.ShapeDtypeStruct((seq_count,stretch,groups*chunks*128),b16),jax.ShapeDtypeStruct((length,chunks*128),f32),jax.ShapeDtypeStruct((length,128),f32),jax.ShapeDtypeStruct(cot_rows.shape,b16),jax.ShapeDtypeStruct((groups,)+own_weight.shape,b16),jax.ShapeDtypeStruct((expert_out.shape[1]*seq_devs,expert_out.shape[2]),b16)],
         scratch_shapes=[pltpu.VMEM((srows,2*length-srows),f32),pltpu.VMEM((length,128),b16),pltpu.VMEM((length,128),b16),pltpu.VMEM((2,block,length),f32),pltpu.VMEM((chunks,length,128),b16),
-            dma(experts),dma(experts),dma(chunks,seq_devs),dma(chunks,seq_devs),dma(1+chunks)],
+            dma(experts),dma(experts),dma(chunks,seq_devs),dma(chunks,seq_devs),dma(groups),dma(groups),dma(2+chunks)]+spread_semaphores(seq_count,groups),
         compiler_params=pltpu.CompilerParams(collective_id=1,has_side_effects=True,vmem_limit_bytes=48*MIB),
         cost_estimate=pl.CostEstimate(flops=16*heads*chunks*length*length*64,bytes_accessed=16*MIB,transcendentals=heads*chunks*length*length),
         name="attend_forward",
-    )(projected,bias_vec,cot_rows)
-
-def backward_kernel(plan,inside,bq,bk,srows,scale,proj_ref,o32_ref,lse_ref,bias_ref,normed_t,bucket_ref,up_ref,res_ref,piece_ref,
+    )(projected,bias_vec,cot_rows,own_weight,expert_out)
+
+def backward_kernel(plan,inside,bq,bk,srows,scale,proj_ref,o32_ref,lse_ref,bias_ref,normed_ref,bucket_ref,up_ref,res_ref,piece_ref,
                     grad_out,ret_out,piece_out,weight_out,table_out,
-                    strip,grads,ka,va,kt,qa,da,dd,qd,dk_acc,dv_acc,ups,outs,weight_parts,diag,table,
+                    strip,grads,ka,va,kt,qa,da,dd,qd,dk_acc,dv_acc,ups,outs,weight_parts,diag,table,normed_t,
                     s_up,r_up,s_res,r_res,s_piece,r_piece,s_grad,r_grad,s_weight,r_weight,s_table,r_table,local_sem,own_sem):
     experts,seq_devs,seq_count,stretch,heads,chunks=plan
     length=stretch*seq_devs
@@ -228,16 +406,18 @@
     def send_piece(i):
         target,where=other(i)
         return remote(piece_ref.at[target],piece_out.at[rank],s_piece.at[i],r_piece.at[i],where)
-    def send_grad(c,i):
+    def grad_lanes(owner_group,c,part):
+        return pl.ds(pl.multiple_of((owner_group*chunks+c)*chunk_span(heads)+part*128,128),128)
+    def send_grad(c,part,i):
         target=lax.rem(place+i,seq_devs)
-        return remote(outs.at[c,rows_of(target)],grad_out.at[sequence,:,lanes_of(group,c,384)],s_grad.at[c,i],r_grad.at[c,i],(me,target))
-    def own_grad(c):
-        return pltpu.make_async_copy(outs.at[c,rows_of(place)],grad_out.at[sequence,:,lanes_of(group,c,384)],local_sem.at[1,c])
+        return remote(outs.at[c,rows_of(target),part*128:(part+1)*128],grad_out.at[sequence,:,grad_lanes(group,c,part)],s_grad.at[c,part,i],r_grad.at[c,part,i],(me,target))
+    def own_grad(c,part):
+        return pltpu.make_async_copy(outs.at[c,rows_of(place),part*128:(part+1)*128],grad_out.at[sequence,:,grad_lanes(group,c,part)],local_sem.at[2+part,c])
     def send_weight(c,i):
         target,where=other(i)
         return remote(weight_parts.at[c,target],weight_out.at[c,rank],s_weight.at[c,i],r_weight.at[c,i],where)
     def own_weight(c):
-        return pltpu.make_async_copy(weight_parts.at[c,rank],weight_out.at[c,rank],local_sem.at[2,c])
+        return pltpu.make_async_copy(weight_parts.at[c,rank],weight_out.at[c,rank],local_sem.at[1,c])
     def send_table(i):
         return remote(table,table_out.at[rank],s_table.at[i],r_table.at[i],other(i)[1])
     own_table=pltpu.make_async_copy(table,table_out.at[rank],own_sem.at[0])
@@ -249,39 +429,38 @@
     own_piece.start()
     loop(0,chunks,lambda c: own_up(c).start())
     pl.semaphore_wait(barrier,devices-1)
-    loop(0,chunks,lambda c: loop(1,seq_devs,lambda i: send_up(c,i).start()))
+    loop(1,seq_devs,lambda i: send_up(0,i).start())
     width=strip.shape[1]
     full_width=2*length
     lanes=lane_iota(length)
     count=length//bk
     if inside:
         weight_parts[...]=jnp.zeros_like(weight_parts)
+        normed_t[...]=jnp.transpose(normed_ref[...])
     diag[...]=jnp.zeros_like(diag)
     def head_back(c,head):
         index=c*heads+head
         def columns(which):
-            return pl.ds(pl.multiple_of(c*384+which*128,128),128)
-        query,key,value=[proj_ref[:,columns(which)] for which in range(3)]
-        fill_strip(strip,bias_ref[pl.ds(index,1),:],srows,width)
+            return slice(c*chunk_span(heads)+which*128,c*chunk_span(heads)+(which+1)*128)
+        query,both=proj_ref[:,columns(0)],proj_ref[:,columns(1+head)]
+        fill_strip(strip,bias_ref[index:index+1,:],srows,width)
         grads[...]=jnp.zeros_like(grads)
-        kd=dup_head(key,head)
+        kd=dup_head(both,0)
         ka[:,:128]=kd.astype(b16)
         ka[:,128:]=jnp.where(lanes<3,1.0,0.0).astype(b16)
         kt[...]=jnp.transpose(kd).astype(b16)
-        va[...]=jnp.where(lanes<64,dup_head(value,head),jnp.where(lanes<67,1.0,0.0)).astype(b16)
+        va[...]=jnp.where(lanes<64,dup_head(both,1),jnp.where(lanes<67,1.0,0.0)).astype(b16)
         qa[:,:128]=split_query(query,head,scale)
         qa[:,128:]=columns_at(lanes,0,three_parts(-head_column(lse_ref[...],index)),0.0).astype(b16)
         qd[...]=dup_head(query,head).astype(b16)
+        if head==0:
+            take_up(c)
         upstream=dup_head(ups[c],head)
         dd[...]=upstream.astype(b16)
-        delta=0.5*jnp.sum(upstream*dup_head(o32_ref[:,pl.ds(pl.multiple_of(c*128,128),128)],head),axis=1,keepdims=True)
+        delta=0.5*jnp.sum(upstream*dup_head(o32_ref[:,c*128:(c+1)*128],head),axis=1,keepdims=True)
         da[...]=columns_at(lanes,64,three_parts(-delta),jnp.where(lanes<64,upstream,0.0)).astype(b16)
         dk_acc[...]=jnp.zeros_like(dk_acc)
         dv_acc[...]=jnp.zeros_like(dv_acc)
-        def keep(part,rows,values):
-            if head:
-                values=jnp.where(lane_iota(values.shape[0])<64,outs[c,rows,part].astype(f32),values)
-            outs[c,rows,part]=values.astype(b16)
         def query_block(qb):
             qs=pl.ds(pl.multiple_of(qb*bq,bq),bq)
             def products(kb):
@@ -310,49 +489,61 @@
                 following=products(kb+1) if kb+1<count else None
                 dq=consume(kb,*ready,dq)
                 ready=following
-            keep(slice(0,128),qs,jnp.transpose(dq)*0.125)
+            dq=jnp.transpose(dq)*0.125
+            if head:
+                dq=jnp.where(lane_iota(bq)<64,outs[c,qs,0:128].astype(f32),dq)
+            outs[c,qs,0:128]=dq.astype(b16)
+            if head==heads-1:
+                for part in range(bq//stretch):
+                    distance=lax.rem(qb*(bq//stretch)+part-place+seq_devs,seq_devs)
+                    @pl.when(distance==0)
+                    def _():
+                        own_grad(c,0).start()
+                    @pl.when(distance!=0)
+                    def _():
+                        send_grad(c,0,distance).start()
         loop(0,length//bq,query_block)
-        every=slice(0,length)
-        keep(slice(128,256),every,dk_acc[...]*0.125)
-        keep(slice(256,384),every,dv_acc[...])
+        outs[c,:,128*(1+head):128*(2+head)]=jnp.where(lanes<64,dk_acc[...]*0.125,dv_acc[...]).astype(b16)
+        loop(1,seq_devs,lambda i: send_grad(c,1+head,i).start())
+        own_grad(c,1+head).start()
         total=grads[0:8,:]
         for part in range(1,srows//8):
             total=total+pltpu.roll(grads[8*part:8*part+8,:],full_width-8*part,1)
         row=lax.broadcasted_iota(jnp.int32,(8,full_width),0)
         for part in range(1,8):
             total=jnp.where(row==part,pltpu.roll(total,full_width-part,1),total)
-        diag[pl.ds(index,1),:]=jnp.sum(total,axis=0,keepdims=True)
-    def one_chunk(c):
+        diag[index:index+1,:]=jnp.sum(total,axis=0,keepdims=True)
+    def take_up(c):
         loop(1,seq_devs,lambda i: landed(ups.at[c,rows_of(lax.rem(place-i+seq_devs,seq_devs))],r_up.at[c,i]))
         own_up(c).wait()
-        @pl.when(c==0)
-        def _():
+        if c==0:
+            loop(1,chunks,lambda later: loop(1,seq_devs,lambda i: send_up(later,i).start()))
             loop(1,experts,lambda i: send_res(i).start())
             loop(1,devices,lambda i: send_piece(i).start())
+    def one_chunk(c):
         for head in range(heads):
             head_back(c,head)
-        loop(1,seq_devs,lambda i: send_grad(c,i).start())
-        own_grad(c).start()
         if inside:
             part=jnp.dot(normed_t[...],outs[c],preferred_element_type=f32)
             block=normed_t.shape[0]//devices
-            weight_parts[c,:,:block,:]=part.reshape(devices,block,384).astype(b16)
+            weight_parts[c,:,:block,:]=part.reshape(devices,block,chunk_span(heads)).astype(b16)
             loop(1,devices,lambda i: send_weight(c,i).start())
             own_weight(c).start()
-    loop(0,chunks,one_chunk)
+    for c in range(chunks):
+        one_chunk(c)
     table[...]=lax.dot_general(bucket_ref[...],diag[...],NT,precision=lax.Precision.HIGHEST,preferred_element_type=f32)
     loop(1,devices,lambda i: send_table(i).start())
     own_table.start()
-    def back(i,total):
-        return lax.rem(i[0]-i[1]+total,total)
     def finish_chunk(c):
         def grad_landed(i):
             source=lax.rem(place-i+seq_devs,seq_devs)
-            landed(grad_out.at[source//groups,:,lanes_of(source%groups,c,384)],r_grad.at[c,i])
-            send_grad(c,i).wait_send()
+            for part in range(1+heads):
+                landed(grad_out.at[source//groups,:,grad_lanes(source%groups,c,part)],r_grad.at[c,part,i])
+                send_grad(c,part,i).wait_send()
             send_up(c,i).wait_send()
         loop(1,seq_devs,grad_landed)
-        own_grad(c).wait()
+        for part in range(1+heads):
+            own_grad(c,part).wait()
         if inside:
             def weight_landed(i):
                 landed(weight_out.at[c,lax.rem(rank-i+devices,devices)],r_weight.at[c,i])
@@ -375,12 +566,12 @@
     own_piece.wait()
     own_table.wait()
 
-def attend_back(plan,projected,o32,lse,bias_vec,normed_t,buckets,upstream,result,piece,bq=512,bk=512,srows=128):
+def attend_back(plan,projected,o32,lse,bias_vec,normed,buckets,upstream,result,piece,bq=512,bk=512,srows=128):
     experts,seq_devs,seq_count,stretch,heads,chunks=plan
     length=stretch*seq_devs
     groups=seq_devs//seq_count
     devices=experts*seq_devs
-    block=normed_t.shape[0]//devices
+    block=normed.shape[1]//devices
     inside=block%8==0
     rows=(block+15)//16*16
     f32,b16=jnp.float32,jnp.bfloat16
@@ -389,24 +580,145 @@
     anywhere=pl.BlockSpec(memory_space=pl.ANY)
     dma=lambda *shape: pltpu.SemaphoreType.DMA(shape)
     shape=lambda kind,*dims: jax.ShapeDtypeStruct(dims,kind)
-    weight_shape=(chunks,devices,rows,384) if inside else (1,1,16,128)
+    weight_shape=(chunks,devices,rows,chunk_span(heads)) if inside else (1,1,16,128)
     return pl.pallas_call(
         functools.partial(backward_kernel,plan,inside,bq,bk,srows,LOG2E/8),
         in_specs=[vmem]*6+[anywhere]*3,
         out_specs=[anywhere]*5,
-        out_shape=[shape(b16,seq_count,stretch,groups*chunks*384),shape(b16,*result.shape),shape(b16,*piece.shape),shape(b16,*weight_shape),shape(f32,devices,buckets.shape[0],diag_rows(plan))],
+        out_shape=[shape(b16,seq_count,stretch,groups*chunks*chunk_span(heads)),shape(b16,*result.shape),shape(b16,*piece.shape),shape(b16,*weight_shape),shape(f32,devices,buckets.shape[0],diag_rows(plan))],
         scratch_shapes=[vm(f32,srows,2*length-srows),vm(f32,srows,2*length),vm(b16,length,256),vm(b16,length,128),vm(b16,128,length),
             vm(b16,length,256),vm(b16,length,128),vm(b16,length,128),vm(b16,length,128),vm(f32,length,128),vm(f32,length,128),
-            vm(b16,chunks,length,128),vm(b16,chunks,length,384),vm(b16,*weight_shape),vm(f32,diag_rows(plan),2*length),vm(f32,buckets.shape[0],diag_rows(plan)),
-            dma(chunks,seq_devs),dma(chunks,seq_devs),dma(experts),dma(experts),dma(devices),dma(devices),dma(chunks,seq_devs),dma(chunks,seq_devs),
-            dma(chunks,devices),dma(chunks,devices),dma(devices),dma(devices),dma(3,chunks),dma(4)],
+            vm(b16,chunks,length,128),vm(b16,chunks,length,chunk_span(heads)),vm(b16,*weight_shape),vm(f32,diag_rows(plan),2*length),vm(f32,buckets.shape[0],diag_rows(plan)),vm(b16,normed.shape[1],length),
+            dma(chunks,seq_devs),dma(chunks,seq_devs),dma(experts),dma(experts),dma(devices),dma(devices),dma(chunks,1+heads,seq_devs),dma(chunks,1+heads,seq_devs),
+            dma(chunks,devices),dma(chunks,devices),dma(devices),dma(devices),dma(3+heads,chunks),dma(4)],
         compiler_params=pltpu.CompilerParams(collective_id=2,has_side_effects=True,vmem_limit_bytes=58*MIB),
         cost_estimate=pl.CostEstimate(flops=40*heads*chunks*length*length*64,bytes_accessed=24*MIB,transcendentals=heads*chunks*length*length),
         name="attend_backward",
-    )(projected,o32,lse,bias_vec,normed_t,buckets,upstream,result,piece)
+    )(projected,o32,lse,bias_vec,normed,buckets,upstream,result,piece)
 
 def diag_rows(plan):
     return 128
+
+def combine_kernel(experts,pos_ref,home_ref,hidden_ref,cot_ref,att_ref,out_w_ref,gain_ref,router_ref,grad_ref,heads_ref,part_ref,total,gain_total):
+    f32,b16=jnp.float32,jnp.bfloat16
+    step=pl.program_id(0)
+    rows=hidden_ref.shape[0]
+    slots=home_ref.shape[0]
+    width=hidden_ref.shape[1]
+    hot=(pos_ref[...]==lax.broadcasted_iota(jnp.int32,(rows,slots),1)).astype(f32).astype(b16)
+    moe_in_grad=jnp.dot(hot,home_ref[...],preferred_element_type=f32)
+    hidden=hidden_ref[...]
+    inverse=lax.rsqrt(jnp.mean(hidden*hidden,axis=-1,keepdims=True)+EPSILON)
+    weighted=moe_in_grad*gain_ref[...]
+    inner=jnp.mean(weighted*hidden,axis=-1,keepdims=True)
+    hidden_grad=cot_ref[...].astype(f32)+weighted*inverse-hidden*(inverse*inverse*inverse)*inner
+    grad_ref[...]=hidden_grad
+    branch=hidden_grad.astype(b16)
+    heads_ref[...]=lax.dot_general(branch,out_w_ref[...],NT,preferred_element_type=f32).astype(b16)
+    part=lax.dot_general(att_ref[...],branch,TN,preferred_element_type=f32)
+    gain_part=jnp.sum(moe_in_grad*hidden*inverse,axis=0,keepdims=True)
+    @pl.when(step==0)
+    def _():
+        total[...]=part
+        gain_total[...]=jnp.broadcast_to(gain_part,gain_total.shape)
+    @pl.when(step>0)
+    def _():
+        total[...]+=part
+        gain_total[...]+=gain_part
+    @pl.when(step==pl.num_programs(0)-1)
+    def _():
+        heads_width=total.shape[0]
+        part_ref[:,:width]=total[...].astype(b16)
+        column=jnp.transpose(jnp.broadcast_to(gain_total[0:1,:],(128,width)))
+        lanes=lax.broadcasted_iota(jnp.int32,(width,128),1)
+        part_ref[:width,width:]=jnp.where(lanes==experts,column,router_ref[...]).astype(b16)
+
+def combine(experts,position,home,hidden,cotangent,attended,out_full,gain,router_part,block=256):
+    count,width=hidden.shape
+    heads_width=attended.shape[1]
+    f32,b16=jnp.float32,jnp.bfloat16
+    block=min(block,count)
+    by_rows=lambda columns: pl.BlockSpec((block,columns),lambda i:(i,0))
+    whole=lambda value: pl.BlockSpec(value.shape,lambda i:(0,0))
+    return pl.pallas_call(
+        functools.partial(combine_kernel,experts),
+        grid=(count//block,),
+        in_specs=[by_rows(1),whole(home),by_rows(width),by_rows(width),by_rows(heads_width),whole(out_full),whole(gain),whole(router_part)],
+        out_specs=[by_rows(width),by_rows(heads_width),pl.BlockSpec((heads_width,width+128),lambda i:(0,0))],
+        out_shape=[jax.ShapeDtypeStruct((count,width),f32),jax.ShapeDtypeStruct((count,heads_width),b16),jax.ShapeDtypeStruct((heads_width,width+128),b16)],
+        scratch_shapes=[pltpu.VMEM((heads_width,width),f32),pltpu.VMEM((8,width),f32)],
+        compiler_params=pltpu.CompilerParams(vmem_limit_bytes=40*MIB),
+        cost_estimate=pl.CostEstimate(flops=6*count*width*width,bytes_accessed=16*MIB,transcendentals=0),
+        name="combine",
+    )(position,home,hidden,cotangent,attended,out_full,gain,router_part)
+
+def finish_kernel(experts,groups,heads,chunks,inside,pos_ref,pick_ref,returned_ref,hidden_ref,grad_ref,token_ref,token_grad_ref,every_ref,gains_ref,router_ref,piece_ref,weight_ref,table_ref,
+                  output_ref,input_ref,piece_sum,query_sum,key_sum,value_sum,table_sum):
+    f32,b16=jnp.float32,jnp.bfloat16
+    step=pl.program_id(0)
+    rows,width=hidden_ref.shape
+    slots=returned_ref.shape[0]
+    cw=chunk_span(heads)
+    span=chunks*cw
+    hidden=hidden_ref[...]
+    moe_in=(hidden*lax.rsqrt(jnp.mean(hidden*hidden,axis=-1,keepdims=True)+EPSILON)*gains_ref[1:2,:]).astype(b16)
+    lanes=lax.broadcasted_iota(jnp.int32,(rows,128),1)
+    logits=jnp.where(lanes<experts,jnp.dot(moe_in,router_ref[...],preferred_element_type=f32),-jnp.inf)
+    raised=jnp.exp(logits-jnp.max(logits,axis=1,keepdims=True))
+    gate=jnp.sum(jnp.where(lanes==pick_ref[...],raised,0.0),axis=1,keepdims=True)/jnp.sum(raised,axis=1,keepdims=True)
+    hot=(pos_ref[...]==lax.broadcasted_iota(jnp.int32,(rows,slots),1)).astype(f32).astype(b16)
+    output_ref[...]=(hidden+gate*jnp.dot(hot,returned_ref[...],preferred_element_type=f32)).astype(b16)
+    normed_grad=jnp.zeros((rows,width),f32)
+    for owner in range(groups):
+        normed_grad=normed_grad+lax.dot_general(token_grad_ref[:,owner*span:(owner+1)*span],every_ref[owner,:,:span],NT,preferred_element_type=f32)
+    x=token_ref[...].astype(f32)
+    inverse=lax.rsqrt(jnp.mean(x*x,axis=-1,keepdims=True)+EPSILON)
+    weighted=normed_grad*gains_ref[0:1,:]
+    inner=jnp.mean(weighted*x,axis=-1,keepdims=True)
+    input_ref[...]=grad_ref[...]+weighted*inverse-x*(inverse*inverse*inverse)*inner
+    @pl.when(step==0)
+    def _():
+        devices=piece_ref.shape[0]
+        def add_piece(i,total):
+            return total+piece_ref[i].astype(f32)
+        piece_sum[...]=lax.fori_loop(1,devices,add_piece,piece_ref[0].astype(f32))
+        for owner in range(groups):
+            def add_table(i,total):
+                return total+table_ref[i*groups+owner]
+            table_sum[owner]=lax.fori_loop(1,devices//groups,add_table,table_ref[owner])
+            if inside:
+                for c in range(chunks):
+                    def add_weight(i,total):
+                        return total+weight_ref[c,i*groups+owner].astype(f32)
+                    summed=lax.fori_loop(1,devices//groups,add_weight,weight_ref[c,owner].astype(f32))
+                    place=slice((owner*chunks+c)*128,(owner*chunks+c+1)*128)
+                    query_sum[:,place]=summed[:,0:128]
+                    first=summed[:,128:256]
+                    second=summed[:,128*heads:128*(heads+1)]
+                    low=lane_iota(summed.shape[0])<64
+                    key_sum[:,place]=jnp.where(low,first,pltpu.roll(second,64,1))
+                    value_sum[:,place]=jnp.where(low,pltpu.roll(first,64,1),second)
+
+def finish(experts,groups,heads,chunks,inside,position,pick,returned,hidden,hidden_grad,tokens,token_grads,every_weight,gains,router,pieces,weights,tables,block=256):
+    count,width=hidden.shape
+    f32,b16=jnp.float32,jnp.bfloat16
+    block=min(block,count)
+    by_rows=lambda columns: pl.BlockSpec((block,columns),lambda i:(i,0))
+    def whole(shape):
+        return pl.BlockSpec(shape,lambda i:(0,)*len(shape))
+    sums=jax.ShapeDtypeStruct((pieces.shape[1],groups*chunks*128),f32)
+    table_shape=jax.ShapeDtypeStruct((groups,)+tables.shape[1:],f32)
+    piece_shape=jax.ShapeDtypeStruct(pieces.shape[1:],f32)
+    return pl.pallas_call(
+        functools.partial(finish_kernel,experts,groups,heads,chunks,inside),
+        grid=(count//block,),
+        in_specs=[by_rows(1),by_rows(1),whole(returned.shape),by_rows(width),by_rows(width),by_rows(width),by_rows(token_grads.shape[1]),whole(every_weight.shape),whole(gains.shape),whole(router.shape),whole(pieces.shape),whole(weights.shape),whole(tables.shape)],
+        out_specs=[by_rows(width),by_rows(width),whole(piece_shape.shape)]+[whole(sums.shape)]*3+[whole(table_shape.shape)],
+        out_shape=[jax.ShapeDtypeStruct((count,width),b16),jax.ShapeDtypeStruct((count,width),f32),piece_shape,sums,sums,sums,table_shape],
+        compiler_params=pltpu.CompilerParams(vmem_limit_bytes=56*MIB),
+        cost_estimate=pl.CostEstimate(flops=8*count*width*width,bytes_accessed=24*MIB,transcendentals=0),
+        name="finish",
+    )(position,pick,returned,hidden,hidden_grad,tokens,token_grads,every_weight,gains,router,pieces,weights,tables)
 
 def gelu_pair(u):
     c=0.7978845608028654
@@ -432,7 +744,7 @@
     load1=pltpu.make_async_copy(w1_hbm,w1,local_sem.at[0])
     load2=pltpu.make_async_copy(w2_hbm,w2,local_sem.at[1])
     own_rows=pltpu.make_async_copy(send_ref.at[me],rows.at[side],local_sem.at[2])
-    local=[load1,load2,own_rows]
+    local=[own_rows,load1,load2]
     cot_loads=[pltpu.make_async_copy(cot_hbm.at[device(-j,m)],cots.at[2*j+m],cot_sem.at[2*j+m]) for j in range(pairs) for m in range(2)]
     for copy in local+cot_loads:
         copy.start()
@@ -531,7 +843,7 @@
     for copy in started:
         copy.wait_send()
 
-def expert_layer(send,cot,w1,w2,router,cid=20):
+def expert_layer(send,cot,w1,w2,router,cid=4):
     experts,cap,width=send.shape
     hidden_width=w1.shape[1]
     b16=jnp.bfloat16
@@ -592,26 +904,34 @@
     per_chunk=2 if own_heads%2==0 else 1
     chunks=own_heads//per_chunk
     used=per_chunk*head_dim
-    span=chunks*384
+    span=chunks*chunk_span(per_chunk)
     heads_width=groups*chunks*128
     row_block=width//devices
     place=lax.axis_index("seq")
     group=place%groups
     def by_group(weight):
-        cut=weight.reshape(row_block,groups,chunks,used)
-        return jnp.pad(cut,((0,0),(0,0),(0,0),(0,128-used)))
-    stacked=jnp.stack([by_group(w) for w in (query_weight,key_weight,value_weight)],axis=3).reshape(row_block,groups*span)
-    stacked_full=lax.all_gather(stacked,BOTH,axis=0,tiled=True)
+        return weight.reshape(row_block,groups,chunks,per_chunk,head_dim)
+    query_part=jnp.pad(by_group(query_weight).reshape(row_block,groups,chunks,used),((0,0),(0,0),(0,0),(0,128-used)))
+    both_part=jnp.concatenate([by_group(key_weight),by_group(value_weight)],axis=4).reshape(row_block,groups,chunks,per_chunk*128)
+    stacked=jnp.concatenate([query_part,both_part],axis=3).reshape(row_block,groups,span)
     gains=jnp.stack([attn_gain,moe_gain],axis=1)
     small=jnp.pad(jnp.concatenate([router_weight,gains],axis=1),((0,0),(0,126-experts)))
-    small_full=lax.all_gather(small,BOTH,axis=0,tiled=True)
+    units=jnp.concatenate([stacked,jnp.broadcast_to(small[:,None],(row_block,groups,128))],axis=2)
     out_full=lax.all_gather(out_weight,BOTH,axis=0,tiled=True)
     out_full=jnp.pad(out_full.reshape(groups*chunks,used,width),((0,0),(0,128-used),(0,0))).reshape(heads_width,width)
-    first_full=lax.all_gather(expert_in,"seq",axis=2,tiled=True)[0]
-    second_full=lax.all_gather(expert_out,"seq",axis=1,tiled=True)[0]
-    copies=jnp.broadcast_to(tokens[:,None],(seq_count,groups,stretch,width)).reshape(seq_devs,stretch,width)
-    own_sequence=swap_parts(copies,"seq").reshape(length,width).astype(f32)
-    weight=lax.dynamic_slice_in_dim(stacked_full,group*span,span,axis=1)
+    plan=(experts,seq_devs,seq_count,stretch,per_chunk,chunks)
+    if row_block%8==0 and row_block*seq_devs%16==0:
+        units=jnp.pad(jnp.swapaxes(units,0,1),((0,0),(0,-row_block%16),(0,0)))
+        projected,normed,own_weight,first_full=gather_start(plan,row_block,tokens,units,expert_in)
+    else:
+        copies=jnp.broadcast_to(tokens[:,None],(seq_count,groups,stretch,width)).reshape(seq_devs,stretch,width)
+        own_sequence=swap_parts(copies,"seq").reshape(length,width).astype(f32)
+        every=lax.all_gather(units,BOTH,axis=0,tiled=True)
+        own_weight=lax.dynamic_index_in_dim(every,group,axis=1,keepdims=False)
+        normed=(own_sequence*inverse_rms(own_sequence)*own_weight[:,span+experts].astype(f32)).astype(b16)
+        projected=matmul(normed,own_weight[:,:span]).astype(b16)
+        first_full=lax.all_gather(expert_in[0],"seq",axis=1,tiled=True)
+    small_full=own_weight[:,span:]
     router_full=small_full[:,:experts]
     router_wide=jnp.where(jnp.arange(128)[None,:]<experts,small_full,jnp.zeros((),b16))
     attn_gain_full=small_full[:,experts].astype(f32)
@@ -628,10 +948,7 @@
     position=jnp.where(slot_pick<capacity,expert_pick*padded_cap+slot_pick,slots)
     hot=(position[None,:]==jnp.arange(slots,dtype=jnp.int32)[:,None]).astype(b16)
     cot_rows=matmul(hot,cotangent.reshape(count,width)).astype(b16).reshape(experts,padded_cap,width)
-    plan=(experts,seq_devs,seq_count,stretch,per_chunk,chunks)
-    normed=(own_sequence*inverse_rms(own_sequence)*attn_gain_full).astype(b16)
-    projected=matmul(normed,weight).astype(b16)
-    attended,out32,log_total,cot_arrived=attend(plan,projected,forward_bias,cot_rows)
+    attended,out32,log_total,cot_arrived,every_weight,second_full=attend(plan,projected,forward_bias,cot_rows,own_weight,expert_out)
     attended=attended.reshape(count,heads_width)
     tokens_f=tokens.astype(f32).reshape(count,width)
     hidden=tokens_f+matmul(attended,out_full)
@@ -641,46 +958,32 @@
     home,result,first_grad,second_grad,router_part=expert_layer(send_rows,cot_arrived,first_full,second_full,router_wide)
     expert_in_grad=lax.psum_scatter(first_grad[None],"seq",scatter_dimension=2,tiled=True).astype(f32)
     expert_out_grad=lax.psum_scatter(second_grad[None],"seq",scatter_dimension=1,tiled=True).astype(f32)
-    grad_out=cotangent.astype(f32).reshape(count,width)
-    moe_in_grad=matmul(hot,home.reshape(slots,width),TN)
-    weighted=moe_in_grad*moe_gain_full
-    moe_gain_part=jnp.sum(moe_in_grad*hidden*moe_inverse,axis=0)
-    inner=jnp.mean(weighted*hidden,axis=-1,keepdims=True)
-    hidden_grad=grad_out+weighted*moe_inverse-hidden*(moe_inverse*moe_inverse*moe_inverse)*inner
-    branch_grad=hidden_grad.astype(b16)
-    heads_grad=matmul(branch_grad,out_full,NT).astype(b16)
-    out_part=matmul(attended,branch_grad,TN).reshape(groups*chunks,128,width)[:,:used].reshape(width,width)
-    extra=jnp.pad(jnp.concatenate([router_part[:,:experts],moe_gain_part[:,None]],axis=1),((0,0),(0,127-experts)))
-    out_piece=jnp.concatenate([out_part,extra],axis=1).astype(b16).reshape(devices,row_block,width+128)
-    out_piece=jnp.pad(out_piece,((0,0),(0,-row_block%16),(0,0)))
+    gain_rows=jnp.transpose(small_full[:,experts:experts+2].astype(f32))
+    home=home.reshape(slots,width)
+    positions=position[:,None]
+    hidden_grad,heads_grad,out_part=combine(experts,positions,home,hidden,cotangent.reshape(count,width),attended,out_full,gain_rows[1:2],router_part)
+    out_part=jnp.concatenate([out_part[:,:width].reshape(groups*chunks,128,width)[:,:used].reshape(width,width),out_part[:width,width:]],axis=1) if used<128 else out_part
+    out_piece=jnp.pad(out_part.reshape(devices,row_block,width+128),((0,0),(0,-row_block%16),(0,0)))
     hot_bucket=(backward_ids[None,:]==jnp.arange(buckets,dtype=jnp.int32)[:,None]).astype(f32)
     hot_bucket=hot_bucket*(jnp.arange(length*2)>0)[None,:]
-    normed_t=jnp.transpose(normed)
-    token_grads,returned,out_pieces,weight_pieces,tables=attend_back(plan,projected,out32,log_total,backward_bias,normed_t,hot_bucket,heads_grad.reshape(seq_count,stretch,heads_width),result,out_piece)
-    out_sum=jnp.sum(out_pieces[:,:row_block].astype(f32),axis=0)
-    logits=matmul(moe_in,router_full)
-    gates=jax.nn.softmax(logits,axis=-1)
-    picked=(expert_pick[:,None]==jnp.arange(experts,dtype=jnp.int32)[None,:]).astype(f32)
-    gate=jnp.sum(gates*picked,axis=-1)
-    output=(hidden+gate[:,None]*matmul(hot,returned.reshape(slots,width),TN)).astype(b16).reshape(seq_count,stretch,width)
-    tables=jnp.sum(tables.reshape(devices//groups,groups,buckets,-1),axis=0)[:,:,:own_heads]
-    bias_table_grad=jnp.transpose(tables,(1,0,2)).reshape(buckets,heads)
+    token_grads,returned,out_pieces,weight_pieces,tables=attend_back(plan,projected,out32,log_total,backward_bias,normed,hot_bucket,heads_grad.reshape(seq_count,stretch,heads_width),result,out_piece)
+    inside=row_block%8==0
     token_grads=token_grads.reshape(count,groups*span)
-    normed_grad=matmul(token_grads,stacked_full,NT)
-    if row_block%8:
+    output,input_grad,out_sum,*weight_grads,tables=finish(experts,groups,per_chunk,chunks,inside,positions,expert_pick[:,None],returned.reshape(slots,width),hidden,hidden_grad,tokens.reshape(count,width),token_grads,every_weight,gain_rows,router_wide,out_pieces,weight_pieces,tables)
+    out_sum=out_sum[:row_block]
+    output=output.reshape(seq_count,stretch,width)
+    bias_table_grad=jnp.transpose(tables[:,:,:own_heads],(1,0,2)).reshape(buckets,heads)
+    if inside:
+        weight_grads=jnp.stack([part[:row_block] for part in weight_grads])
+    else:
+        tokens_f=tokens.astype(f32).reshape(count,width)
         normed_own=(tokens_f*inverse_rms(tokens_f)*attn_gain_full).astype(b16)
-        parts=matmul(normed_own,token_grads,TN).astype(b16).reshape(devices,row_block,groups,chunks,3,128)
+        parts=matmul(normed_own,token_grads,TN).astype(b16).reshape(devices,row_block,groups*chunks,1+per_chunk,128)
         summed=jnp.sum(swap_parts(parts,BOTH).astype(f32),axis=0)
-    else:
-        parts=weight_pieces[:,:,:row_block].astype(f32).reshape(chunks,devices//groups,groups,row_block,3,128)
-        summed=jnp.transpose(jnp.sum(parts,axis=1),(2,1,0,3,4))
-    weight_grads=jnp.transpose(summed[...,:used],(3,0,1,2,4)).reshape(3,row_block,width)
+        both_sum=summed[:,:,1:].reshape(row_block,groups*chunks,per_chunk,2,head_dim)
+        weight_grads=jnp.stack([summed[:,:,0,:used].reshape(row_block,width)]+[both_sum[:,:,:,i].reshape(row_block,width) for i in range(2)])
     own_weights=jnp.stack([query_weight,key_weight,value_weight]).astype(f32)
     attn_gain_grad=jnp.sum(weight_grads*own_weights,axis=(0,2))/attn_gain.astype(f32)
-    tokens_inverse=inverse_rms(tokens_f)
-    weighted=normed_grad*attn_gain_full
-    inner=jnp.mean(weighted*tokens_f,axis=-1,keepdims=True)
-    input_grad=hidden_grad+weighted*tokens_inverse-tokens_f*(tokens_inverse*tokens_inverse*tokens_inverse)*inner
     return (
         output,
         input_grad.reshape(seq_count,stretch,width),

time: 580 us -> 495 us (0.85)
  Pallas kernels: 312 us -> 404 us
  blocking collectives: 74.1 us -> 0 us
  waiting for transfers between devices: 51.1 us -> 0.72 us
  matrix products: 46.6 us -> 15.3 us
  other arithmetic: 35.7 us -> 14.4 us
  local copies, waits for them, and re-layouts: 31.5 us -> 37.6 us
    pallas_call x0 -> x3, Pallas kernels: none -> 87.3 us  [the longest x1 59.8 us: gather_start(): pl.pallas_call(functools.partial(start_kernel, plan, rows, span), in_spec...]
    all_gather x1 -> x0, blocking collectives: 74.1 us -> none  [shards(): small_full = lax.all_gather(small, BOTH, axis=0, tiled=True)]
    all_gather x3 -> x0, waiting for transfers between devices: 49.2 us -> none  [the longest x1 38.9 us: shards(): second_full = lax.all_gather(expert_out, 'seq', axis=1, tiled=True)[0]]
    dot_general x11 -> x4, matrix products: 45.4 us -> 13.4 us  [matmul(): lax.dot_general(left, right, dims, preferred_element_type=jnp.float32)]
    unnamed x92 -> x69, local copies, waits for them, and re-layouts: 9.22 us -> 18.7 us
    reduce_sum x7 -> x0, other arithmetic: 8.77 us -> none  [the longest x1 3.63 us: shards(): summed = jnp.transpose(jnp.sum(parts, axis=1), (2, 1, 0, 3, 4))]
    pallas_call x1, Pallas kernels: 163 us -> 169 us  [attend_back(): pl.pallas_call(functools.partial(backward_kernel, plan, inside, bq, bk, s...]
  transfers between devices with their start and end apart: 7 -> 3, of which waited for: 2 -> 0; matrix products, arithmetic and copies ran while one was open for 17% -> 9% of each run, Pallas kernels for 38% -> 63%
where the time goes in v3:
time: 495 us; the launch traced here: 486 us
  Pallas kernels  404 us (82%)
  local copies, waits for them, and re-layouts  37.6 us (8%)
  matrix products  15.3 us (3%)
  between operations  14.6 us (3%)
  other arithmetic  14.4 us (3%)
    pallas_call x1, Pallas kernels, attend_back(): pl.pallas_call(functools.partial(backward_kernel, plan, inside, bq, bk, s...  169 us
    pallas_call x1, Pallas kernels, expert_layer(): pl.pallas_call(functools.partial(expert_kernel, experts, cap, width, hidd...  98.1 us
    pallas_call x1, Pallas kernels, gather_start(): pl.pallas_call(functools.partial(start_kernel, plan, rows, span), in_spec...  59.8 us
    pallas_call x1, Pallas kernels, attend(): pl.pallas_call(functools.partial(forward_kernel, plan, block, srows, LOG2...  48.9 us
    unnamed x69, local copies, waits for them, and re-layouts  18.7 us
    pallas_call x1, Pallas kernels, finish(): pl.pallas_call(functools.partial(finish_kernel, experts, groups, heads, c...  17 us
    dot_general x4, matrix products, matmul(): lax.dot_general(left, right, dims, preferred_element_type=jnp.float32)  13.4 us
    pallas_call x1, Pallas kernels, combine(): pl.pallas_call(functools.partial(combine_kernel, experts), grid=(count //...  10.5 us
  transfers between devices with their start and end apart: 3, of which 0 were waited for; matrix products, arithmetic and copies ran while one was open for 9% of the time, Pallas kernels for 63%

profile of v3, /device:TPU:0, one launch (start us, length us, event | category | flops | bytes accessed | tf_op | source)
XLA Modules:
  0.0 486.4 jit_solution(18016873149035181394)
XLA Ops:
  9.5 1.3 convert.7
  13.9 1.3 copy-done.6
  15.2 59.8 %gather_start.1 = (bf16[2048,1152]{1,0:T(8,128)(2,1)S(1)}, bf16[2048,768]{1,0:T(8,128)(2,1)S(1)}, bf16[768,1280]{1,0:T(8,128)(2,1)S(1)}, bf16[768,3072]{1,0:T(8,128)(2,1)}) custom-call(bf16[2,512,768]{2,1,0:T(8,128)(2,1)S(1)} %copy-done.4, bf16[2,32,1280]{2,1,0:T(8,128)(2,1)S(1)} %pad.13.unit_ref, bf16[1,768,768]{2,1,0:T(8,128)(2,1)S(1)} %copy-done.6), custom_call_target="tpu_custom_call" | custom-call | flops 3623878656 | bytes 25165824 | tf_op jit(solution)/shard_map/gather_start/pallas_call | solution.py:208
  75.0 2.2 copy-done.13
  77.3 1.7 copy-done.15
  80.6 5.1 %fusion.2 = bf16[1280,768]{1,0:T(8,128)(2,1)} fusion(bf16[1024,768]{1,0:T(8,128)(2,1)} %bitcast.72, s32[1024]{0:T(1024)S(1)} %bitcast.91), kind=kOutput, calls=%fused_computation.3 | convolution fusion | flops 2015559680 | bytes 3543040 | tf_op jit(solution)/shard_map/dot_general | solution.py:873
  85.7 1.1 fusion.8
  87.8 1.3 copy-done.7
  89.1 48.9 %attend_forward.1 = (bf16[2,512,768]{2,1,0:T(8,128)(2,1)S(1)}, f32[2048,384]{1,0:T(8,128)}, f32[2048,128]{1,0:T(8,128)S(1)}, bf16[8,160,768]{2,1,0:T(8,128)(2,1)...) custom-call(bf16[2048,1152]{1,0:T(8,128)(2,1)} %copy-done.13, f32[6,4096]{1,0:T(8,128)S(1)} %fusion.12.bias_ref, ...), custom_call_target="tpu_custom_call" | custom-call | flops 25769803776 | bytes 16777216 | tf_op jit(solution)/shard_map/attend_forward/pallas_call | solution.py:365
  138.0 1.3 copy-done.16
  140.3 3.4 multiply_reduce_fusion
  143.7 3.9 fusion.3
  147.6 98.1 %expert_layer.1 = (bf16[8,160,768]{2,1,0:T(8,128)(2,1)}, bf16[8,160,768]{2,1,0:T(8,128)(2,1)}, bf16[768,3072]{1,0:T(8,128)(2,1)}, bf16[3072,768]{1,0:T(8,128)(2,1)}, f32[768,128]{1,0:T(8,128)}) custom-call(bf16[8,160,768]{2,1,0:T(8,128)(2,1)} %bitcast.98, bf16[8,160,768]{2,1,0:T(8,128)(2,1)} %copy-done.16, bf16[768,3072]{1,0:T(8,128)(2,1)} %get-tuple-element.49.w1_hbm, ...), custom_call_target="tpu_custom_call" | custom-call | flops 36238786560 | bytes 41943040 | tf_op jit(solution)/shard_map/expert_layer/pallas_call | solution.py:856
  245.8 1.4 copy-done.2
  247.3 2.4 copy.59
  251.7 1.0 copy.70
  252.7 1.0 copy.68
  253.7 1.5 fusion.9.pos_ref
  256.2 1.9 copy-done.9
  258.1 1.7 copy-done.11
  259.8 10.5 %combine.1 = (f32[1024,768]{1,0:T(8,128)S(1)}, bf16[1024,768]{1,0:T(8,128)(2,1)S(1)}, bf16[768,896]{1,0:T(8,128)(2,1)S(1)}) custom-call(s32[1024,1]{1,0:T(8,128)S(1)} %fusion.9.pos_ref, bf16[1280,768]{1,0:T(8,128)(2,1)S(1)} %bitcast.74, f32[1024,768]{1,0:T(8,128)} %copy-done.18, bf16[1024,768]{1,0:T(8,128)(2,1)S(1)} %bitcast.73, ...), custom_call_target="tpu_custom_call" | custom-call | flops 3623878656 | bytes 16777216 | tf_op jit(solution)/shard_map/combine/pallas_call | solution.py:643
  270.4 1.7 copy-done
  272.1 1.5 pad.14.piece_ref
  273.8 169.2 %attend_backward.1 = (bf16[2,512,2304]{2,1,0:T(8,128)(2,1)}, bf16[8,160,768]{2,1,0:T(8,128)(2,1)}, bf16[32,32,896]{2,1,0:T(8,128)(2,1)}, bf16[3,32,32,384]{3,2,1,0:T(8,128)(2,1)}, f32[32,32,128]{2,1,0:T(8,128)}) custom-call(bf16[2048,1152]{1,0:T(8,128)(2,1)} %copy-done.13, f32[2048,384]{1,0:T(8,128)} %get-tuple-element.44.o32_ref, f32[2048,128]{1,0:T(8,128)} %copy-done.17, ...), custom_call_target="tpu_custom_call" | custom-call | flops 64424509440 | bytes 25165824 | tf_op jit(solution)/shard_map/attend_backward/pallas_call | solution.py:584
  443.1 17.0 %finish.1 = (bf16[1024,768]{1,0:T(8,128)(2,1)}, f32[1024,768]{1,0:T(8,128)}, f32[32,896]{1,0:T(8,128)}, f32[32,768]{1,0:T(8,128)}, f32[32,768]{1,0:T(8,128)}, /*index=5*/f32[32,768]{1,0:T(8,128)}, f32[2,32,128]{2,1,0:T(8,128)}) custom-call(s32[1024,1]{1,0:T(8,128)} %copy-done.3, s32[1024,1]{1,0:T(8,128)} %bitcast.78, bf16[1280,768]{1,0:T(8,128)(2,1)} %bitcast.82, ...), custom_call_target="tpu_custom_call" | custom-call | flops 4831838208 | bytes 25165824 | tf_op jit(solution)/shard_map/finish/pallas_call | solution.py:712
  460.8 1.5 slice.46
  464.4 1.5 slice.43
  466.0 1.5 slice.44
  467.5 1.5 slice.45
  471.8 1.4 slice_reduce_fusion
  473.8 2.8 convert_element_type.86
  476.6 2.8 convert_element_type.85
  (102 shorter events, 18.3 us)
Async XLA Ops:
  7.2 6.7 %copy-start.4 = (bf16[2,512,768]{2,1,0:T(8,128)(2,1)S(1)}, bf16[2,512,768]{2,1,0:T(8,128)(2,1)}, u32[]{:S(2)}) copy-start(bf16[2,512,768]{2,1,0:T(8,128)(2,1)} %token_ref.1) | copy-start | bytes 4718596
  7.2 133.1 %all-gather.2.cloned.1.call-start = ((), (), s32[]{:S(2)}) async-start(), calls=%async_computation.2 | async-start | bytes 1216512 | tf_op jit(solution)/shard_map/all_gather | solution.py:920
  7.9 465.8 %reduce-scatter.5.cloned.1.call-start = ((), (), s32[]{:S(2)}) async-start(), calls=%async_computation.4 | async-start | bytes 5898240 | tf_op jit(solution)/shard_map/reduce_scatter | solution.py:960
  9.5 71.1 %copy-start.28 = (s32[1,4,2,128]{3,1,2,0:T(4,128)}, s32[1,4,2,128]{3,1,2,0:T(4,128)S(1)}, u32[]{:S(2)}) copy-start(s32[1,4,2,128]{3,1,2,0:T(4,128)S(1)} %copy.71) | copy-start | bytes 12292
  13.9 1.3 copy-start.6
  75.0 2.2 copy-start.13
  77.2 1.7 copy-start.15
  78.9 6.8 %copy-start.1 = (bf16[768,1280]{1,0:T(8,128)(2,1)}, bf16[768,1280]{1,0:T(8,128)(2,1)S(1)}, u32[]{:S(2)}) copy-start(bf16[768,1280]{1,0:T(8,128)(2,1)S(1)} %get-tuple-element.43.own_ref) | copy-start | bytes 5898244
  87.8 1.3 copy-start.7
  138.0 1.3 copy-start.16
  139.3 1.0 copy-start.17
  140.3 3.4 copy-start.10
  140.3 3.4 copy-start.27
  140.3 3.4 copy-start.29
  143.7 3.9 copy-start.18
  245.7 1.5 copy-start.2
  245.7 4.0 copy-start.22
  245.8 4.0 copy-start.26
  245.8 230.9 %reduce-scatter.3.cloned.1.call-start = ((), (), s32[]{:S(2)}) async-start(), calls=%async_computation.3 | async-start | bytes 5898240 | tf_op jit(solution)/shard_map/reduce_scatter | solution.py:959
  250.7 5.4 %copy-start.5 = (bf16[2,512,768]{2,1,0:T(8,128)(2,1)S(1)}, bf16[2,512,768]{2,1,0:T(8,128)(2,1)}, u32[]{:S(2)}) copy-start(bf16[2,512,768]{2,1,0:T(8,128)(2,1)} %param.31) | copy-start | bytes 4718596
  250.8 5.4 %copy-start.8 = (bf16[768,768]{1,0:T(8,128)(2,1)S(1)}, bf16[768,768]{1,0:T(8,128)(2,1)}, u32[]{:S(2)}) copy-start(bf16[768,768]{1,0:T(8,128)(2,1)} %all-gather.2.cloned.1.call-done.out_w_ref) | copy-start | bytes 3538948
  250.8 5.4 %copy-start.14 = (f32[768,128]{1,0:T(8,128)S(1)}, f32[768,128]{1,0:T(8,128)}, u32[]{:S(2)}) copy-start(f32[768,128]{1,0:T(8,128)} %get-tuple-element.52.router_ref) | copy-start | bytes 1179652
  251.6 18.7 %copy-start.23 = (f32[2,768]{1,0:T(2,128)}, f32[2,768]{1,0:T(2,128)S(1)}, u32[]{:S(2)}) copy-start(f32[2,768]{1,0:T(2,128)S(1)} %convert_bitcast_fusion.gains_ref) | copy-start | bytes 18436
  255.3 15.1 %copy-start.3 = (s32[1024,1]{1,0:T(8,128)}, s32[1024,1]{1,0:T(8,128)S(1)}, u32[]{:S(2)}) copy-start(s32[1024,1]{1,0:T(8,128)S(1)} %fusion.9.pos_ref) | copy-start | bytes 12292
  256.2 1.9 copy-start.9
  258.1 1.7 copy-start.11
  270.4 1.7 copy-start
  272.1 1.7 copy-start.12
  443.1 28.6 %copy-start.19 = (bf16[24,768]{1,0:T(8,128)(2,1)S(1)}, bf16[24,768]{1,0:T(8,128)(2,1)}, u32[]{:S(2)}) copy-start(bf16[24,768]{1,0:T(8,128)(2,1)} %param.20) | copy-start | bytes 110596
  443.1 28.6 %copy-start.20 = (bf16[24,768]{1,0:T(8,128)(2,1)S(1)}, bf16[24,768]{1,0:T(8,128)(2,1)}, u32[]{:S(2)}) copy-start(bf16[24,768]{1,0:T(8,128)(2,1)} %param.19) | copy-start | bytes 110596
  443.1 28.6 %copy-start.21 = (bf16[24,768]{1,0:T(8,128)(2,1)S(1)}, bf16[24,768]{1,0:T(8,128)(2,1)}, u32[]{:S(2)}) copy-start(bf16[24,768]{1,0:T(8,128)(2,1)} %param.18) | copy-start | bytes 110596
  443.1 30.1 %copy-start.30 = (bf16[24]{0:T(256)(128)(2,1)S(1)}, bf16[24]{0:T(256)(128)(2,1)}, u32[]{:S(2)}) copy-start(bf16[24]{0:T(256)(128)(2,1)} %param.23) | copy-start | bytes 148
  (2 other events, 1.9 us)
Sparse Core Ops, SparseCore 0:
  10.9 61.3 all-gather.1
  245.9 58.2 reduce-scatter.4
  306.8 111.0 reduce-scatter.2

commit v4 on v3

--- a/solution.py
+++ b/solution.py
@@ -112,7 +112,7 @@
     dma=lambda n: pltpu.SemaphoreType.DMA((n,))
     return [dma(seq_count+groups-2),dma(max((seq_count-1)*(groups-1),1)),dma(seq_count*groups),pltpu.SemaphoreType.DMA]
 
-def start_kernel(plan,rows,span,token_ref,unit_ref,w1_ref,proj_ref,normed_ref,own_out,w1_out,
+def start_kernel(plan,rows,span,token_ref,unit_ref,w1_ref,pos_ref,cot_ref,proj_ref,normed_ref,cot_rows_ref,own_out,w1_out,
                  tok,scaled,units,land,s_unit,r_unit,s_block,r_block,s_pass,own_sem,*spread_sems):
     experts,seq_devs,seq_count,stretch,heads,chunks=plan
     groups=seq_devs//seq_count
@@ -167,6 +167,12 @@
     for j,copy in zip(visit,passes):
         landed(block_of(device(j,side)),r_block.at[device(j,side)])
         copy.start()
+    cap=cot_rows_ref.shape[1]
+    def place_rows(expert):
+        slots=lax.broadcasted_iota(jnp.int32,(cap,pos_ref.shape[1]),0)+expert*cap
+        hot=(slots==pos_ref[...]).astype(f32).astype(b16)
+        cot_rows_ref[expert]=jnp.dot(hot,cot_ref[...],preferred_element_type=f32).astype(b16)
+    loop(0,experts,place_rows)
     piece=512 if length%512==0 else 128
     tokens.relay()
     tokens.finish()
@@ -194,7 +200,7 @@
     for i in range(1,seq_devs):
         send_unit(i).wait_send()
 
-def gather_start(plan,rows,tokens,units,expert_in):
+def gather_start(plan,rows,tokens,units,expert_in,position,cotangent,cap):
     experts,seq_devs,seq_count,stretch,heads,chunks=plan
     groups=seq_devs//seq_count
     length=stretch*seq_devs
@@ -207,20 +213,33 @@
     shape=lambda *dims: jax.ShapeDtypeStruct(dims,b16)
     return pl.pallas_call(
         functools.partial(start_kernel,plan,rows,span),
-        in_specs=[anywhere,anywhere,vmem],
-        out_specs=[vmem,vmem,anywhere,anywhere],
-        out_shape=[shape(length,span),shape(length,width),shape(width,span+128),shape(width,expert_in.shape[2]*seq_devs)],
+        in_specs=[anywhere,anywhere,vmem,vmem,vmem],
+        out_specs=[vmem,vmem,vmem,anywhere,anywhere],
+        out_shape=[shape(length,span),shape(length,width),shape(experts,cap,width),shape(width,span+128),shape(width,expert_in.shape[2]*seq_devs)],
         scratch_shapes=[pltpu.VMEM((length,width),b16),pltpu.VMEM((length,width),jnp.float32),pltpu.VMEM((seq_devs,)+units.shape[1:],b16),pltpu.VMEM((width,span+128),b16),
             dma(seq_devs),dma(seq_devs),dma(experts),dma(experts),dma(experts),dma(3)]+spread_semaphores(seq_count,groups)*2,
         compiler_params=pltpu.CompilerParams(collective_id=3,has_side_effects=True,vmem_limit_bytes=40*MIB),
         cost_estimate=pl.CostEstimate(flops=2*length*width*span,bytes_accessed=24*MIB,transcendentals=0),
         name="gather_start",
-    )(tokens,units,expert_in)
+    )(tokens,units,expert_in,position,cotangent)
+
+def one_hot_rows(ids):
+    return (lax.broadcasted_iota(jnp.int32,(128,ids.shape[1]),0)==ids).astype(jnp.float32).astype(jnp.bfloat16)
+
+def stack_parts(values):
+    return jnp.concatenate(three_parts(values),axis=0).astype(jnp.bfloat16)
+
+def join_parts(product):
+    rows=product.shape[0]//3
+    return product[:rows]+product[rows:2*rows]+product[2*rows:]
+
+def table_rows(table,hot):
+    return join_parts(jnp.dot(stack_parts(table),hot,preferred_element_type=jnp.float32))
 
 def chunk_span(heads):
     return 128*(1+heads)
 
-def forward_kernel(plan,block,srows,scale,proj_ref,bias_ref,cot_ref,own_ref,w2_ref,att_out,o32_ref,lse_ref,cot_out,all_out,w2_out,strip,kd,va,scr,outs,s_cot,r_cot,s_att,r_att,s_all,r_all,local_sem,*spread_sems):
+def forward_kernel(plan,block,srows,scale,proj_ref,ids_ref,rows_ref,cot_ref,own_ref,w2_ref,att_out,o32_ref,lse_ref,cot_out,all_out,w2_out,strip,bias_ref,kd,va,scr,outs,s_cot,r_cot,s_att,r_att,s_all,r_all,local_sem,*spread_sems):
     experts,seq_devs,seq_count,stretch,heads,chunks=plan
     length=stretch*seq_devs
     groups=seq_devs//seq_count
@@ -261,6 +280,7 @@
     lanes=lane_iota(length)
     block_lanes=lane_iota(block)
     lse_ref[...]=jnp.zeros_like(lse_ref)
+    bias_ref[...]=table_rows(rows_ref[...],one_hot_rows(ids_ref[...]))
     def attend_head(c,head):
         index=c*heads+head
         def columns(which):
@@ -354,7 +374,7 @@
     own_cot.wait()
     seconds.finish()
 
-def attend(plan,projected,bias_vec,cot_rows,own_weight,expert_out,block=512,srows=128):
+def attend(plan,projected,ids,table,cot_rows,own_weight,expert_out,block=512,srows=128):
     experts,seq_devs,seq_count,stretch,heads,chunks=plan
     length=stretch*seq_devs
     groups=seq_devs//seq_count
@@ -364,20 +384,20 @@
     dma=lambda *shape: pltpu.SemaphoreType.DMA(shape)
     return pl.pallas_call(
         functools.partial(forward_kernel,plan,block,srows,LOG2E/8),
-        in_specs=[vmem,vmem,anywhere,vmem,vmem],
+        in_specs=[vmem,vmem,vmem,anywhere,vmem,vmem],
         out_specs=[anywhere,vmem,vmem]+[anywhere]*3,
         out_shape=[jax.ShapeDtypeStruct((seq_count,stretch,groups*chunks*128),b16),jax.ShapeDtypeStruct((length,chunks*128),f32),jax.ShapeDtypeStruct((length,128),f32),jax.ShapeDtypeStruct(cot_rows.shape,b16),jax.ShapeDtypeStruct((groups,)+own_weight.shape,b16),jax.ShapeDtypeStruct((expert_out.shape[1]*seq_devs,expert_out.shape[2]),b16)],
-        scratch_shapes=[pltpu.VMEM((srows,2*length-srows),f32),pltpu.VMEM((length,128),b16),pltpu.VMEM((length,128),b16),pltpu.VMEM((2,block,length),f32),pltpu.VMEM((chunks,length,128),b16),
+        scratch_shapes=[pltpu.VMEM((srows,2*length-srows),f32),pltpu.VMEM((table.shape[0],2*length),f32),pltpu.VMEM((length,128),b16),pltpu.VMEM((length,128),b16),pltpu.VMEM((2,block,length),f32),pltpu.VMEM((chunks,length,128),b16),
             dma(experts),dma(experts),dma(chunks,seq_devs),dma(chunks,seq_devs),dma(groups),dma(groups),dma(2+chunks)]+spread_semaphores(seq_count,groups),
         compiler_params=pltpu.CompilerParams(collective_id=1,has_side_effects=True,vmem_limit_bytes=48*MIB),
         cost_estimate=pl.CostEstimate(flops=16*heads*chunks*length*length*64,bytes_accessed=16*MIB,transcendentals=heads*chunks*length*length),
         name="attend_forward",
-    )(projected,bias_vec,cot_rows,own_weight,expert_out)
-
-def backward_kernel(plan,inside,bq,bk,srows,scale,proj_ref,o32_ref,lse_ref,bias_ref,normed_ref,bucket_ref,up_ref,res_ref,piece_ref,
+    )(projected,ids,table,cot_rows,own_weight,expert_out)
+
+def backward_kernel(plan,inside,bq,bk,srows,scale,proj_ref,o32_ref,lse_ref,ids_ref,rows_ref,normed_ref,up_ref,res_ref,piece_ref,
                     grad_out,ret_out,piece_out,weight_out,table_out,
-                    strip,grads,ka,va,kt,qa,da,dd,qd,dk_acc,dv_acc,ups,outs,weight_parts,diag,table,normed_t,
-                    s_up,r_up,s_res,r_res,s_piece,r_piece,s_grad,r_grad,s_weight,r_weight,s_table,r_table,local_sem,own_sem):
+                    strip,grads,kk,kt,qa,da,qd,dkv_acc,lse_t,delta,ups,outs,weight_parts,piece_parts,piece_land,diag,table,normed_t,hot,bias_ref,
+                    s_up,r_up,s_res,r_res,s_piece,r_piece,s_grad,r_grad,s_weight,r_weight,s_half,r_half,s_table,r_table,local_sem,own_sem):
     experts,seq_devs,seq_count,stretch,heads,chunks=plan
     length=stretch*seq_devs
     groups=seq_devs//seq_count
@@ -403,9 +423,31 @@
     def send_res(i):
         target=lax.rem(me+i,experts)
         return remote(res_ref.at[target],ret_out.at[me],s_res.at[i],r_res.at[i],(target,place))
+    half=experts*seq_count
+    spot=me*seq_count+sequence
+    def fellow(i):
+        target=lax.rem(spot+i,half)
+        return target,(target//seq_count,(target%seq_count)*groups+group)
+    def half_piece(i):
+        target=lax.rem(group+i,groups)
+        return remote(piece_ref.at[target],piece_land.at[i-1],s_half.at[i],r_half.at[i],(me,sequence*groups+target))
+    own_piece=pltpu.make_async_copy(piece_ref.at[group],piece_parts,own_sem.at[2])
     def send_piece(i):
-        target,where=other(i)
-        return remote(piece_ref.at[target],piece_out.at[rank],s_piece.at[i],r_piece.at[i],where)
+        target,where=fellow(i)
+        return remote(piece_parts.at[target],piece_out.at[spot],s_piece.at[i],r_piece.at[i],where)
+    keep_piece=pltpu.make_async_copy(piece_parts.at[spot],piece_out.at[spot],own_sem.at[4])
+    def meet_pieces():
+        own_piece.wait()
+        for j in range(1,groups):
+            landed(piece_land.at[j-1],r_half.at[j])
+        def add(i):
+            total=piece_parts[i].astype(f32)
+            for j in range(1,groups):
+                total=total+piece_land[j-1,i].astype(f32)
+            piece_parts[i]=total.astype(b16)
+        loop(0,half,add)
+        loop(1,half,lambda i: send_piece(i).start())
+        keep_piece.start()
     def grad_lanes(owner_group,c,part):
         return pl.ds(pl.multiple_of((owner_group*chunks+c)*chunk_span(heads)+part*128,128),128)
     def send_grad(c,part,i):
@@ -422,7 +464,6 @@
         return remote(table,table_out.at[rank],s_table.at[i],r_table.at[i],other(i)[1])
     own_table=pltpu.make_async_copy(table,table_out.at[rank],own_sem.at[0])
     own_res=pltpu.make_async_copy(res_ref.at[me],ret_out.at[me],own_sem.at[1])
-    own_piece=pltpu.make_async_copy(piece_ref.at[rank],piece_out.at[rank],own_sem.at[2])
     def landed(landing,received):
         remote(landing,landing,own_sem.at[3],received,(me,place)).wait_recv()
     own_res.start()
@@ -438,50 +479,58 @@
         weight_parts[...]=jnp.zeros_like(weight_parts)
         normed_t[...]=jnp.transpose(normed_ref[...])
     diag[...]=jnp.zeros_like(diag)
+    lse_t[...]=jnp.transpose(lse_ref[...])
+    hot[...]=one_hot_rows(ids_ref[...])
+    bias_ref[...]=table_rows(rows_ref[...],hot[...])
     def head_back(c,head):
         index=c*heads+head
         def columns(which):
-            return slice(c*chunk_span(heads)+which*128,c*chunk_span(heads)+(which+1)*128)
+            return pl.ds(pl.multiple_of(c*chunk_span(heads)+which*128,128),128)
         query,both=proj_ref[:,columns(0)],proj_ref[:,columns(1+head)]
-        fill_strip(strip,bias_ref[index:index+1,:],srows,width)
+        fill_strip(strip,bias_ref[pl.ds(index,1),:],srows,width)
         grads[...]=jnp.zeros_like(grads)
-        kd=dup_head(both,0)
-        ka[:,:128]=kd.astype(b16)
-        ka[:,128:]=jnp.where(lanes<3,1.0,0.0).astype(b16)
-        kt[...]=jnp.transpose(kd).astype(b16)
-        va[...]=jnp.where(lanes<64,dup_head(both,1),jnp.where(lanes<67,1.0,0.0)).astype(b16)
-        qa[:,:128]=split_query(query,head,scale)
-        qa[:,128:]=columns_at(lanes,0,three_parts(-head_column(lse_ref[...],index)),0.0).astype(b16)
-        qd[...]=dup_head(query,head).astype(b16)
+        low_lanes=lanes<64
+        kk[:,:128]=both
+        kk[:,128:]=both
+        kt[...]=jnp.transpose(both)
+        query=query.astype(f32)
+        query=jnp.where(low_lanes,pltpu.roll(query,64,1) if head else query,0.0)
+        scaled=query*scale
+        high=scaled.astype(b16).astype(f32)
+        qa[:,:128]=high.astype(b16)
+        qa[:,128:]=(scaled-high).astype(b16)
+        qd[...]=(query*0.125).astype(b16)
         if head==0:
             take_up(c)
-        upstream=dup_head(ups[c],head)
-        dd[...]=upstream.astype(b16)
-        delta=0.5*jnp.sum(upstream*dup_head(o32_ref[:,c*128:(c+1)*128],head),axis=1,keepdims=True)
-        da[...]=columns_at(lanes,64,three_parts(-delta),jnp.where(lanes<64,upstream,0.0)).astype(b16)
-        dk_acc[...]=jnp.zeros_like(dk_acc)
-        dv_acc[...]=jnp.zeros_like(dv_acc)
+            products_sum=ups[c].astype(f32)*o32_ref[:,pl.ds(pl.multiple_of(c*128,128),128)]
+            halves=lax.broadcasted_iota(jnp.int32,(8,128),0)==lax.broadcasted_iota(jnp.int32,(8,128),1)//64
+            halves=halves.astype(f32).astype(b16)
+            delta[...]=sum(lax.dot_general(halves,part.astype(b16),NT,preferred_element_type=f32) for part in three_parts(products_sum))
+        upstream=ups[c].astype(f32)
+        da[...]=jnp.where(low_lanes,0.0,upstream if head else pltpu.roll(upstream,64,1)).astype(b16)
+        dkv_acc[...]=jnp.zeros_like(dkv_acc)
         def query_block(qb):
             qs=pl.ds(pl.multiple_of(qb*bq,bq),bq)
             def products(kb):
                 ks=slice(kb*bk,(kb+1)*bk)
-                raw=lax.dot_general(ka[ks,:],qa[qs,:],NT,preferred_element_type=f32)
-                up=lax.dot_general(va[ks,:],da[qs,:],NT,preferred_element_type=f32)
+                raw=lax.dot_general(kk[ks,:],qa[qs,:],NT,preferred_element_type=f32)
+                up=lax.dot_general(kk[ks,:128],da[qs,:],NT,preferred_element_type=f32)
                 return raw,up
+            log_row=lse_t[pl.ds(index,1),qs]
+            delta_row=delta[head:head+1,qs]
             def consume(kb,raw,up,dq):
                 ks=slice(kb*bk,(kb+1)*bk)
                 probs,score_grads=[],[]
                 for part in range(bk//srows):
                     start=qb*bq+(length-srows)-kb*bk-part*srows
                     rows=slice(part*srows,(part+1)*srows)
-                    prob=jnp.exp2(raw[rows]+strip[:,pl.ds(pl.multiple_of(start,128),bq)])
-                    grad=prob*up[rows]
+                    prob=jnp.exp2(raw[rows]+strip[:,pl.ds(pl.multiple_of(start,128),bq)]-log_row)
+                    grad=prob*(up[rows]-delta_row)
                     grads[:,pl.ds(pl.multiple_of(start+srows,128),bq)]+=grad
                     probs.append(prob.astype(b16))
                     score_grads.append(grad.astype(b16))
                 low=jnp.concatenate(score_grads,axis=0)
-                dv_acc[ks,:]+=jnp.dot(jnp.concatenate(probs,axis=0),dd[qs,:],preferred_element_type=f32)
-                dk_acc[ks,:]+=jnp.dot(low,qd[qs,:],preferred_element_type=f32)
+                dkv_acc[ks,:]+=jnp.dot(jnp.concatenate(probs,axis=0),da[qs,:],preferred_element_type=f32)+jnp.dot(low,qd[qs,:],preferred_element_type=f32)
                 return dq+jnp.dot(kt[:,ks],low,preferred_element_type=f32)
             dq=jnp.zeros((128,bq),f32)
             ready=products(0)
@@ -491,7 +540,7 @@
                 ready=following
             dq=jnp.transpose(dq)*0.125
             if head:
-                dq=jnp.where(lane_iota(bq)<64,outs[c,qs,0:128].astype(f32),dq)
+                dq=jnp.where(lane_iota(bq)<64,outs[c,qs,0:128].astype(f32),pltpu.roll(dq,64,1))
             outs[c,qs,0:128]=dq.astype(b16)
             if head==heads-1:
                 for part in range(bq//stretch):
@@ -503,7 +552,7 @@
                     def _():
                         send_grad(c,0,distance).start()
         loop(0,length//bq,query_block)
-        outs[c,:,128*(1+head):128*(2+head)]=jnp.where(lanes<64,dk_acc[...]*0.125,dv_acc[...]).astype(b16)
+        outs[c,:,128*(1+head):128*(2+head)]=dkv_acc[...].astype(b16)
         loop(1,seq_devs,lambda i: send_grad(c,1+head,i).start())
         own_grad(c,1+head).start()
         total=grads[0:8,:]
@@ -512,26 +561,30 @@
         row=lax.broadcasted_iota(jnp.int32,(8,full_width),0)
         for part in range(1,8):
             total=jnp.where(row==part,pltpu.roll(total,full_width-part,1),total)
-        diag[index:index+1,:]=jnp.sum(total,axis=0,keepdims=True)
+        diag[pl.ds(index,1),:]=jnp.sum(total,axis=0,keepdims=True)
     def take_up(c):
         loop(1,seq_devs,lambda i: landed(ups.at[c,rows_of(lax.rem(place-i+seq_devs,seq_devs))],r_up.at[c,i]))
         own_up(c).wait()
-        if c==0:
+        @pl.when(c==0)
+        def _():
             loop(1,chunks,lambda later: loop(1,seq_devs,lambda i: send_up(later,i).start()))
+            loop(1,groups,lambda i: half_piece(i).start())
             loop(1,experts,lambda i: send_res(i).start())
-            loop(1,devices,lambda i: send_piece(i).start())
     def one_chunk(c):
         for head in range(heads):
             head_back(c,head)
+            if head==0:
+                @pl.when(c==0)
+                def _():
+                    meet_pieces()
         if inside:
             part=jnp.dot(normed_t[...],outs[c],preferred_element_type=f32)
             block=normed_t.shape[0]//devices
             weight_parts[c,:,:block,:]=part.reshape(devices,block,chunk_span(heads)).astype(b16)
             loop(1,devices,lambda i: send_weight(c,i).start())
             own_weight(c).start()
-    for c in range(chunks):
-        one_chunk(c)
-    table[...]=lax.dot_general(bucket_ref[...],diag[...],NT,precision=lax.Precision.HIGHEST,preferred_element_type=f32)
+    loop(0,chunks,one_chunk)
+    table[...]=join_parts(lax.dot_general(stack_parts(diag[...]),hot[...],NT,preferred_element_type=f32))
     loop(1,devices,lambda i: send_table(i).start())
     own_table.start()
     def finish_chunk(c):
@@ -556,17 +609,19 @@
         send_res(i).wait_send()
     loop(1,experts,res_landed)
     def piece_landed(i):
-        source=lax.rem(rank-i+devices,devices)
-        landed(piece_out.at[source],r_piece.at[i])
+        landed(piece_out.at[lax.rem(spot-i+half,half)],r_piece.at[i])
         send_piece(i).wait_send()
-        landed(table_out.at[source],r_table.at[i])
+    loop(1,half,piece_landed)
+    def table_landed(i):
+        landed(table_out.at[lax.rem(rank-i+devices,devices)],r_table.at[i])
         send_table(i).wait_send()
-    loop(1,devices,piece_landed)
+    loop(1,devices,table_landed)
     own_res.wait()
-    own_piece.wait()
+    loop(1,groups,lambda i: half_piece(i).wait_send())
+    keep_piece.wait()
     own_table.wait()
 
-def attend_back(plan,projected,o32,lse,bias_vec,normed,buckets,upstream,result,piece,bq=512,bk=512,srows=128):
+def attend_back(plan,projected,o32,lse,ids,table,normed,upstream,result,piece,bq=512,bk=512,srows=128):
     experts,seq_devs,seq_count,stretch,heads,chunks=plan
     length=stretch*seq_devs
     groups=seq_devs//seq_count
@@ -585,19 +640,17 @@
         functools.partial(backward_kernel,plan,inside,bq,bk,srows,LOG2E/8),
         in_specs=[vmem]*6+[anywhere]*3,
         out_specs=[anywhere]*5,
-        out_shape=[shape(b16,seq_count,stretch,groups*chunks*chunk_span(heads)),shape(b16,*result.shape),shape(b16,*piece.shape),shape(b16,*weight_shape),shape(f32,devices,buckets.shape[0],diag_rows(plan))],
-        scratch_shapes=[vm(f32,srows,2*length-srows),vm(f32,srows,2*length),vm(b16,length,256),vm(b16,length,128),vm(b16,128,length),
-            vm(b16,length,256),vm(b16,length,128),vm(b16,length,128),vm(b16,length,128),vm(f32,length,128),vm(f32,length,128),
-            vm(b16,chunks,length,128),vm(b16,chunks,length,chunk_span(heads)),vm(b16,*weight_shape),vm(f32,diag_rows(plan),2*length),vm(f32,buckets.shape[0],diag_rows(plan)),vm(b16,normed.shape[1],length),
-            dma(chunks,seq_devs),dma(chunks,seq_devs),dma(experts),dma(experts),dma(devices),dma(devices),dma(chunks,1+heads,seq_devs),dma(chunks,1+heads,seq_devs),
-            dma(chunks,devices),dma(chunks,devices),dma(devices),dma(devices),dma(3+heads,chunks),dma(4)],
+        out_shape=[shape(b16,seq_count,stretch,groups*chunks*chunk_span(heads)),shape(b16,*result.shape),shape(b16,*piece.shape[1:]),shape(b16,*weight_shape),shape(f32,devices,table.shape[0],128)],
+        scratch_shapes=[vm(f32,srows,2*length-srows),vm(f32,srows,2*length),vm(b16,length,256),vm(b16,128,length),vm(b16,length,256),vm(b16,length,128),
+            vm(b16,length,128),vm(f32,length,128),vm(f32,128,length),vm(f32,8,length),
+            vm(b16,chunks,length,128),vm(b16,chunks,length,chunk_span(heads)),vm(b16,*weight_shape),vm(b16,*piece.shape[1:]),vm(b16,max(groups-1,1),*piece.shape[1:]),vm(f32,table.shape[0],2*length),vm(f32,table.shape[0],128),vm(b16,normed.shape[1],length),vm(b16,128,2*length),vm(f32,table.shape[0],2*length),
+            dma(chunks,seq_devs),dma(chunks,seq_devs),dma(experts),dma(experts),dma(experts*seq_count),dma(experts*seq_count),dma(chunks,1+heads,seq_devs),dma(chunks,1+heads,seq_devs),
+            dma(chunks,devices),dma(chunks,devices),dma(groups),dma(groups),dma(devices),dma(devices),dma(3+heads,chunks),dma(5)],
         compiler_params=pltpu.CompilerParams(collective_id=2,has_side_effects=True,vmem_limit_bytes=58*MIB),
         cost_estimate=pl.CostEstimate(flops=40*heads*chunks*length*length*64,bytes_accessed=24*MIB,transcendentals=heads*chunks*length*length),
         name="attend_backward",
-    )(projected,o32,lse,bias_vec,normed,buckets,upstream,result,piece)
-
-def diag_rows(plan):
-    return 128
+    )(projected,o32,lse,ids,table,normed,upstream,result,piece)
+
 
 def combine_kernel(experts,pos_ref,home_ref,hidden_ref,cot_ref,att_ref,out_w_ref,gain_ref,router_ref,grad_ref,heads_ref,part_ref,total,gain_total):
     f32,b16=jnp.float32,jnp.bfloat16
@@ -652,11 +705,14 @@
         name="combine",
     )(position,home,hidden,cotangent,attended,out_full,gain,router_part)
 
-def finish_kernel(experts,groups,heads,chunks,inside,pos_ref,pick_ref,returned_ref,hidden_ref,grad_ref,token_ref,token_grad_ref,every_ref,gains_ref,router_ref,piece_ref,weight_ref,table_ref,
-                  output_ref,input_ref,piece_sum,query_sum,key_sum,value_sum,table_sum):
+def finish_kernel(experts,groups,heads,chunks,inside,pos_ref,pick_ref,returned_ref,hidden_ref,grad_ref,token_ref,token_grad_ref,every_ref,gains_ref,router_ref,piece_ref,weight_ref,table_ref,first_ref,second_ref,own_ref,own_gain_ref,
+                  output_ref,input_ref,first_out,second_out,out_sum,small_sum,query_sum,key_sum,value_sum,gain_sum,table_sum):
     f32,b16=jnp.float32,jnp.bfloat16
     step=pl.program_id(0)
     rows,width=hidden_ref.shape
+    row_block=out_sum.shape[0]
+    first_out[...]=first_ref[...].astype(f32)
+    second_out[...]=second_ref[...].astype(f32)
     slots=returned_ref.shape[0]
     cw=chunk_span(heads)
     span=chunks*cw
@@ -681,16 +737,18 @@
         devices=piece_ref.shape[0]
         def add_piece(i,total):
             return total+piece_ref[i].astype(f32)
-        piece_sum[...]=lax.fori_loop(1,devices,add_piece,piece_ref[0].astype(f32))
+        total=lax.fori_loop(1,devices,add_piece,piece_ref[0].astype(f32))[:row_block]
+        out_sum[...]=total[:,:width]
+        small_sum[...]=total[:,width:]
         for owner in range(groups):
             def add_table(i,total):
                 return total+table_ref[i*groups+owner]
-            table_sum[owner]=lax.fori_loop(1,devices//groups,add_table,table_ref[owner])
+            table_sum[owner]=lax.fori_loop(1,table_ref.shape[0]//groups,add_table,table_ref[owner])
             if inside:
                 for c in range(chunks):
                     def add_weight(i,total):
                         return total+weight_ref[c,i*groups+owner].astype(f32)
-                    summed=lax.fori_loop(1,devices//groups,add_weight,weight_ref[c,owner].astype(f32))
+                    summed=lax.fori_loop(1,weight_ref.shape[1]//groups,add_weight,weight_ref[c,owner].astype(f32))[:row_block]
                     place=slice((owner*chunks+c)*128,(owner*chunks+c+1)*128)
                     query_sum[:,place]=summed[:,0:128]
                     first=summed[:,128:256]
@@ -698,27 +756,34 @@
                     low=lane_iota(summed.shape[0])<64
                     key_sum[:,place]=jnp.where(low,first,pltpu.roll(second,64,1))
                     value_sum[:,place]=jnp.where(low,pltpu.roll(first,64,1),second)
-
-def finish(experts,groups,heads,chunks,inside,position,pick,returned,hidden,hidden_grad,tokens,token_grads,every_weight,gains,router,pieces,weights,tables,block=256):
+        if inside:
+            products=query_sum[...]*own_ref[0].astype(f32)+key_sum[...]*own_ref[1].astype(f32)+value_sum[...]*own_ref[2].astype(f32)
+            gain_sum[...]=jnp.broadcast_to(jnp.sum(products,axis=1,keepdims=True),gain_sum.shape)/own_gain_ref[...]
+
+def finish(experts,groups,heads,chunks,inside,position,pick,returned,hidden,hidden_grad,tokens,token_grads,every_weight,gains,router,pieces,weights,tables,first,second,own_weights,own_gain,block=256):
     count,width=hidden.shape
     f32,b16=jnp.float32,jnp.bfloat16
     block=min(block,count)
     by_rows=lambda columns: pl.BlockSpec((block,columns),lambda i:(i,0))
     def whole(shape):
         return pl.BlockSpec(shape,lambda i:(0,)*len(shape))
-    sums=jax.ShapeDtypeStruct((pieces.shape[1],groups*chunks*128),f32)
+    row_block=own_gain.shape[0]
+    sums=jax.ShapeDtypeStruct((row_block,width),f32)
+    steps=count//block
+    by_steps=lambda value: pl.BlockSpec((value.shape[0]//steps,value.shape[1]),lambda i:(i,0))
+    wide=lambda value: jax.ShapeDtypeStruct(value.shape,f32)
+    small_shape=jax.ShapeDtypeStruct((row_block,128),f32)
     table_shape=jax.ShapeDtypeStruct((groups,)+tables.shape[1:],f32)
-    piece_shape=jax.ShapeDtypeStruct(pieces.shape[1:],f32)
     return pl.pallas_call(
         functools.partial(finish_kernel,experts,groups,heads,chunks,inside),
         grid=(count//block,),
-        in_specs=[by_rows(1),by_rows(1),whole(returned.shape),by_rows(width),by_rows(width),by_rows(width),by_rows(token_grads.shape[1]),whole(every_weight.shape),whole(gains.shape),whole(router.shape),whole(pieces.shape),whole(weights.shape),whole(tables.shape)],
-        out_specs=[by_rows(width),by_rows(width),whole(piece_shape.shape)]+[whole(sums.shape)]*3+[whole(table_shape.shape)],
-        out_shape=[jax.ShapeDtypeStruct((count,width),b16),jax.ShapeDtypeStruct((count,width),f32),piece_shape,sums,sums,sums,table_shape],
+        in_specs=[by_rows(1),by_rows(1),whole(returned.shape),by_rows(width),by_rows(width),by_rows(width),by_rows(token_grads.shape[1]),whole(every_weight.shape),whole(gains.shape),whole(router.shape),whole(pieces.shape),whole(weights.shape),whole(tables.shape),by_steps(first),by_steps(second),whole(own_weights.shape),whole(own_gain.shape)],
+        out_specs=[by_rows(width),by_rows(width),by_steps(first),by_steps(second),whole(sums.shape),whole(small_shape.shape)]+[whole(sums.shape)]*3+[whole(small_shape.shape),whole(table_shape.shape)],
+        out_shape=[jax.ShapeDtypeStruct((count,width),b16),jax.ShapeDtypeStruct((count,width),f32),wide(first),wide(second),sums,small_shape,sums,sums,sums,small_shape,table_shape],
         compiler_params=pltpu.CompilerParams(vmem_limit_bytes=56*MIB),
         cost_estimate=pl.CostEstimate(flops=8*count*width*width,bytes_accessed=24*MIB,transcendentals=0),
         name="finish",
-    )(position,pick,returned,hidden,hidden_grad,tokens,token_grads,every_weight,gains,router,pieces,weights,tables)
+    )(position,pick,returned,hidden,hidden_grad,tokens,token_grads,every_weight,gains,router,pieces,weights,tables,first,second,own_weights,own_gain)
 
 def gelu_pair(u):
     c=0.7978845608028654
@@ -883,10 +948,6 @@
     grid=matmul(grid,jnp.asarray(flip,jnp.bfloat16)).astype(jnp.bfloat16)
     return matmul(jnp.asarray(flip_rows,jnp.bfloat16),grid).reshape(-1).astype(jnp.int32)
 
-def offset_rows(ids,table):
-    hot=(ids[None,:]==jnp.arange(table.shape[0],dtype=jnp.int32)[:,None]).astype(jnp.float32)
-    return lax.dot_general(table,hot,TN,precision=lax.Precision.HIGHEST)
-
 def shards(tokens,query_weight,key_weight,value_weight,out_weight,router_weight,attn_gain,moe_gain,bias_table,expert_in,expert_out,expert_id,slot_id,bucket_id,cotangent):
     f32,b16=jnp.float32,jnp.bfloat16
     seq_count,stretch,width=tokens.shape
@@ -917,12 +978,17 @@
     gains=jnp.stack([attn_gain,moe_gain],axis=1)
     small=jnp.pad(jnp.concatenate([router_weight,gains],axis=1),((0,0),(0,126-experts)))
     units=jnp.concatenate([stacked,jnp.broadcast_to(small[:,None],(row_block,groups,128))],axis=2)
+    expert_pick=expert_id.reshape(count)
+    slot_pick=slot_id.reshape(count)
+    slots=experts*padded_cap
+    position=jnp.where(slot_pick<capacity,expert_pick*padded_cap+slot_pick,slots)
+    hot=(position[None,:]==jnp.arange(slots,dtype=jnp.int32)[:,None]).astype(b16)
     out_full=lax.all_gather(out_weight,BOTH,axis=0,tiled=True)
     out_full=jnp.pad(out_full.reshape(groups*chunks,used,width),((0,0),(0,128-used),(0,0))).reshape(heads_width,width)
     plan=(experts,seq_devs,seq_count,stretch,per_chunk,chunks)
     if row_block%8==0 and row_block*seq_devs%16==0:
         units=jnp.pad(jnp.swapaxes(units,0,1),((0,0),(0,-row_block%16),(0,0)))
-        projected,normed,own_weight,first_full=gather_start(plan,row_block,tokens,units,expert_in)
+        projected,normed,cot_rows,own_weight,first_full=gather_start(plan,row_block,tokens,units,expert_in,position[None,:],cotangent.reshape(count,width),padded_cap)
     else:
         copies=jnp.broadcast_to(tokens[:,None],(seq_count,groups,stretch,width)).reshape(seq_devs,stretch,width)
         own_sequence=swap_parts(copies,"seq").reshape(length,width).astype(f32)
@@ -931,24 +997,18 @@
         normed=(own_sequence*inverse_rms(own_sequence)*own_weight[:,span+experts].astype(f32)).astype(b16)
         projected=matmul(normed,own_weight[:,:span]).astype(b16)
         first_full=lax.all_gather(expert_in[0],"seq",axis=1,tiled=True)
+        cot_rows=matmul(hot,cotangent.reshape(count,width)).astype(b16).reshape(experts,padded_cap,width)
     small_full=own_weight[:,span:]
     router_full=small_full[:,:experts]
     router_wide=jnp.where(jnp.arange(128)[None,:]<experts,small_full,jnp.zeros((),b16))
     attn_gain_full=small_full[:,experts].astype(f32)
     moe_gain_full=small_full[:,experts+1].astype(f32)
-    zero_id=jnp.zeros((1,),jnp.int32)
-    backward_ids=jnp.concatenate([zero_id,bucket_id])
-    forward_ids=reversed_ids(jnp.concatenate([bucket_id,zero_id]))
+    no_id=jnp.full((1,),-1,jnp.int32)
+    backward_ids=jnp.concatenate([no_id,bucket_id])[None,:]
+    forward_ids=reversed_ids(jnp.concatenate([bucket_id,no_id]))[None,:]
     own_table=lax.dynamic_slice_in_dim(bias_table,group*own_heads,own_heads,axis=1)*LOG2E
-    forward_bias=offset_rows(forward_ids,own_table)
-    backward_bias=offset_rows(backward_ids,own_table)
-    expert_pick=expert_id.reshape(count)
-    slot_pick=slot_id.reshape(count)
-    slots=experts*padded_cap
-    position=jnp.where(slot_pick<capacity,expert_pick*padded_cap+slot_pick,slots)
-    hot=(position[None,:]==jnp.arange(slots,dtype=jnp.int32)[:,None]).astype(b16)
-    cot_rows=matmul(hot,cotangent.reshape(count,width)).astype(b16).reshape(experts,padded_cap,width)
-    attended,out32,log_total,cot_arrived,every_weight,second_full=attend(plan,projected,forward_bias,cot_rows,own_weight,expert_out)
+    own_table=jnp.pad(own_table.T,((0,-own_heads%8),(0,128-buckets)))
+    attended,out32,log_total,cot_arrived,every_weight,second_full=attend(plan,projected,forward_ids,own_table,cot_rows,own_weight,expert_out)
     attended=attended.reshape(count,heads_width)
     tokens_f=tokens.astype(f32).reshape(count,width)
     hidden=tokens_f+matmul(attended,out_full)
@@ -956,45 +1016,42 @@
     moe_in=(hidden*moe_inverse*moe_gain_full).astype(b16)
     send_rows=matmul(hot,moe_in).astype(b16).reshape(experts,padded_cap,width)
     home,result,first_grad,second_grad,router_part=expert_layer(send_rows,cot_arrived,first_full,second_full,router_wide)
-    expert_in_grad=lax.psum_scatter(first_grad[None],"seq",scatter_dimension=2,tiled=True).astype(f32)
-    expert_out_grad=lax.psum_scatter(second_grad[None],"seq",scatter_dimension=1,tiled=True).astype(f32)
+    expert_in_grad=lax.psum_scatter(first_grad[None],"seq",scatter_dimension=2,tiled=True)[0]
+    expert_out_grad=lax.psum_scatter(second_grad[None],"seq",scatter_dimension=1,tiled=True)[0]
     gain_rows=jnp.transpose(small_full[:,experts:experts+2].astype(f32))
     home=home.reshape(slots,width)
     positions=position[:,None]
     hidden_grad,heads_grad,out_part=combine(experts,positions,home,hidden,cotangent.reshape(count,width),attended,out_full,gain_rows[1:2],router_part)
     out_part=jnp.concatenate([out_part[:,:width].reshape(groups*chunks,128,width)[:,:used].reshape(width,width),out_part[:width,width:]],axis=1) if used<128 else out_part
-    out_piece=jnp.pad(out_part.reshape(devices,row_block,width+128),((0,0),(0,-row_block%16),(0,0)))
-    hot_bucket=(backward_ids[None,:]==jnp.arange(buckets,dtype=jnp.int32)[:,None]).astype(f32)
-    hot_bucket=hot_bucket*(jnp.arange(length*2)>0)[None,:]
-    token_grads,returned,out_pieces,weight_pieces,tables=attend_back(plan,projected,out32,log_total,backward_bias,normed,hot_bucket,heads_grad.reshape(seq_count,stretch,heads_width),result,out_piece)
+    out_piece=jnp.moveaxis(out_part.reshape(experts*seq_count,groups,row_block,width+128),1,0)
+    out_piece=jnp.pad(out_piece,((0,0),(0,0),(0,-row_block%16),(0,0)))
+    token_grads,returned,out_pieces,weight_pieces,tables=attend_back(plan,projected,out32,log_total,backward_ids,own_table,normed,heads_grad.reshape(seq_count,stretch,heads_width),result,out_piece)
     inside=row_block%8==0
     token_grads=token_grads.reshape(count,groups*span)
-    output,input_grad,out_sum,*weight_grads,tables=finish(experts,groups,per_chunk,chunks,inside,positions,expert_pick[:,None],returned.reshape(slots,width),hidden,hidden_grad,tokens.reshape(count,width),token_grads,every_weight,gain_rows,router_wide,out_pieces,weight_pieces,tables)
-    out_sum=out_sum[:row_block]
+    own_weights=jnp.stack([query_weight,key_weight,value_weight])
+    output,input_grad,expert_in_grad,expert_out_grad,out_sum,small_sum,*weight_grads,attn_gain_grad,tables=finish(experts,groups,per_chunk,chunks,inside,positions,expert_pick[:,None],returned.reshape(slots,width),hidden,hidden_grad,tokens.reshape(count,width),token_grads,every_weight,gain_rows,router_wide,out_pieces,weight_pieces,tables,expert_in_grad,expert_out_grad,own_weights,attn_gain.astype(f32)[:,None])
+    attn_gain_grad=attn_gain_grad[:,0]
     output=output.reshape(seq_count,stretch,width)
-    bias_table_grad=jnp.transpose(tables[:,:,:own_heads],(1,0,2)).reshape(buckets,heads)
-    if inside:
-        weight_grads=jnp.stack([part[:row_block] for part in weight_grads])
-    else:
+    bias_table_grad=tables[:,:own_heads,:buckets].reshape(heads,buckets).T
+    if not inside:
         tokens_f=tokens.astype(f32).reshape(count,width)
         normed_own=(tokens_f*inverse_rms(tokens_f)*attn_gain_full).astype(b16)
         parts=matmul(normed_own,token_grads,TN).astype(b16).reshape(devices,row_block,groups*chunks,1+per_chunk,128)
         summed=jnp.sum(swap_parts(parts,BOTH).astype(f32),axis=0)
         both_sum=summed[:,:,1:].reshape(row_block,groups*chunks,per_chunk,2,head_dim)
-        weight_grads=jnp.stack([summed[:,:,0,:used].reshape(row_block,width)]+[both_sum[:,:,:,i].reshape(row_block,width) for i in range(2)])
-    own_weights=jnp.stack([query_weight,key_weight,value_weight]).astype(f32)
-    attn_gain_grad=jnp.sum(weight_grads*own_weights,axis=(0,2))/attn_gain.astype(f32)
+        weight_grads=[summed[:,:,0,:used].reshape(row_block,width)]+[both_sum[:,:,:,i].reshape(row_block,width) for i in range(2)]
+        attn_gain_grad=jnp.sum(jnp.stack(weight_grads)*own_weights.astype(f32),axis=(0,2))/attn_gain.astype(f32)
     return (
         output,
         input_grad.reshape(seq_count,stretch,width),
         weight_grads[0],weight_grads[1],weight_grads[2],
-        out_sum[:,:width],
-        out_sum[:,width:width+experts],
+        out_sum,
+        small_sum[:,:experts],
         attn_gain_grad,
-        out_sum[:,width+experts],
+        small_sum[:,experts],
         bias_table_grad,
-        expert_in_grad,
-        expert_out_grad,
+        expert_in_grad[None],
+        expert_out_grad[None],
     )
 
 def solution(mesh):

time: 495 us -> 465 us (0.939)
  Pallas kernels: 404 us -> 394 us
  matrix products: 15.3 us -> 8.24 us
  other arithmetic: 14.4 us -> 8.35 us
  local copies, waits for them, and re-layouts: 37.6 us -> 32.4 us
    pallas_call x1, Pallas kernels: 169 us -> 156 us  [attend_back(): pl.pallas_call(functools.partial(backward_kernel, plan, inside, bq, bk, s...]
    slice x6 -> x1, local copies, waits for them, and re-layouts: 8.2 us -> 1.42 us  [shards(): small_sum[:, experts]]
    convert_element_type x3 -> x0, other arithmetic: 5.69 us -> none  [the longest x1 2.85 us: shards(): lax.psum_scatter(second_grad[None], 'seq', scatter_dimension=1, tiled=True)]
    dot_general x4 -> x3, matrix products: 13.4 us -> 8.24 us  [matmul(): lax.dot_general(left, right, dims, preferred_element_type=jnp.float32)]
    unnamed x69 -> x72, local copies, waits for them, and re-layouts: 18.7 us -> 21.7 us
  transfers between devices with their start and end apart: 3 -> 3, of which waited for: 0 -> 0; matrix products, arithmetic and copies ran while one was open for 9% -> 4% of each run, Pallas kernels for 63% -> 61%
where the time goes in v4:
time: 465 us; the launch traced here: 459 us
  Pallas kernels  394 us (85%)
  local copies, waits for them, and re-layouts  32.4 us (7%)
  between operations  14.4 us (3%)
  other arithmetic  8.35 us (2%)
  matrix products  8.24 us (2%)
    pallas_call x1, Pallas kernels, attend_back(): pl.pallas_call(functools.partial(backward_kernel, plan, inside, bq, bk, s...  156 us
    pallas_call x1, Pallas kernels, expert_layer(): pl.pallas_call(functools.partial(expert_kernel, experts, cap, width, hidd...  97.9 us
    pallas_call x1, Pallas kernels, gather_start(): pl.pallas_call(functools.partial(start_kernel, plan, rows, span), in_spec...  61.9 us
    pallas_call x1, Pallas kernels, attend(): pl.pallas_call(functools.partial(forward_kernel, plan, block, srows, LOG2...  49.1 us
    unnamed x72, local copies, waits for them, and re-layouts  21.7 us
    pallas_call x1, Pallas kernels, finish(): pl.pallas_call(functools.partial(finish_kernel, experts, groups, heads, c...  18.1 us
    pallas_call x1, Pallas kernels, combine(): pl.pallas_call(functools.partial(combine_kernel, experts), grid=(count //...  10.5 us
  transfers between devices with their start and end apart: 3, of which 0 were waited for; matrix products, arithmetic and copies ran while one was open for 4% of the time, Pallas kernels for 61%

profile of v4, /device:TPU:0, one launch (start us, length us, event | category | flops | bytes accessed | tf_op | source)
XLA Modules:
  0.0 458.7 jit_solution(17708554098345940138)
XLA Ops:
  8.8 1.3 convert.8
  12.3 0.9 reshape.204
  13.1 0.9 reshape.205
  14.5 1.4 copy-done.6
  15.9 1.3 copy-done.8
  17.2 61.9 %gather_start.1 = (bf16[2048,1152]{1,0:T(8,128)(2,1)}, bf16[2048,768]{1,0:T(8,128)(2,1)S(1)}, bf16[8,160,768]{2,1,0:T(8,128)(2,1)S(1)}, bf16[768,1280]{1,0:T(8,128)(2,1)S(1)}, bf16[768,3072]{1,0:T(8,128)(2,1)}) custom-call(bf16[2,512,768]{2,1,0:T(8,128)(2,1)S(1)} %copy-done.4, bf16[2,32,1280]{2,1,0:T(8,128)(2,1)S(1)} %pad.17.unit_ref, ...), custom_call_target="tpu_custom_call" | custom-call | flops 3623878656 | bytes 25165824 | tf_op jit(solution)/shard_map/gather_start/pallas_call | solution.py:214
  79.1 1.7 copy-done.16
  80.8 1.3 copy-done.17
  82.1 1.0 convert_reduce_fusion
  84.4 1.1 convolution_convert_fusion
  86.2 1.3 copy-done.9
  87.4 49.1 %attend_forward.1 = (bf16[2,512,768]{2,1,0:T(8,128)(2,1)S(1)}, f32[2048,384]{1,0:T(8,128)}, f32[2048,128]{1,0:T(8,128)S(1)}, bf16[8,160,768]{2,1,0:T(8,128)(2,1)...) custom-call(bf16[2048,1152]{1,0:T(8,128)(2,1)} %get-tuple-element.47.proj_ref, s32[1,4096]{1,0:T(1,128)S(1)} %bitcast.77, ...), custom_call_target="tpu_custom_call" | custom-call | flops 25769803776 | bytes 16777216 | tf_op jit(solution)/shard_map/attend_forward/pallas_call | solution.py:385
  136.5 1.1 copy-done.12
  137.7 1.3 copy-done.18
  139.0 1.0 copy-done.19
  140.0 3.3 multiply_reduce_fusion
  143.3 3.9 fusion.1
  147.2 97.9 %expert_layer.1 = (bf16[8,160,768]{2,1,0:T(8,128)(2,1)}, bf16[8,160,768]{2,1,0:T(8,128)(2,1)}, bf16[768,3072]{1,0:T(8,128)(2,1)}, bf16[3072,768]{1,0:T(8,128)(2,1)}, f32[768,128]{1,0:T(8,128)}) custom-call(bf16[8,160,768]{2,1,0:T(8,128)(2,1)} %bitcast.112, bf16[8,160,768]{2,1,0:T(8,128)(2,1)} %copy-done.18, bf16[768,3072]{1,0:T(8,128)(2,1)} %get-tuple-element.55.w1_hbm, ...), custom_call_target="tpu_custom_call" | custom-call | flops 36238786560 | bytes 41943040 | tf_op jit(solution)/shard_map/expert_layer/pallas_call | solution.py:921
  246.8 2.3 copy.61
  249.8 1.0 copy.73
  250.8 1.0 copy.71
  253.9 1.6 fusion.5.pos_ref
  255.5 1.8 copy-done.11
  257.3 1.8 copy-done.13
  259.1 1.0 copy-done.15
  260.1 10.5 %combine.1 = (f32[1024,768]{1,0:T(8,128)S(1)}, bf16[1024,768]{1,0:T(8,128)(2,1)S(1)}, bf16[768,896]{1,0:T(8,128)(2,1)S(1)}) custom-call(s32[1024,1]{1,0:T(8,128)S(1)} %fusion.5.pos_ref, bf16[1280,768]{1,0:T(8,128)(2,1)S(1)} %bitcast.81, f32[1024,768]{1,0:T(8,128)} %copy-done.20, bf16[1024,768]{1,0:T(8,128)(2,1)S(1)} %bitcast.80, ...), custom_call_target="tpu_custom_call" | custom-call | flops 3623878656 | bytes 16777216 | tf_op jit(solution)/shard_map/combine/pallas_call | solution.py:696
  270.8 1.6 pad.19.piece_ref
  273.4 156.4 %attend_backward.1 = (bf16[2,512,2304]{2,1,0:T(8,128)(2,1)}, bf16[8,160,768]{2,1,0:T(8,128)(2,1)}, bf16[16,32,896]{2,1,0:T(8,128)(2,1)}, bf16[3,32,32,384]{3,2,1,0:T(8,128)(2,1)}, f32[32,8,128]{2,1,0:T(8,128)}) custom-call(bf16[2048,1152]{1,0:T(8,128)(2,1)} %get-tuple-element.47.proj_ref, f32[2048,384]{1,0:T(8,128)} %get-tuple-element.50.o32_ref, ...), custom_call_target="tpu_custom_call" | custom-call | flops 64424509440 | bytes 25165824 | tf_op jit(solution)/shard_map/attend_backward/pallas_call | solution.py:639
  429.8 18.1 %finish.1 = (bf16[1024,768]{1,0:T(8,128)(2,1)}, f32[1024,768]{1,0:T(8,128)}, f32[768,768]{1,0:T(8,128)}, f32[768,768]{1,0:T(8,128)}, f32[24,768]{1,0:T(8,128)}, ...) custom-call(s32[1024,1]{1,0:T(8,128)} %copy-done.3, ...), custom_call_target="tpu_custom_call" | custom-call | flops 4831838208 | bytes 25165824 | tf_op jit(solution)/shard_map/finish/pallas_call | solution.py:777
  447.9 1.4 slice_reduce_fusion
  449.3 1.4 copy.65
  450.7 1.3 reshape.220
  (92 shorter events, 11.7 us)
Async XLA Ops:
  7.2 7.3 %copy-start.4 = (bf16[2,512,768]{2,1,0:T(8,128)(2,1)S(1)}, bf16[2,512,768]{2,1,0:T(8,128)(2,1)}, u32[]{:S(2)}) copy-start(bf16[2,512,768]{2,1,0:T(8,128)(2,1)} %token_ref.1) | copy-start | bytes 4718596
  7.2 132.8 %all-gather.2.cloned.1.call-start = ((), (), s32[]{:S(2)}) async-start(), calls=%async_computation.2 | async-start | bytes 1216512 | tf_op jit(solution)/shard_map/all_gather | solution.py:986
  7.9 421.8 %reduce-scatter.3.cloned.1.call-start = ((), (), s32[]{:S(2)}) async-start(), calls=%async_computation.3 | async-start | bytes 5898240 | tf_op jit(solution)/shard_map/reduce_scatter | solution.py:1019
  14.5 1.4 copy-start.6
  15.9 1.3 copy-start.8
  17.2 66.6 %copy-start.30 = (f32[32,12]{0,1:T(8,128)S(1)}, f32[32,12]{0,1:T(8,128)}, u32[]{:S(2)}) copy-start(f32[32,12]{0,1:T(8,128)} %param.25) | copy-start | bytes 4612
  79.1 1.7 copy-start.16
  80.8 1.3 copy-start.17
  82.1 3.4 copy-start.1
  86.2 1.3 copy-start.9
  136.5 1.1 copy-start.12
  137.7 1.3 copy-start.18
  140.0 3.3 copy-start.28
  140.0 3.3 copy-start.29
  143.3 3.9 copy-start.20
  245.1 184.7 %reduce-scatter.5.cloned.1.call-start = ((), (), s32[]{:S(2)}) async-start(), calls=%async_computation.4 | async-start | bytes 5898240 | tf_op jit(solution)/shard_map/reduce_scatter | solution.py:1020
  245.2 1.5 copy-start.2
  246.7 2.3 copy-start.26
  246.7 2.3 copy-start.27
  246.7 2.3 copy-start.31
  246.7 5.8 %copy-start.24 = (s32[4095]{0:T(1024)S(1)}, s32[4095]{0:T(1024)}, u32[]{:S(2)}) copy-start(s32[4095]{0:T(1024)} %param.30) | copy-start | bytes 49144
  246.7 6.5 %copy-start.21 = (bf16[24,768]{1,0:T(8,128)(2,1)S(1)}, bf16[24,768]{1,0:T(8,128)(2,1)}, u32[]{:S(2)}) copy-start(bf16[24,768]{1,0:T(8,128)(2,1)} %param.20) | copy-start | bytes 110596
  246.7 6.5 %copy-start.22 = (bf16[24,768]{1,0:T(8,128)(2,1)S(1)}, bf16[24,768]{1,0:T(8,128)(2,1)}, u32[]{:S(2)}) copy-start(bf16[24,768]{1,0:T(8,128)(2,1)} %param.19) | copy-start | bytes 110596
  246.8 6.5 %copy-start.23 = (bf16[24,768]{1,0:T(8,128)(2,1)S(1)}, bf16[24,768]{1,0:T(8,128)(2,1)}, u32[]{:S(2)}) copy-start(bf16[24,768]{1,0:T(8,128)(2,1)} %param.18) | copy-start | bytes 110596
  249.0 6.5 %copy-start.7 = (bf16[2,512,768]{2,1,0:T(8,128)(2,1)S(1)}, bf16[2,512,768]{2,1,0:T(8,128)(2,1)}, u32[]{:S(2)}) copy-start(bf16[2,512,768]{2,1,0:T(8,128)(2,1)} %param.31) | copy-start | bytes 4718596
  249.0 6.5 %copy-start.10 = (bf16[768,768]{1,0:T(8,128)(2,1)S(1)}, bf16[768,768]{1,0:T(8,128)(2,1)}, u32[]{:S(2)}) copy-start(bf16[768,768]{1,0:T(8,128)(2,1)} %all-gather.2.cloned.1.call-done.out_w_ref) | copy-start | bytes 3538948
  252.5 18.1 %copy-start.25 = (f32[2,768]{1,0:T(2,128)}, f32[2,768]{1,0:T(2,128)S(1)}, u32[]{:S(2)}) copy-start(f32[2,768]{1,0:T(2,128)S(1)} %convert_bitcast_fusion.gains_ref) | copy-start | bytes 18436
  255.5 15.1 %copy-start.3 = (s32[1024,1]{1,0:T(8,128)}, s32[1024,1]{1,0:T(8,128)S(1)}, u32[]{:S(2)}) copy-start(s32[1024,1]{1,0:T(8,128)S(1)} %fusion.5.pos_ref) | copy-start | bytes 12292
  255.5 1.8 copy-start.11
  257.3 1.8 copy-start.13
  270.6 2.3 copy-start
  270.6 2.7 copy-start.14
  (3 other events, 2.7 us)
Sparse Core Ops, SparseCore 0:
  10.9 63.0 all-gather.1
  245.2 58.5 reduce-scatter.2
  306.5 103.0 reduce-scatter.4

commit v5 on v4

--- a/solution.py
+++ b/solution.py
@@ -36,10 +36,9 @@
         out=jnp.where(lanes==start+place,part,out)
     return out
 
-def split_query(query,head,scale):
-    both=dup_head(query,head)*scale
-    high=both.astype(jnp.bfloat16).astype(jnp.float32)
-    return jnp.where(lane_iota(query.shape[0])<64,high,both-high).astype(jnp.bfloat16)
+def lone_query(query,head):
+    both=dup_head(query,head)*0.125
+    return jnp.where(lane_iota(query.shape[0])<64,both,0.0).astype(jnp.bfloat16)
 
 def fill_strip(strip,vector,rows,width):
     full=width+rows
@@ -239,7 +238,7 @@
 def chunk_span(heads):
     return 128*(1+heads)
 
-def forward_kernel(plan,block,srows,scale,proj_ref,ids_ref,rows_ref,cot_ref,own_ref,w2_ref,att_out,o32_ref,lse_ref,cot_out,all_out,w2_out,strip,bias_ref,kd,va,scr,outs,s_cot,r_cot,s_att,r_att,s_all,r_all,local_sem,*spread_sems):
+def forward_kernel(plan,block,srows,proj_ref,ids_ref,rows_ref,cot_ref,own_ref,w2_ref,att_out,o32_ref,lse_ref,cot_out,all_out,w2_out,strip,bias_ref,kd,va,scr,outs,s_cot,r_cot,s_att,r_att,s_all,r_all,local_sem,*spread_sems):
     experts,seq_devs,seq_count,stretch,heads,chunks=plan
     length=stretch*seq_devs
     groups=seq_devs//seq_count
@@ -296,7 +295,7 @@
             parts=[]
             for part in range(block//srows):
                 start=length-srows-step*block-part*srows+p*wide
-                parts.append(raw[part*srows:(part+1)*srows]+strip[:,pl.ds(start,wide)])
+                parts.append(raw[part*srows:(part+1)*srows]*LOG2E+strip[:,pl.ds(start,wide)])
             scores=jnp.concatenate(parts,axis=0)
             scr[slot,:,p*wide:(p+1)*wide]=scores
             for j in range(wide//128):
@@ -326,7 +325,7 @@
                     send_att(c,distance).start()
         def advance(step,slot,top):
             mixing=top is not None
-            qa=split_query(proj_ref[rows_of(step),columns(0)],head,scale)
+            qa=lone_query(proj_ref[rows_of(step),columns(0)],head)
             new=jnp.full((block,128),-jnp.inf,f32)
             mixed=jnp.zeros((block,128),f32)
             for p in range(pieces):
@@ -383,7 +382,7 @@
     anywhere=pl.BlockSpec(memory_space=pl.ANY)
     dma=lambda *shape: pltpu.SemaphoreType.DMA(shape)
     return pl.pallas_call(
-        functools.partial(forward_kernel,plan,block,srows,LOG2E/8),
+        functools.partial(forward_kernel,plan,block,srows),
         in_specs=[vmem,vmem,vmem,anywhere,vmem,vmem],
         out_specs=[anywhere,vmem,vmem]+[anywhere]*3,
         out_shape=[jax.ShapeDtypeStruct((seq_count,stretch,groups*chunks*128),b16),jax.ShapeDtypeStruct((length,chunks*128),f32),jax.ShapeDtypeStruct((length,128),f32),jax.ShapeDtypeStruct(cot_rows.shape,b16),jax.ShapeDtypeStruct((groups,)+own_weight.shape,b16),jax.ShapeDtypeStruct((expert_out.shape[1]*seq_devs,expert_out.shape[2]),b16)],
@@ -394,9 +393,9 @@
         name="attend_forward",
     )(projected,ids,table,cot_rows,own_weight,expert_out)
 
-def backward_kernel(plan,inside,bq,bk,srows,scale,proj_ref,o32_ref,lse_ref,ids_ref,rows_ref,normed_ref,up_ref,res_ref,piece_ref,
+def backward_kernel(plan,inside,bq,bk,srows,proj_ref,o32_ref,lse_ref,ids_ref,rows_ref,normed_ref,up_ref,res_ref,piece_ref,
                     grad_out,ret_out,piece_out,weight_out,table_out,
-                    strip,grads,kk,kt,qa,da,qd,dkv_acc,lse_t,delta,ups,outs,weight_parts,piece_parts,piece_land,diag,table,normed_t,hot,bias_ref,
+                    strip,grads,kk,kt,da,qd,dkv_acc,lse_t,delta,ups,outs,weight_parts,piece_parts,piece_land,diag,table,normed_t,hot,bias_ref,
                     s_up,r_up,s_res,r_res,s_piece,r_piece,s_grad,r_grad,s_weight,r_weight,s_half,r_half,s_table,r_table,local_sem,own_sem):
     experts,seq_devs,seq_count,stretch,heads,chunks=plan
     length=stretch*seq_devs
@@ -490,15 +489,10 @@
         fill_strip(strip,bias_ref[pl.ds(index,1),:],srows,width)
         grads[...]=jnp.zeros_like(grads)
         low_lanes=lanes<64
-        kk[:,:128]=both
-        kk[:,128:]=both
+        kk[...]=both
         kt[...]=jnp.transpose(both)
         query=query.astype(f32)
         query=jnp.where(low_lanes,pltpu.roll(query,64,1) if head else query,0.0)
-        scaled=query*scale
-        high=scaled.astype(b16).astype(f32)
-        qa[:,:128]=high.astype(b16)
-        qa[:,128:]=(scaled-high).astype(b16)
         qd[...]=(query*0.125).astype(b16)
         if head==0:
             take_up(c)
@@ -513,8 +507,8 @@
             qs=pl.ds(pl.multiple_of(qb*bq,bq),bq)
             def products(kb):
                 ks=slice(kb*bk,(kb+1)*bk)
-                raw=lax.dot_general(kk[ks,:],qa[qs,:],NT,preferred_element_type=f32)
-                up=lax.dot_general(kk[ks,:128],da[qs,:],NT,preferred_element_type=f32)
+                raw=lax.dot_general(kk[ks,:],qd[qs,:],NT,preferred_element_type=f32)
+                up=lax.dot_general(kk[ks,:],da[qs,:],NT,preferred_element_type=f32)
                 return raw,up
             log_row=lse_t[pl.ds(index,1),qs]
             delta_row=delta[head:head+1,qs]
@@ -524,7 +518,7 @@
                 for part in range(bk//srows):
                     start=qb*bq+(length-srows)-kb*bk-part*srows
                     rows=slice(part*srows,(part+1)*srows)
-                    prob=jnp.exp2(raw[rows]+strip[:,pl.ds(pl.multiple_of(start,128),bq)]-log_row)
+                    prob=jnp.exp2(raw[rows]*LOG2E+strip[:,pl.ds(pl.multiple_of(start,128),bq)]-log_row)
                     grad=prob*(up[rows]-delta_row)
                     grads[:,pl.ds(pl.multiple_of(start+srows,128),bq)]+=grad
                     probs.append(prob.astype(b16))
@@ -637,11 +631,11 @@
     shape=lambda kind,*dims: jax.ShapeDtypeStruct(dims,kind)
     weight_shape=(chunks,devices,rows,chunk_span(heads)) if inside else (1,1,16,128)
     return pl.pallas_call(
-        functools.partial(backward_kernel,plan,inside,bq,bk,srows,LOG2E/8),
+        functools.partial(backward_kernel,plan,inside,bq,bk,srows),
         in_specs=[vmem]*6+[anywhere]*3,
         out_specs=[anywhere]*5,
         out_shape=[shape(b16,seq_count,stretch,groups*chunks*chunk_span(heads)),shape(b16,*result.shape),shape(b16,*piece.shape[1:]),shape(b16,*weight_shape),shape(f32,devices,table.shape[0],128)],
-        scratch_shapes=[vm(f32,srows,2*length-srows),vm(f32,srows,2*length),vm(b16,length,256),vm(b16,128,length),vm(b16,length,256),vm(b16,length,128),
+        scratch_shapes=[vm(f32,srows,2*length-srows),vm(f32,srows,2*length),vm(b16,length,128),vm(b16,128,length),vm(b16,length,128),
             vm(b16,length,128),vm(f32,length,128),vm(f32,128,length),vm(f32,8,length),
             vm(b16,chunks,length,128),vm(b16,chunks,length,chunk_span(heads)),vm(b16,*weight_shape),vm(b16,*piece.shape[1:]),vm(b16,max(groups-1,1),*piece.shape[1:]),vm(f32,table.shape[0],2*length),vm(f32,table.shape[0],128),vm(b16,normed.shape[1],length),vm(b16,128,2*length),vm(f32,table.shape[0],2*length),
             dma(chunks,seq_devs),dma(chunks,seq_devs),dma(experts),dma(experts),dma(experts*seq_count),dma(experts*seq_count),dma(chunks,1+heads,seq_devs),dma(chunks,1+heads,seq_devs),

time: 465 us -> 464 us (level)
  transfers between devices with their start and end apart: 3 -> 3, of which waited for: 0 -> 0; matrix products, arithmetic and copies ran while one was open for 4% -> 4% of each run, Pallas kernels for 61% -> 60%
where the time goes in v5:
time: 464 us; the launch traced here: 458 us
  Pallas kernels  393 us (85%)
  local copies, waits for them, and re-layouts  32.6 us (7%)
  between operations  14.5 us (3%)
  other arithmetic  8.31 us (2%)
  matrix products  8.24 us (2%)
    pallas_call x1, Pallas kernels, attend_back(): pl.pallas_call(functools.partial(backward_kernel, plan, inside, bq, bk, s...  156 us
    pallas_call x1, Pallas kernels, expert_layer(): pl.pallas_call(functools.partial(expert_kernel, experts, cap, width, hidd...  97.9 us
    pallas_call x1, Pallas kernels, gather_start(): pl.pallas_call(functools.partial(start_kernel, plan, rows, span), in_spec...  61.9 us
    pallas_call x1, Pallas kernels, attend(): pl.pallas_call(functools.partial(forward_kernel, plan, block, srows), in_...  49.1 us
    unnamed x72, local copies, waits for them, and re-layouts  22 us
    pallas_call x1, Pallas kernels, finish(): pl.pallas_call(functools.partial(finish_kernel, experts, groups, heads, c...  18.1 us
    pallas_call x1, Pallas kernels, combine(): pl.pallas_call(functools.partial(combine_kernel, experts), grid=(count //...  10.4 us
  transfers between devices with their start and end apart: 3, of which 0 were waited for; matrix products, arithmetic and copies ran while one was open for 4% of the time, Pallas kernels for 60%

profile of v5, /device:TPU:0, one launch (start us, length us, event | category | flops | bytes accessed | tf_op | source)
XLA Modules:
  0.0 458.1 jit_solution(13309148601313068974)
XLA Ops:
  8.8 1.3 convert.8
  12.3 0.9 reshape.204
  13.1 0.9 reshape.205
  14.5 1.4 copy-done.6
  15.9 1.3 copy-done.8
  17.2 61.9 %gather_start.1 = (bf16[2048,1152]{1,0:T(8,128)(2,1)}, bf16[2048,768]{1,0:T(8,128)(2,1)S(1)}, bf16[8,160,768]{2,1,0:T(8,128)(2,1)S(1)}, bf16[768,1280]{1,0:T(8,128)(2,1)S(1)}, bf16[768,3072]{1,0:T(8,128)(2,1)}) custom-call(bf16[2,512,768]{2,1,0:T(8,128)(2,1)S(1)} %copy-done.4, bf16[2,32,1280]{2,1,0:T(8,128)(2,1)S(1)} %pad.17.unit_ref, ...), custom_call_target="tpu_custom_call" | custom-call | flops 3623878656 | bytes 25165824 | tf_op jit(solution)/shard_map/gather_start/pallas_call | solution.py:213
  79.1 1.7 copy-done.16
  80.8 1.3 copy-done.17
  82.1 1.0 convert_reduce_fusion
  84.4 1.1 convolution_convert_fusion
  86.2 1.3 copy-done.9
  87.4 49.1 %attend_forward.1 = (bf16[2,512,768]{2,1,0:T(8,128)(2,1)S(1)}, f32[2048,384]{1,0:T(8,128)}, f32[2048,128]{1,0:T(8,128)S(1)}, bf16[8,160,768]{2,1,0:T(8,128)(2,1)...) custom-call(bf16[2048,1152]{1,0:T(8,128)(2,1)} %get-tuple-element.47.proj_ref, s32[1,4096]{1,0:T(1,128)S(1)} %bitcast.77, ...), custom_call_target="tpu_custom_call" | custom-call | flops 25769803776 | bytes 16777216 | tf_op jit(solution)/shard_map/attend_forward/pallas_call | solution.py:384
  136.5 1.1 copy-done.12
  137.7 1.3 copy-done.18
  139.0 1.0 copy-done.19
  140.0 3.3 multiply_reduce_fusion
  143.3 3.9 fusion.1
  147.2 97.9 %expert_layer.1 = (bf16[8,160,768]{2,1,0:T(8,128)(2,1)}, bf16[8,160,768]{2,1,0:T(8,128)(2,1)}, bf16[768,3072]{1,0:T(8,128)(2,1)}, bf16[3072,768]{1,0:T(8,128)(2,1)}, f32[768,128]{1,0:T(8,128)}) custom-call(bf16[8,160,768]{2,1,0:T(8,128)(2,1)} %bitcast.112, bf16[8,160,768]{2,1,0:T(8,128)(2,1)} %copy-done.18, bf16[768,3072]{1,0:T(8,128)(2,1)} %get-tuple-element.55.w1_hbm, ...), custom_call_target="tpu_custom_call" | custom-call | flops 36238786560 | bytes 41943040 | tf_op jit(solution)/shard_map/expert_layer/pallas_call | solution.py:915
  246.7 2.3 copy.61
  249.7 1.0 copy.73
  250.8 1.0 copy.71
  253.9 1.5 fusion.5.pos_ref
  255.4 2.0 copy-done.11
  257.5 1.8 copy-done.13
  259.3 1.0 copy-done.15
  260.3 10.4 %combine.1 = (f32[1024,768]{1,0:T(8,128)S(1)}, bf16[1024,768]{1,0:T(8,128)(2,1)S(1)}, bf16[768,896]{1,0:T(8,128)(2,1)S(1)}) custom-call(s32[1024,1]{1,0:T(8,128)S(1)} %fusion.5.pos_ref, bf16[1280,768]{1,0:T(8,128)(2,1)S(1)} %bitcast.81, f32[1024,768]{1,0:T(8,128)} %copy-done.20, bf16[1024,768]{1,0:T(8,128)(2,1)S(1)} %bitcast.80, ...), custom_call_target="tpu_custom_call" | custom-call | flops 3623878656 | bytes 16777216 | tf_op jit(solution)/shard_map/combine/pallas_call | solution.py:690
  270.9 1.6 pad.19.piece_ref
  273.5 155.5 %attend_backward.1 = (bf16[2,512,2304]{2,1,0:T(8,128)(2,1)}, bf16[8,160,768]{2,1,0:T(8,128)(2,1)}, bf16[16,32,896]{2,1,0:T(8,128)(2,1)}, bf16[3,32,32,384]{3,2,1,0:T(8,128)(2,1)}, f32[32,8,128]{2,1,0:T(8,128)}) custom-call(bf16[2048,1152]{1,0:T(8,128)(2,1)} %get-tuple-element.47.proj_ref, f32[2048,384]{1,0:T(8,128)} %get-tuple-element.50.o32_ref, ...), custom_call_target="tpu_custom_call" | custom-call | flops 64424509440 | bytes 25165824 | tf_op jit(solution)/shard_map/attend_backward/pallas_call | solution.py:633
  429.1 18.1 %finish.1 = (bf16[1024,768]{1,0:T(8,128)(2,1)}, f32[1024,768]{1,0:T(8,128)}, f32[768,768]{1,0:T(8,128)}, f32[768,768]{1,0:T(8,128)}, f32[24,768]{1,0:T(8,128)}, ...) custom-call(s32[1024,1]{1,0:T(8,128)} %copy-done.3, ...), custom_call_target="tpu_custom_call" | custom-call | flops 4831838208 | bytes 25165824 | tf_op jit(solution)/shard_map/finish/pallas_call | solution.py:771
  447.1 1.4 slice_reduce_fusion
  448.6 1.4 copy.65
  449.9 1.3 reshape.220
  (92 shorter events, 11.7 us)
Async XLA Ops:
  7.2 7.3 %copy-start.4 = (bf16[2,512,768]{2,1,0:T(8,128)(2,1)S(1)}, bf16[2,512,768]{2,1,0:T(8,128)(2,1)}, u32[]{:S(2)}) copy-start(bf16[2,512,768]{2,1,0:T(8,128)(2,1)} %token_ref.1) | copy-start | bytes 4718596
  7.2 132.8 %all-gather.2.cloned.1.call-start = ((), (), s32[]{:S(2)}) async-start(), calls=%async_computation.2 | async-start | bytes 1216512 | tf_op jit(solution)/shard_map/all_gather | solution.py:980
  7.9 421.1 %reduce-scatter.3.cloned.1.call-start = ((), (), s32[]{:S(2)}) async-start(), calls=%async_computation.3 | async-start | bytes 5898240 | tf_op jit(solution)/shard_map/reduce_scatter | solution.py:1013
  14.5 1.4 copy-start.6
  15.9 1.3 copy-start.8
  17.2 66.6 %copy-start.30 = (f32[32,12]{0,1:T(8,128)S(1)}, f32[32,12]{0,1:T(8,128)}, u32[]{:S(2)}) copy-start(f32[32,12]{0,1:T(8,128)} %param.25) | copy-start | bytes 4612
  79.1 1.7 copy-start.16
  80.8 1.3 copy-start.17
  82.1 3.4 copy-start.1
  86.2 1.3 copy-start.9
  136.5 1.1 copy-start.12
  137.7 1.3 copy-start.18
  140.0 3.3 copy-start.28
  140.0 3.3 copy-start.29
  143.3 3.9 copy-start.20
  245.1 184.0 %reduce-scatter.5.cloned.1.call-start = ((), (), s32[]{:S(2)}) async-start(), calls=%async_computation.4 | async-start | bytes 5898240 | tf_op jit(solution)/shard_map/reduce_scatter | solution.py:1014
  245.1 1.5 copy-start.2
  246.7 2.3 copy-start.26
  246.7 2.3 copy-start.27
  246.7 2.3 copy-start.31
  246.7 5.8 %copy-start.24 = (s32[4095]{0:T(1024)S(1)}, s32[4095]{0:T(1024)}, u32[]{:S(2)}) copy-start(s32[4095]{0:T(1024)} %param.30) | copy-start | bytes 49144
  246.7 6.5 %copy-start.21 = (bf16[24,768]{1,0:T(8,128)(2,1)S(1)}, bf16[24,768]{1,0:T(8,128)(2,1)}, u32[]{:S(2)}) copy-start(bf16[24,768]{1,0:T(8,128)(2,1)} %param.20) | copy-start | bytes 110596
  246.7 6.5 %copy-start.22 = (bf16[24,768]{1,0:T(8,128)(2,1)S(1)}, bf16[24,768]{1,0:T(8,128)(2,1)}, u32[]{:S(2)}) copy-start(bf16[24,768]{1,0:T(8,128)(2,1)} %param.19) | copy-start | bytes 110596
  246.7 6.5 %copy-start.23 = (bf16[24,768]{1,0:T(8,128)(2,1)S(1)}, bf16[24,768]{1,0:T(8,128)(2,1)}, u32[]{:S(2)}) copy-start(bf16[24,768]{1,0:T(8,128)(2,1)} %param.18) | copy-start | bytes 110596
  249.0 6.4 %copy-start.7 = (bf16[2,512,768]{2,1,0:T(8,128)(2,1)S(1)}, bf16[2,512,768]{2,1,0:T(8,128)(2,1)}, u32[]{:S(2)}) copy-start(bf16[2,512,768]{2,1,0:T(8,128)(2,1)} %param.31) | copy-start | bytes 4718596
  249.0 6.4 %copy-start.10 = (bf16[768,768]{1,0:T(8,128)(2,1)S(1)}, bf16[768,768]{1,0:T(8,128)(2,1)}, u32[]{:S(2)}) copy-start(bf16[768,768]{1,0:T(8,128)(2,1)} %all-gather.2.cloned.1.call-done.out_w_ref) | copy-start | bytes 3538948
  252.5 18.2 %copy-start.25 = (f32[2,768]{1,0:T(2,128)}, f32[2,768]{1,0:T(2,128)S(1)}, u32[]{:S(2)}) copy-start(f32[2,768]{1,0:T(2,128)S(1)} %convert_bitcast_fusion.gains_ref) | copy-start | bytes 18436
  255.4 15.4 %copy-start.3 = (s32[1024,1]{1,0:T(8,128)}, s32[1024,1]{1,0:T(8,128)S(1)}, u32[]{:S(2)}) copy-start(s32[1024,1]{1,0:T(8,128)S(1)} %fusion.5.pos_ref) | copy-start | bytes 12292
  255.4 2.0 copy-start.11
  257.5 1.8 copy-start.13
  270.8 2.3 copy-start
  270.8 2.7 copy-start.14
  (3 other events, 2.7 us)
Sparse Core Ops, SparseCore 0:
  10.9 63.0 all-gather.1
  245.2 58.3 reduce-scatter.2
  306.3 103.2 reduce-scatter.4
